TPU v7x, 32 devices: a whole 2x2x4 slice. The times are simulated.
32 devices in a mesh: dp: 4 (over z), section: 2 (over core), tensor: 4 (over y, x).
Axes of the slice: x: 2, y: 2, z: 4, core: 2. Of those that a mesh axis runs over, the one named last changes fastest.
Arguments:
- tokens: bfloat16 [1024, 2048], P('dp'), may hold values from -6 to 6
- base_rows: int32 [16], replicated, may hold values from 1 to 48, as said below
- baseline_owner: int32 [16], replicated, may hold values from 0 to 3, as said below
- cotangent: bfloat16 [2, 2048, 2048], P('section', 'dp'), may hold values from -6 to 6
- pre_gain: float32 [2, 2048], P('section'), may hold values from 0.25 to 1.75
- input_proj: bfloat16 [2, 2048, 2048], P('section', None, 'tensor'), may hold values from -0.125 to 0.125
- gate_proj: bfloat16 [2, 2048, 2048], P('section', None, 'tensor'), may hold values from -0.125 to 0.125
- state_proj: bfloat16 [2, 2048, 256], P('section'), may hold values from -0.125 to 0.125
- step_proj: bfloat16 [2, 2048, 32], P('section', None, 'tensor'), may hold values from -0.125 to 0.125
- step_bias: float32 [2, 32], P('section', 'tensor'), may hold values from -6 to -1.5
- decay_log: float32 [2, 32], P('section', 'tensor'), may hold values from 0 to 2.5
- skip_gain: float32 [2, 32], P('section', 'tensor'), may hold values from 0.5 to 1.5
- norm_gain: float32 [2, 2048], P('section', 'tensor'), may hold values from 0.25 to 1.75
- out_proj: bfloat16 [2, 2048, 2048], P('section', 'tensor'), may hold values from -0.125 to 0.125
Outputs:
- activations: bfloat16 [2, 2048, 2048], P('section', 'dp')
- out_grad: bfloat16 [2, 2048, 2048], P('section', 'tensor', 'dp')
Inputs may be any that keep to these rules, and one draw needn't show every extreme that they name: `base_rows`: over all baselines they sum to 256; some baseline has exactly 48. `baseline_owner`: every owner holds exactly 4 baselines; the base_rows of one owner's baselines sum to at most 128, and for some owner to exactly 128.
All inputs are finite; a program needn't handle non-finite values.
Results may differ from a plain program's by a relative error of at most 0.025.
Values may be sent and summed in bfloat16 or wider, within the bound.
No kernel may reach another device: no remote copies, remote signals or barrier semaphores. Data moves between devices by JAX's collectives and lax.ppermute only.
A program may use at most 128 MiB of HBM per device.

v0:
```python
import jax
import jax.numpy as jnp
from jax import lax
from jax.sharding import PartitionSpec as P

HEADS = 32
HEADDIM = 64
NSTATE = 128
BLOCK = 64
MICRO = 2


EPS = 1e-05


def from_behind(value, axis, steps):
    count = lax.axis_size(axis)
    first, last = (max(0, -steps), min(count, count - steps))
    return lax.ppermute(value, axis, [(source, source + steps) for source in range(first, last)])


def layout_tables(base_rows, baseline_owner):
    count = base_rows.shape[0]
    index = jnp.arange(count, dtype=jnp.int32)
    ends = jnp.cumsum(base_rows)
    starts = ends - base_rows
    earlier = (baseline_owner[:, None] == baseline_owner[None, :]) & (
        index[None, :] < index[:, None]
    )
    owner_start = jnp.sum(jnp.where(earlier, base_rows[None, :], 0), axis=1)
    return (index, starts, ends, owner_start)


def block_scan(
    heads_in, b_rows, c_rows, step_size, decay_rate, segment, state, prev_segment, block
):
    total_rows, head_count, head_dim = heads_in.shape
    blocks = total_rows // block

    def advance(carried_in, item):
        state_now, segment_before = carried_in
        x_blk, b_blk, c_blk, dt_blk, seg_blk = item
        running = jnp.cumsum(dt_blk * decay_rate[None, :], axis=0)
        positions = jnp.arange(block, dtype=jnp.int32)
        together = (seg_blk[:, None] == seg_blk[None, :]) & (
            positions[:, None] >= positions[None, :]
        )
        spread = jnp.minimum(running[:, None, :] - running[None, :, :], 0.0)
        decay_mask = jnp.where(together[:, :, None], jnp.exp(spread), 0.0)
        scores = jnp.dot(c_blk, b_blk.T, preferred_element_type=jnp.float32)
        weights = (decay_mask * scores[:, :, None] * dt_blk[None, :, :]).astype(jnp.bfloat16)
        within = jnp.einsum("ijh,jhp->ihp", weights, x_blk, preferred_element_type=jnp.float32)
        keep_in = (seg_blk == segment_before).astype(jnp.float32)
        readout = jnp.einsum(
            "in,hpn->ihp", c_blk, state_now.astype(jnp.bfloat16), preferred_element_type=jnp.float32
        )
        from_state = keep_in[:, None, None] * jnp.exp(running)[:, :, None] * readout
        last_segment = seg_blk[-1]
        tail_weight = (
            jnp.where(
                (seg_blk == last_segment)[:, None], jnp.exp(running[-1][None, :] - running), 0.0
            )
            * dt_blk
        )
        scaled = (tail_weight[:, :, None] * x_blk.astype(jnp.float32)).astype(jnp.bfloat16)
        fresh_term = jnp.einsum("jhp,jn->hpn", scaled, b_blk, preferred_element_type=jnp.float32)
        keep_state = (last_segment == segment_before).astype(jnp.float32)
        state_next = keep_state * jnp.exp(running[-1])[:, None, None] * state_now + fresh_term
        return ((state_next, last_segment), within + from_state)

    scanned = (
        heads_in.reshape(blocks, block, head_count, head_dim),
        b_rows.reshape(blocks, block, -1),
        c_rows.reshape(blocks, block, -1),
        step_size.reshape(blocks, block, head_count),
        segment.reshape(blocks, block),
    )
    (state, prev_segment), outputs = lax.scan(advance, (state, prev_segment), scanned)
    return (outputs.reshape(total_rows, head_count, head_dim), state, prev_segment)


def block_layer(rows_in, segment, carried_state, params):
    (
        pre_gain,
        input_proj,
        gate_proj,
        state_proj,
        step_proj,
        step_bias,
        decay_log,
        skip_gain,
        norm_gain,
        out_proj,
    ) = params
    row_count = rows_in.shape[0]
    local_heads = step_proj.shape[1]
    rows_f = rows_in.astype(jnp.float32)
    normed = (
        rows_f * lax.rsqrt(jnp.mean(rows_f * rows_f, axis=-1, keepdims=True) + EPS) * pre_gain
    ).astype(jnp.bfloat16)
    scan_in = jax.nn.silu(jnp.dot(normed, input_proj, preferred_element_type=jnp.float32)).astype(
        jnp.bfloat16
    )
    gate_pre = jnp.dot(normed, gate_proj, preferred_element_type=jnp.float32)
    state_io = jax.nn.silu(jnp.dot(normed, state_proj, preferred_element_type=jnp.float32)).astype(
        jnp.bfloat16
    )
    step_size = jax.nn.softplus(
        jnp.dot(normed, step_proj, preferred_element_type=jnp.float32) + step_bias
    )
    decay_rate = -jnp.exp(decay_log)
    heads_in = scan_in.reshape(row_count, local_heads, HEADDIM)
    scan_out, state_end, segment_end = block_scan(
        heads_in,
        state_io[:, :NSTATE],
        state_io[:, NSTATE:],
        step_size,
        decay_rate,
        segment,
        carried_state[0],
        carried_state[1],
        BLOCK,
    )
    scan_out = scan_out + skip_gain[None, :, None] * heads_in.astype(jnp.float32)
    gated = scan_out.reshape(row_count, local_heads * HEADDIM) * jax.nn.silu(gate_pre)
    sq_sum = lax.psum(jnp.sum(gated * gated, axis=-1), "tensor")
    y_norm = (gated * lax.rsqrt(sq_sum[:, None] / (HEADS * HEADDIM) + EPS) * norm_gain).astype(
        jnp.bfloat16
    )
    row_share = row_count // lax.axis_size("tensor")
    summed = lax.psum_scatter(
        jnp.dot(y_norm, out_proj, preferred_element_type=jnp.float32).astype(jnp.bfloat16),
        "tensor",
        scatter_dimension=0,
        tiled=True,
    ).astype(jnp.float32)
    own_rows = lax.dynamic_slice_in_dim(rows_f, lax.axis_index("tensor") * row_share, row_share, 0)
    own_out = (own_rows + summed).astype(jnp.bfloat16)
    result = lax.all_gather(own_out, "tensor", axis=0, tiled=True)
    return (result, y_norm, (state_end, segment_end))


def grad_term(y_norm, cot_rows):
    return lax.dot_general(
        y_norm, cot_rows, (((0,), (0,)), ((), ())), preferred_element_type=jnp.float32
    )


def per_device(
    tokens,
    base_rows,
    baseline_owner,
    cotangent,
    pre_gain,
    input_proj,
    gate_proj,
    state_proj,
    step_proj,
    step_bias,
    decay_log,
    skip_gain,
    norm_gain,
    out_proj,
):
    dp_count = lax.axis_size("dp")
    tok_rows, feat_width = tokens.shape
    slot_cap = 2 * tok_rows // dp_count
    own_slots = slot_cap * dp_count
    index, starts, ends, owner_start = layout_tables(base_rows, baseline_owner)
    local = jnp.arange(tok_rows, dtype=jnp.int32)
    inside = ((starts[None, :] <= local[:, None]) & (local[:, None] < ends[None, :])).astype(
        jnp.int32
    )
    row_start = jnp.sum(inside * starts[None, :], axis=1)
    row_owner = jnp.sum(inside * baseline_owner[None, :], axis=1)
    row_ostart = jnp.sum(inside * owner_start[None, :], axis=1)
    send_slot = row_owner * slot_cap + row_ostart + local - row_start
    outgoing = (
        jnp.zeros((own_slots, feat_width), jnp.bfloat16)
        .at[send_slot]
        .set(tokens)
        .reshape(dp_count, slot_cap, feat_width)
    )
    owner_index = lax.axis_index("dp")
    place = jnp.arange(slot_cap, dtype=jnp.int32)
    held = (
        (baseline_owner[None, :] == owner_index)
        & (owner_start[None, :] <= place[:, None])
        & (place[:, None] < owner_start[None, :] + base_rows[None, :])
    ).astype(jnp.int32)
    got_start = jnp.sum(held * owner_start[None, :], axis=1)
    got_len = jnp.sum(held * base_rows[None, :], axis=1)
    got_id = jnp.sum(held * index[None, :], axis=1)
    got_any = jnp.sum(held, axis=1)
    sender = jnp.arange(dp_count, dtype=jnp.int32)[:, None]
    recv_slot = (
        dp_count * got_start[None, :]
        + sender * got_len[None, :]
        + place[None, :]
        - got_start[None, :]
    )
    recv_slot = jnp.where(got_any[None, :] > 0, recv_slot, own_slots).reshape(-1)
    id_rows = jnp.broadcast_to(got_id[None, :], (dp_count, slot_cap)).reshape(-1)
    slot_ids = jnp.full((own_slots,), -1, jnp.int32).at[recv_slot].set(id_rows, mode="drop")
    arrived = lax.all_to_all(outgoing, "dp", split_axis=0, concat_axis=0, tiled=True)
    width = arrived.shape[-1]
    stream = (
        jnp.zeros((own_slots, width), jnp.bfloat16)
        .at[recv_slot]
        .set(arrived.reshape(-1, width), mode="drop")
    )
    starts_flag = jnp.concatenate(
        [jnp.ones((1,), jnp.int32), (slot_ids[1:] != slot_ids[:-1]).astype(jnp.int32)]
    )
    segment = jnp.cumsum(starts_flag)
    section_idx = lax.axis_index("section")
    params = (
        pre_gain[0],
        input_proj[0],
        gate_proj[0],
        state_proj[0],
        step_proj[0],
        step_bias[0],
        decay_log[0],
        skip_gain[0],
        norm_gain[0],
        out_proj[0],
    )
    local_heads = step_proj.shape[2]
    micro_rows = own_slots // MICRO
    zero_state = (jnp.zeros((local_heads, HEADDIM, NSTATE), jnp.float32), jnp.array(-1, jnp.int32))
    cot_own = cotangent[0]
    carried_state = zero_state
    handed = jnp.zeros((micro_rows, feat_width), jnp.bfloat16)
    outputs_all = jnp.zeros((own_slots, feat_width), jnp.bfloat16)
    grad_acc = jnp.zeros((out_proj.shape[1], feat_width), jnp.float32)
    for turn_index in range(MICRO + 1):
        micro_index = turn_index - section_idx
        active_turn = (micro_index >= 0) & (micro_index < MICRO)
        micro_index = jnp.clip(micro_index, 0, MICRO - 1)
        first_row = micro_index * micro_rows
        own_in = lax.dynamic_slice_in_dim(stream, first_row, micro_rows, 0)
        source = jnp.where(section_idx == 0, own_in, handed)
        seg_part = lax.dynamic_slice_in_dim(segment, first_row, micro_rows, 0)
        result, y_norm, moved = block_layer(source, seg_part, carried_state, params)
        carried_state = jax.tree.map(
            lambda new_val, old_val: jnp.where(active_turn, new_val, old_val), moved, carried_state
        )
        outputs_all = jnp.where(
            active_turn,
            lax.dynamic_update_slice_in_dim(outputs_all, result, first_row, 0),
            outputs_all,
        )
        cot_part = lax.dynamic_slice_in_dim(cot_own, first_row, micro_rows, 0)
        grad_acc = grad_acc + jnp.where(active_turn, grad_term(y_norm, cot_part), 0.0)
        if turn_index < MICRO:
            handed = from_behind(result, "section", 1)
    grad_share = lax.psum_scatter(
        grad_acc.astype(jnp.bfloat16), "dp", scatter_dimension=1, tiled=True
    )
    return (outputs_all[None], grad_share[None])


def solution(mesh):
    return jax.shard_map(
        per_device,
        mesh=mesh,
        in_specs=(
            P("dp", None),
            P(),
            P(),
            P("section", "dp", None),
            P("section", None),
            P("section", None, "tensor"),
            P("section", None, "tensor"),
            P("section", None, None),
            P("section", None, "tensor"),
            P("section", "tensor"),
            P("section", "tensor"),
            P("section", "tensor"),
            P("section", "tensor"),
            P("section", "tensor", None),
        ),
        out_specs=(P("section", "dp", None), P("section", "tensor", "dp")),
        check_vma=False,
    )
```

profile of v0, /device:TPU:9, one launch (start us, length us, event | category | flops | bytes accessed | tf_op | source)
XLA Modules:
  0.0 470.1 jit_solution(4971296607184869887)
XLA Ops:
  10.5 4.4 scatter_custom_fusion
  14.9 4.9 %all-to-all-start = ((bf16[4,128,2048]{2,1,0:T(8,128)(2,1)}), bf16[4,128,2048]{2,1,0:T(8,128)(2,1)}, u32[]{:S(2)}, u32[]{:S(2)}) async-start(bf16[4,128,2048]{2,1,0:T(8,128)(2,1)} %bitcast.300), calls=%async_computation | async-start | bytes 4194304 | tf_op jit(solution)/shard_map/all_to_all | solution.py:205
  20.8 2.4 scatter_custom_fusion.2
  24.8 39.4 %all-to-all-done = bf16[4,128,2048]{2,1,0:T(8,128)(2,1)} async-done(((bf16[4,128,2048]{2,1,0:T(8,128)(2,1)}), bf16[4,128,2048]{2,1,0:T(8,128)(2,1)}, u32[]{:S(2)}, u32[]{:S(2)}) %all-to-all-start) | async-done | bytes 2097184 | tf_op jit(solution)/shard_map/all_to_all | solution.py:205
  64.1 6.1 %scatter_custom_fusion.1 = bf16[512,2048]{1,0:T(8,128)(2,1)} fusion(s32[512]{0:T(512)S(1)} %bitcast.321, bf16[512,2048]{1,0:T(8,128)(2,1)} %bitcast.31, bf16[]{:T(256)} %constant.122.clone.1), kind=kCustom, calls=%fused_computation.183 | custom fusion | bytes 2097664 | tf_op jit(solution)/shard_map/scatter | solution.py:210
  70.3 1.6 multiply_reduce_fusion.2
  71.9 1.7 compare_select_fusion.2
  74.4 2.2 multiply_convert_fusion.20
  79.4 33.1 %while.45 = (s32[]{:T(128)}, f32[8,64,128]{2,1,0:T(8,128)S(1)}, s32[]{:T(128)}, f32[4,64,8,64]{3,2,1,0:T(8,128)}, s32[4,64]{1,0:T(4,128)S(1)}, /*index=5*/f32[4,...) while((s32[]{:T(128)}, f32[8,64,128]{2,1,0:T(8,128)S(1)}, ...), condition=%wide.region_17.18_spmd.clone, body=%wide.region_15.17_spmd.clone.sunk | while | flops 22689996 | bytes 2389582 | solution.py:78
  112.5 1.5 reshape.687
  114.0 2.9 multiply_reduce_fusion.5
  116.9 7.9 %psum.21 = f32[256]{0:T(256)S(1)} all-reduce(f32[256]{0:T(256)S(1)} %get-tuple-element.392), channel_id=1, replica_groups=mesh['dp'=4,'section'=2,'tensor'=4] {'tensor'}, use_global_device_ids=true, to_apply=%region_19.20 | all-reduce | flops 256 | bytes 2048 | tf_op jit(solution)/shard_map/psum | solution.py:126
  124.8 3.4 convolution_convert_fusion.2
  128.3 2.8 fusion.116
  131.1 28.3 %reduce-scatter.5.cloned.1.call-done = bf16[64,2048]{1,0:T(8,128)(2,1)} async-done(((bf16[256,2048]{1,0:T(8,128)(2,1)}), bf16[64,2048]{1,0:T(8,128)(2,1)}) %reduce-scatter.5.cloned.1.call-update) | async-done | bytes 262160 | tf_op jit(solution)/shard_map/reduce_scatter | solution.py:131
  159.4 1.9 add_convert_fusion.3
  161.3 27.3 %all-gather.4.cloned.1.call-done = bf16[256,2048]{1,0:T(8,128)(2,1)} async-done(((bf16[64,2048]{1,0:T(8,128)(2,1)}), bf16[256,2048]{1,0:T(8,128)(2,1)}) %all-gather.4.cloned.1.call-update) | async-done | bytes 1048592 | tf_op jit(solution)/shard_map/all_gather | solution.py:139
  188.6 1.3 collective-permute-start
  190.6 2.9 collective-permute-done
  193.5 3.3 fusion.154
  201.0 1.1 reshape_reshape.10
  202.1 1.0 broadcast.407.clone2.1
  203.1 31.4 %while.43 = (s32[]{:T(128)}, f32[8,64,128]{2,1,0:T(8,128)S(1)}, s32[]{:T(128)}, f32[4,64,8,64]{3,2,1,0:T(8,128)}, s32[4,64]{1,0:T(4,128)}, /*index=5*/f32[4,64,8...) while((s32[]{:T(128)}, f32[8,64,128]{2,1,0:T(8,128)S(1)}, ...), condition=%wide.region_24.25_spmd, body=%wide.region_22.24_spmd.sunk | while | flops 22624460 | bytes 2581539 | solution.py:78
  234.5 2.3 reshape.692
  236.8 3.0 multiply_reduce_fusion.4
  239.8 7.1 %psum.22 = f32[256]{0:T(256)S(1)} all-reduce(f32[256]{0:T(256)S(1)} %get-tuple-element.394), channel_id=1, replica_groups=mesh['dp'=4,'section'=2,'tensor'=4] {'tensor'}, use_global_device_ids=true, to_apply=%region_26.27 | all-reduce | flops 256 | bytes 2048 | tf_op jit(solution)/shard_map/psum | solution.py:126
  247.0 3.4 convolution_convert_fusion.1
  250.4 28.7 %reduce-scatter.7.cloned.1.call-done = bf16[64,2048]{1,0:T(8,128)(2,1)} async-done(((bf16[256,2048]{1,0:T(8,128)(2,1)}), bf16[64,2048]{1,0:T(8,128)(2,1)}) %reduce-scatter.7.cloned.1.call-update) | async-done | bytes 262160 | tf_op jit(solution)/shard_map/reduce_scatter | solution.py:131
  279.2 1.9 add_convert_fusion.2
  281.1 27.0 %all-gather.6.cloned.1.call-done = bf16[256,2048]{1,0:T(8,128)(2,1)} async-done(((bf16[64,2048]{1,0:T(8,128)(2,1)}), bf16[256,2048]{1,0:T(8,128)(2,1)}) %all-gather.6.cloned.1.call-update) | async-done | bytes 1048592 | tf_op jit(solution)/shard_map/all_gather | solution.py:139
  308.1 1.5 collective-permute-start.1
  309.8 3.2 collective-permute-done.1
  313.0 3.3 fusion.153
  320.5 1.1 reshape_reshape.11
  321.6 1.0 broadcast.407.clone
  322.6 23.8 %while.44 = (s32[]{:T(128)}, f32[8,64,128]{2,1,0:T(8,128)S(1)}, s32[]{:T(128)}, f32[4,64,8,64]{3,2,1,0:T(8,128)}, s32[4,64]{1,0:T(4,128)S(1)}, /*index=5*/f32[4,...) while((s32[]{:T(128)}, f32[8,64,128]{2,1,0:T(8,128)S(1)}, ...), condition=%wide.region_31.32_spmd, body=%wide.region_29.31_spmd.sunk | while | flops 22624460 | bytes 2590267 | solution.py:78
  346.4 1.5 reshape.697
  347.9 2.9 multiply_reduce_fusion.3
  350.8 7.1 %psum.23 = f32[256]{0:T(256)S(1)} all-reduce(f32[256]{0:T(256)S(1)} %get-tuple-element.396), channel_id=1, replica_groups=mesh['dp'=4,'section'=2,'tensor'=4] {'tensor'}, use_global_device_ids=true, to_apply=%region_33.34 | all-reduce | flops 256 | bytes 2048 | tf_op jit(solution)/shard_map/psum | solution.py:126
  357.9 3.3 convolution_convert_fusion
  361.3 28.8 %reduce-scatter.9.cloned.1.call-done = bf16[64,2048]{1,0:T(8,128)(2,1)} async-done(((bf16[256,2048]{1,0:T(8,128)(2,1)}), bf16[64,2048]{1,0:T(8,128)(2,1)}) %reduce-scatter.9.cloned.1.call-update) | async-done | bytes 262160 | tf_op jit(solution)/shard_map/reduce_scatter | solution.py:131
  390.1 1.9 add_convert_fusion.1
  394.0 2.4 add_convert_fusion
  398.4 1.3 copy-done.1
  399.7 1.3 copy.198
  401.0 17.8 %all-gather.8.cloned.1.call-done = bf16[256,2048]{1,0:T(8,128)(2,1)} async-done(((bf16[64,2048]{1,0:T(8,128)(2,1)}), bf16[256,2048]{1,0:T(8,128)(2,1)}) %all-gather.8.cloned.1.call-update) | async-done | bytes 1048592 | tf_op jit(solution)/shard_map/all_gather | solution.py:139
  418.8 2.9 bitcast_dynamic-update-slice_fusion
  421.7 41.6 %reduce-scatter.11.cloned.1.call-done = bf16[512,512]{1,0:T(8,128)(2,1)} async-done(((bf16[512,2048]{1,0:T(8,128)(2,1)}), bf16[512,512]{1,0:T(8,128)(2,1)}) %reduce-scatter.11.cloned.1.call-update) | async-done | bytes 524304 | tf_op jit(solution)/shard_map/reduce_scatter | solution.py:258
  (443 shorter events, 94.6 us)
Async XLA Ops:
  7.2 384.9 %copy-start = (bf16[1,512,2048]{2,1,0:T(8,128)(2,1)S(1)}, bf16[1,512,2048]{2,1,0:T(8,128)(2,1)}, u32[]{:S(2)}) copy-start(bf16[1,512,2048]{2,1,0:T(8,128)(2,1)} %param.23) | copy-start | bytes 6291460
  14.9 5.0 %copy-start.30 = (f32[1,8]{1,0:T(1,128)S(1)}, f32[1,8]{1,0:T(1,128)}, u32[]{:S(2)}) copy-start(f32[1,8]{1,0:T(1,128)} %param.31) | copy-start | bytes 100
  14.9 5.7 %copy-start.22 = (s32[16]{0:T(128)S(1)}, s32[16]{0:T(128)}, u32[]{:S(2)}) copy-start(s32[16]{0:T(128)} %param.22) | copy-start | bytes 196
  14.9 5.7 %copy-start.21 = (s32[16]{0:T(128)S(1)}, s32[16]{0:T(128)}, u32[]{:S(2)}) copy-start(s32[16]{0:T(128)} %param.21) | copy-start | bytes 196
  14.9 9.8 %copy-start.43 = (f32[1,8]{1,0:T(1,128)S(1)}, f32[1,8]{1,0:T(1,128)}, u32[]{:S(2)}) copy-start(f32[1,8]{1,0:T(1,128)} %param.30) | copy-start | bytes 100
  14.9 49.2 %all-to-all-start = ((bf16[4,128,2048]{2,1,0:T(8,128)(2,1)}), bf16[4,128,2048]{2,1,0:T(8,128)(2,1)}, u32[]{:S(2)}, u32[]{:S(2)}) async-start(bf16[4,128,2048]{2,1,0:T(8,128)(2,1)} %bitcast.300), calls=%async_computation | async-start | bytes 4194304 | tf_op jit(solution)/shard_map/all_to_all | solution.py:205
  19.8 52.0 %copy-start.36 = (bf16[1,2048,8]{1,2,0:T(8,128)(2,1)S(1)}, bf16[1,2048,8]{1,2,0:T(8,128)(2,1)}, u32[]{:S(2)}) copy-start(bf16[1,2048,8]{1,2,0:T(8,128)(2,1)} %param.28) | copy-start | bytes 98308
  19.8 52.0 %copy-start.39 = (f32[1,2048]{1,0:T(1,128)S(1)}, f32[1,2048]{1,0:T(1,128)}, u32[]{:S(2)}) copy-start(f32[1,2048]{1,0:T(1,128)} %param.24) | copy-start | bytes 24580
  19.8 52.0 %copy-start.44 = (f32[1,8]{1,0:T(1,128)S(1)}, f32[1,8]{1,0:T(1,128)}, u32[]{:S(2)}) copy-start(f32[1,8]{1,0:T(1,128)} %param.29) | copy-start | bytes 100
  19.8 139.5 %reduce-scatter.5.cloned.1.call-start = ((), (), s32[]{:S(2)}) async-start(), calls=%async_computation.5 | async-start | bytes 1310720 | tf_op jit(solution)/shard_map/reduce_scatter | solution.py:131
  71.8 5.4 %copy-start.28 = (f32[256]{0:T(256)}, f32[256]{0:T(256)S(1)}, u32[]{:S(2)}) copy-start(f32[256]{0:T(256)S(1)} %add_rsqrt_fusion.5) | copy-start | bytes 3076
  74.4 2.9 copy-start.2
  74.4 2.9 copy-start.31
  79.4 4.2 copy-start.19
  87.7 4.2 copy-start.19
  96.0 4.2 copy-start.19
  101.0 2.7 copy-start.20
  104.3 4.2 copy-start.19
  109.2 2.7 copy-start.20
  114.0 10.8 %copy-start.11 = (f32[1,512]{1,0:T(1,128)S(1)}, f32[1,512]{1,0:T(1,128)}, u32[]{:S(2)}) copy-start(f32[1,512]{1,0:T(1,128)} %param.32) | copy-start | bytes 6148
  116.9 11.3 %copy-start.5 = (f32[256,512]{1,0:T(8,128)}, f32[256,512]{1,0:T(8,128)S(1)}, u32[]{:S(2)}) copy-start(f32[256,512]{1,0:T(8,128)S(1)} %get-tuple-element.393) | copy-start | bytes 1572868
  124.8 3.4 copy-start.15
  128.2 60.4 %all-gather.4.cloned.1.call-start = ((), (), s32[]{:S(2)}) async-start(), calls=%async_computation.6 | async-start | bytes 1310720 | tf_op jit(solution)/shard_map/all_gather | solution.py:139
  128.3 61.6 %copy-start.24 = (s32[256]{0:T(256)S(1)}, s32[256]{0:T(256)}, u32[]{:S(2)}) copy-start(s32[256]{0:T(256)} %get-tuple-element.388) | copy-start | bytes 3076
  161.3 117.9 %reduce-scatter.7.cloned.1.call-start = ((), (), s32[]{:S(2)}) async-start(), calls=%async_computation.7 | async-start | bytes 1310720 | tf_op jit(solution)/shard_map/reduce_scatter | solution.py:131
  188.6 4.9 %collective-permute-start = (bf16[256,2048]{1,0:T(8,128)(2,1)}, bf16[256,2048]{1,0:T(8,128)(2,1)}, u32[]{:S(2)}, u32[]{:S(2)}) collective-permute-start(bf16[256,2048]{1,0:T(8,128)(2,1)} %all-gather.4.cloned.1.call-done), channel_id=1, source_target_pairs={{0,4},{1,5},{2,6},{3,7},{8,12},{9,13},{10,14},{11,15},{16,20},{17,... | collective-permute-start | bytes 3145736 | tf_op jit(solution)/shard_map/ppermute | solution.py:19
  190.6 6.5 %copy-start.37 = (bf16[1,2048,8]{1,2,0:T(8,128)(2,1)S(1)}, bf16[1,2048,8]{1,2,0:T(8,128)(2,1)}, u32[]{:S(2)}) copy-start(bf16[1,2048,8]{1,2,0:T(8,128)(2,1)} %param.28) | copy-start | bytes 98308
  190.6 6.5 %copy-start.40 = (f32[1,2048]{1,0:T(1,128)S(1)}, f32[1,2048]{1,0:T(1,128)}, u32[]{:S(2)}) copy-start(f32[1,2048]{1,0:T(1,128)} %param.24) | copy-start | bytes 24580
  190.6 6.5 %copy-start.45 = (f32[1,8]{1,0:T(1,128)S(1)}, f32[1,8]{1,0:T(1,128)}, u32[]{:S(2)}) copy-start(f32[1,8]{1,0:T(1,128)} %param.29) | copy-start | bytes 100
  239.8 10.6 %copy-start.7 = (f32[256,512]{1,0:T(8,128)}, f32[256,512]{1,0:T(8,128)S(1)}, u32[]{:S(2)}) copy-start(f32[256,512]{1,0:T(8,128)S(1)} %get-tuple-element.395) | copy-start | bytes 1572868
  250.3 59.3 %copy-start.23 = (s32[256]{0:T(256)S(1)}, s32[256]{0:T(256)}, u32[]{:S(2)}) copy-start(s32[256]{0:T(256)} %get-tuple-element.387) | copy-start | bytes 3076
  250.4 57.7 %all-gather.6.cloned.1.call-start = ((), (), s32[]{:S(2)}) async-start(), calls=%async_computation.8 | async-start | bytes 1310720 | tf_op jit(solution)/shard_map/all_gather | solution.py:139
  281.1 109.0 %reduce-scatter.9.cloned.1.call-start = ((), (), s32[]{:S(2)}) async-start(), calls=%async_computation.9 | async-start | bytes 1310720 | tf_op jit(solution)/shard_map/reduce_scatter | solution.py:131
  308.1 4.9 %collective-permute-start.1 = (bf16[256,2048]{1,0:T(8,128)(2,1)}, bf16[256,2048]{1,0:T(8,128)(2,1)}, u32[]{:S(2)}, u32[]{:S(2)}) collective-permute-start(bf16[256,2048]{1,0:T(8,128)(2,1)} %all-gather.6.cloned.1.call-done), channel_id=1, source_target_pairs={{0,4},{1,5},{2,6},{3,7},{8,12},{9,13},{10,14},{11,15},{16,20},{17,... | collective-permute-start | bytes 3145736 | tf_op jit(solution)/shard_map/ppermute | solution.py:19
  309.7 6.9 %copy-start.38 = (bf16[1,2048,8]{1,2,0:T(8,128)(2,1)S(1)}, bf16[1,2048,8]{1,2,0:T(8,128)(2,1)}, u32[]{:S(2)}) copy-start(bf16[1,2048,8]{1,2,0:T(8,128)(2,1)} %param.28) | copy-start | bytes 98308
  309.7 6.9 %copy-start.41 = (f32[1,2048]{1,0:T(1,128)S(1)}, f32[1,2048]{1,0:T(1,128)}, u32[]{:S(2)}) copy-start(f32[1,2048]{1,0:T(1,128)} %param.24) | copy-start | bytes 24580
  309.8 6.9 %copy-start.46 = (f32[1,8]{1,0:T(1,128)S(1)}, f32[1,8]{1,0:T(1,128)}, u32[]{:S(2)}) copy-start(f32[1,8]{1,0:T(1,128)} %param.29) | copy-start | bytes 100
  322.6 25.3 %copy-start.25 = (f32[512]{0:T(512)S(1)}, f32[512]{0:T(512)}, u32[]{:S(2)}) copy-start(f32[512]{0:T(512)} %mul.551) | copy-start | bytes 6148
  322.6 25.3 %copy-start.27 = (f32[256]{0:T(256)S(1)}, f32[256]{0:T(256)}, u32[]{:S(2)}) copy-start(f32[256]{0:T(256)} %copy-done.26) | copy-start | bytes 3076
  322.6 25.3 %copy-start.42 = (f32[1,2048]{1,0:T(1,128)S(1)}, f32[1,2048]{1,0:T(1,128)}, u32[]{:S(2)}) copy-start(f32[1,2048]{1,0:T(1,128)} %param.24) | copy-start | bytes 24580
  325.1 2.8 copy-start.18
  331.1 2.8 copy-start.18
  337.0 2.8 copy-start.18
  343.0 2.8 copy-start.18
  361.3 30.8 %copy-start.6 = (f32[256,512]{1,0:T(8,128)S(1)}, f32[256,512]{1,0:T(8,128)}, u32[]{:S(2)}) copy-start(f32[256,512]{1,0:T(8,128)} %copy-done.5) | copy-start | bytes 1572868
  361.3 30.8 %copy-start.16 = (f32[256]{0:T(256)S(1)}, f32[256]{0:T(256)}, u32[]{:S(2)}) copy-start(f32[256]{0:T(256)} %copy-done.15) | copy-start | bytes 3076
  361.3 57.5 %all-gather.8.cloned.1.call-start = ((), (), s32[]{:S(2)}) async-start(), calls=%async_computation.10 | async-start | bytes 1310720 | tf_op jit(solution)/shard_map/all_gather | solution.py:139
  392.0 71.2 %reduce-scatter.11.cloned.1.call-start = ((), (), s32[]{:S(2)}) async-start(), calls=%async_computation.11 | async-start | bytes 2621440 | tf_op jit(solution)/shard_map/reduce_scatter | solution.py:258
  (21 other events, 35.8 us)
Sparse Core Ops, SparseCore 0:
  128.3 30.9 reduce-scatter.4
  161.9 26.6 all-gather.3
  250.5 28.6 reduce-scatter.6
  281.4 26.6 all-gather.5
  361.4 28.6 reduce-scatter.8
  392.1 26.6 all-gather.7
  421.8 41.4 reduce-scatter.10
where the time goes:
time: 477 us; the launch traced here: 470 us
  waiting for transfers between devices  245 us (51%)
  local copies, waits for them, and re-layouts  66.7 us (14%)
  matrix products  51.8 us (11%)
  other arithmetic  45.5 us (10%)
  blocking collectives  22.2 us (5%)
  loops' own time  16.2 us (3%)
  between operations  14.8 us (3%)
  starting transfers between devices  7.97 us (2%)
    reduce_scatter x3, waiting for transfers between devices, block_layer(): lax.psum_scatter(jnp.dot(y_norm, out_proj, preferred_element_type=jnp.flo...  85.8 us
    all_gather x3, waiting for transfers between devices, block_layer(): result = lax.all_gather(own_out, 'tensor', axis=0, tiled=True)  72.1 us
    reduce_scatter x1, waiting for transfers between devices, per_device(): lax.psum_scatter(grad_acc.astype(jnp.bfloat16), 'dp', scatter_dimension=1...  41.6 us
    all_to_all x1, waiting for transfers between devices, per_device(): lax.all_to_all(outgoing, 'dp', split_axis=0, concat_axis=0, tiled=True)  39.4 us
    psum x3, blocking collectives, block_layer(): sq_sum = lax.psum(jnp.sum(gated * gated, axis=-1), 'tensor')  22.2 us
    another operation x3, loops' own time, block_scan(): lax.scan(advance, (state, prev_segment), scanned)  16.2 us
    dynamic_update_slice x24, local copies, waits for them, and re-layouts, block_scan(): lax.scan(advance, (state, prev_segment), scanned)  10.5 us
    dot_general x3, matrix products, block_layer(): jnp.dot(y_norm, out_proj, preferred_element_type=jnp.float32)  10 us
  transfers between devices with their start and end apart: 10, of which 10 were waited for; matrix products, arithmetic and copies ran while one was open for 4% of the time, Pallas kernels for 0%

commit v1 on v0

v1 whole, which is shorter than its diff:
```python
import functools

import jax
import jax.numpy as jnp
from jax import lax
from jax.experimental import pallas as pl
from jax.experimental.pallas import tpu as pltpu
from jax.sharding import PartitionSpec as P

HEADDIM = 64
NSTATE = 128
MICRO = 2
TILE = 128
EXTRA = 16
EPS = 1e-05
LOG2E = 1.4426950408889634
F32 = jnp.float32
BF16 = jnp.bfloat16
VMEM_LIMIT = 48 * 1024 * 1024

NN = (((1,), (0,)), ((), ()))
NT = (((1,), (1,)), ((), ()))
TN = (((0,), (0,)), ((), ()))


def mm(a, b, dims=NN):
    return lax.dot_general(a, b, dims, preferred_element_type=F32)


def split3(value):
    high = value.astype(BF16)
    rest = value - high.astype(F32)
    mid = rest.astype(BF16)
    low = (rest - mid.astype(F32)).astype(BF16)
    return high, mid, low


def silu(x):
    return x * (1.0 / (1.0 + jnp.exp(-x)))


def iota(shape, axis):
    return lax.broadcasted_iota(jnp.int32, shape, axis)


def vmem():
    return pl.BlockSpec(memory_space=pltpu.VMEM)


def smem():
    return pl.BlockSpec(memory_space=pltpu.SMEM)


def params():
    return pltpu.CompilerParams(vmem_limit_bytes=VMEM_LIMIT)


def cost(flops, moved):
    return pl.CostEstimate(flops=int(flops), bytes_accessed=int(moved), transcendentals=0)


def walk_baselines(rows_ref, owner_ref, count_ref, dp_count, visit):
    for owner in range(dp_count):
        count_ref[owner] = 0

    def step(b, start):
        owner = owner_ref[b]
        length = rows_ref[b]
        owner_start = count_ref[owner]
        visit(b, owner, length, start, owner_start)
        count_ref[owner] = owner_start + length
        return start + length

    lax.fori_loop(0, rows_ref.shape[0], step, jnp.int32(0))


def select_kernel(dp_count, cap, pos_ref, rows_ref, owner_ref, tokens_ref, *refs):
    outs, (slot_ref, count_ref) = refs[:dp_count], refs[dp_count:]
    me, part = pos_ref[0], pos_ref[1]
    tok_rows = tokens_ref.shape[0]
    width = outs[0].shape[1]
    local = iota((8, tok_rows), 1)
    slot_ref[...] = jnp.full((8, tok_rows), -1, jnp.int32)

    def visit(b, owner, length, start, owner_start):
        inside = (local >= start) & (local < start + length)
        slot_ref[...] = jnp.where(inside, local + (owner * cap + owner_start - start), slot_ref[...])

    walk_baselines(rows_ref, owner_ref, count_ref, dp_count, visit)
    columns = tokens_ref[:, pl.ds(pl.multiple_of(part * width, width), width)]
    slots = slot_ref[0:1, :]
    for k in range(dp_count):
        owner = lax.rem(me + k, dp_count)
        chosen = (iota((cap, tok_rows), 0) + owner * cap) == slots
        outs[k][...] = mm(chosen.astype(F32).astype(BF16), columns).astype(BF16)


def place_kernel(dp_count, cap, pos_ref, rows_ref, owner_ref, *refs):
    arrived = refs[:dp_count]
    outs = refs[dp_count : dp_count + MICRO]
    seg_ref, slot_ref, count_ref, packed_ref = refs[dp_count + MICRO :]
    me = pos_ref[0]
    own_slots = seg_ref.shape[0]
    arrival = iota((8, own_slots), 1)
    turn = arrival // cap
    place = arrival - turn * cap
    sender = lax.rem(me - turn + dp_count, dp_count)
    slot_ref[...] = jnp.full((8, own_slots), -1, jnp.int32)
    position = iota((own_slots, TILE), 0)
    seg_ref[...] = jnp.zeros((own_slots, TILE), jnp.int32)

    def visit(b, owner, length, start, owner_start):
        @pl.when(owner == me)
        def _():
            inside = (place >= owner_start) & (place < owner_start + length)
            slot = dp_count * owner_start + sender * length + place - owner_start
            slot_ref[...] = jnp.where(inside, slot, slot_ref[...])
            seg_ref[...] = jnp.where(
                position >= dp_count * owner_start, dp_count * owner_start, seg_ref[...]
            )

    walk_baselines(rows_ref, owner_ref, count_ref, dp_count, visit)
    filled = dp_count * count_ref[me]
    seg_ref[...] = jnp.where(position >= filled, filled, seg_ref[...])
    for k in range(dp_count):
        packed_ref[k * cap : (k + 1) * cap, :] = arrived[k][...]
    micro_rows = own_slots // MICRO
    for m in range(MICRO):
        chosen = (iota((micro_rows, own_slots), 0) + m * micro_rows) == slot_ref[0:1, :]
        outs[m][...] = mm(chosen.astype(F32).astype(BF16), packed_ref[...]).astype(BF16)


def layer_kernel(micro, tensor, band, pos_ref, *refs):
    (blocks, refs) = (refs[:tensor], refs[tensor:])
    (seg_ref, gain_ref, win_ref, wgate_ref, wstate_ref, wstep_ref, bias_ref, decay_ref) = refs[:8]
    (skip_ref, ngain_ref, wout_ref) = refs[8:11]
    refs = refs[11:]
    prev = None
    if micro > 0:
        prev, refs = refs[:4], refs[4:]
    outs, refs = refs[:tensor], refs[tensor:]
    gn_ref, xdt_ref, b_ref, cumt_ref, a_ref = refs[:5]
    normed_ref, xs_ref, z_ref, c_ref, y_ref = refs[5:]
    part = pos_ref[1]
    rows, width = blocks[0].shape
    inner = win_ref.shape[1]
    depth = width * tensor
    square = jnp.zeros((rows, 1), F32)
    for block in blocks:
        value = block[...].astype(F32)
        square = square + jnp.sum(value * value, axis=1, keepdims=True)
    scale = lax.rsqrt(square * (1.0 / depth) + EPS)
    for k, block in enumerate(blocks):
        columns = pl.ds(pl.multiple_of((part ^ k) * width, width), width)
        normed_ref[:, columns] = (block[...].astype(F32) * scale * gain_ref[:, columns]).astype(BF16)
    normed = normed_ref[...]
    state_io = silu(mm(normed, wstate_ref[...])).astype(BF16)
    b_ref[...] = state_io[:, :NSTATE]
    c_ref[...] = state_io[:, NSTATE:]
    pre = mm(normed, wstep_ref[...]) + bias_ref[...]
    step = jnp.maximum(pre, 0.0) + jnp.log1p(jnp.exp(-jnp.abs(pre)))
    heads = inner // HEADDIM
    xs = silu(mm(normed, win_ref[...])).astype(BF16)
    xs_ref[...] = xs
    spread = (iota((TILE, inner), 1) // HEADDIM == iota((TILE, inner), 0)).astype(F32).astype(BF16)
    step_wide = sum(mm(piece, spread) for piece in split3(step))
    xdt_ref[...] = (step_wide * xs.astype(F32)).astype(BF16)
    z_ref[...] = mm(normed, wgate_ref[...])
    a_ref[...] = step * (jnp.exp(decay_ref[...]) * (-LOG2E))

    tiles = rows // TILE
    first = micro * tiles

    def key_rows(ref_now, ref_before, tile):
        if tile >= first:
            return ref_now[(tile - first) * TILE : (tile - first + 1) * TILE, :]
        return ref_before[(tile - first + tiles) * TILE : (tile - first + tiles + 1) * TILE, :]

    before = prev if prev is not None else (None,) * 4
    lane = iota((TILE, TILE), 1)
    low_half = lane < HEADDIM
    nothing = jnp.zeros((TILE, TILE), BF16)
    for q in range(first, first + tiles):
        here = (q - first) * TILE
        keys = [k for k in range(max(0, q - band), q + 1)]
        seg = seg_ref[here : here + TILE, :]
        row_at = iota((TILE, TILE), 0) + q * TILE
        c_rows = c_ref[here : here + TILE, :]
        scores = []
        cum = jnp.zeros((TILE, TILE), F32)
        for k in keys:
            at = lane + k * TILE
            valid = at >= seg
            if k == q:
                valid = valid & (at <= row_at)
            scores.append(jnp.where(valid, mm(c_rows, key_rows(b_ref, before[1], k), NT), 0.0))
            ones = jnp.where(valid, 1.0, 0.0).astype(BF16)
            for piece in split3(key_rows(a_ref, before[3], k)):
                cum = cum + mm(ones, piece)
        cumt_ref[here : here + TILE, :] = cum.T
        cum_rows = [key_rows(cumt_ref, before[2], k) for k in keys]
        for pair in range(heads // 2):
            total = jnp.zeros((TILE, TILE), F32)
            for half in range(2):
                h = 2 * pair + half
                own = jnp.broadcast_to(cum[:, h : h + 1], (TILE, TILE))
                for k, score, cum_row in zip(keys, scores, cum_rows):
                    weight = jnp.exp2(jnp.minimum(own - cum_row[h : h + 1, :], 0.0)) * score
                    x_rows = key_rows(xdt_ref, before[0], k)[:, pair * TILE : (pair + 1) * TILE]
                    keep = low_half if half == 0 else ~low_half
                    x_rows = jnp.where(keep, x_rows, nothing)
                    total = total + mm(weight.astype(BF16), x_rows)
            y_ref[here : here + TILE, pair * TILE : (pair + 1) * TILE] = total

    gated = (y_ref[...] + skip_ref[...] * xs_ref[...].astype(F32)) * silu(z_ref[...])
    sq = gated * gated
    sq_high = sq.astype(BF16)
    sq_low = (sq - sq_high.astype(F32)).astype(BF16)
    ones = jnp.ones((EXTRA, inner), BF16)
    sums = mm(ones, sq_high, NT) + mm(ones, sq_low, NT)
    high, mid, low = split3(sums)
    row = iota(sums.shape, 0)
    zero = jnp.zeros(sums.shape, F32)
    message = jnp.where(
        row == 0,
        high.astype(F32),
        jnp.where(row == 1, mid.astype(F32), jnp.where(row == 2, low.astype(F32), zero)),
    ).astype(BF16)
    gn = (gated * ngain_ref[...]).astype(BF16)
    gn_ref[...] = gn
    for k, out in enumerate(outs):
        columns = pl.ds(pl.multiple_of((part ^ k) * width, width), width)
        out[0:rows, :] = mm(gn, wout_ref[:, columns]).astype(BF16)
        out[rows : rows + EXTRA, :] = jnp.zeros((EXTRA, width), BF16)
        out[rows : rows + EXTRA, 0:rows] = message


def sum_kernel(tensor, inner_all, *refs):
    parts, (residual_ref, gn_ref, out_ref, y_ref) = refs[:tensor], refs[tensor:]
    rows, width = residual_ref.shape
    ones = jnp.ones((EXTRA, TILE), BF16)
    square = sum(mm(part[rows : rows + EXTRA, 0:rows], ones, TN) for part in parts)
    scale = lax.rsqrt(square * (1.0 / inner_all) + EPS)
    for c in range(0, width, TILE):
        total = sum(part[0:rows, c : c + TILE].astype(F32) for part in parts)
        out_ref[:, c : c + TILE] = (
            residual_ref[:, c : c + TILE].astype(F32) + total * scale
        ).astype(BF16)
    for c in range(0, gn_ref.shape[1], TILE):
        y_ref[:, c : c + TILE] = (gn_ref[:, c : c + TILE].astype(F32) * scale).astype(BF16)


def grad_kernel(dp_count, pos_ref, *refs):
    ys, (cot_ref,), outs = refs[:MICRO], refs[MICRO : MICRO + 1], refs[MICRO + 1 :]
    me = pos_ref[0]
    rows = ys[0].shape[0]
    width = outs[0].shape[1]
    for k, out in enumerate(outs):
        columns = pl.ds(pl.multiple_of(lax.rem(me + k, dp_count) * width, width), width)
        total = 0.0
        for m in range(MICRO):
            total = total + mm(ys[m][...], cot_ref[m * rows : (m + 1) * rows, columns], TN)
        out[...] = total.astype(BF16)


def whole_grad_kernel(*refs):
    ys, (cot_ref, out_ref) = refs[:MICRO], refs[MICRO:]
    rows = ys[0].shape[0]
    total = 0.0
    for m in range(MICRO):
        total = total + mm(ys[m][...], cot_ref[m * rows : (m + 1) * rows, :], TN)
    out_ref[...] = total.astype(BF16)


def assemble_kernel(tensor, pos_ref, *refs):
    out_ref = refs[-1]
    part = pos_ref[1]
    for m in range(MICRO):
        for k in range(tensor):
            block = refs[m * tensor + k]
            rows, width = block.shape
            columns = pl.ds(pl.multiple_of((part ^ k) * width, width), width)
            out_ref[0, m * rows : (m + 1) * rows, columns] = block[...]


def tensor_exchange(values, sections):
    count = lax.axis_size("tensor")
    return [values[0]] + [
        lax.ppermute(
            values[k],
            ("section", "tensor"),
            [(s * count + t, s * count + (t ^ k)) for s in sections for t in range(count)],
        )
        for k in range(1, count)
    ]


def dp_exchange(values, section):
    count = lax.axis_size("dp")
    return [values[0]] + [
        lax.ppermute(
            values[k],
            ("dp", "section"),
            [(d * 2 + section, (d + k) % count * 2 + section) for d in range(count)],
        )
        for k in range(1, count)
    ]


def hand_over(value):
    count = lax.axis_size("tensor")
    return [
        lax.ppermute(value, ("section", "tensor"), [(t, count + (t ^ k)) for t in range(count)])
        for k in range(count)
    ]


def per_device(
    tokens,
    base_rows,
    baseline_owner,
    cotangent,
    pre_gain,
    input_proj,
    gate_proj,
    state_proj,
    step_proj,
    step_bias,
    decay_log,
    skip_gain,
    norm_gain,
    out_proj,
):
    dp_count = lax.axis_size("dp")
    tensor = lax.axis_size("tensor")
    tok_rows, feat = tokens.shape
    cap = 2 * tok_rows // dp_count
    own_slots = cap * dp_count
    width = feat // tensor
    micro_rows = own_slots // MICRO
    inner = input_proj.shape[2]
    heads = step_proj.shape[2]
    longest = 3 * tok_rows // base_rows.shape[0] * dp_count
    band = (longest - 1 + TILE - 1) // TILE
    dp_at = lax.axis_index("dp")
    section = lax.axis_index("section")
    pos = jnp.stack([dp_at, lax.axis_index("tensor")]).astype(jnp.int32)
    shape = jax.ShapeDtypeStruct
    tables = (pos, base_rows, baseline_owner)

    outgoing = pl.pallas_call(
        functools.partial(select_kernel, dp_count, cap),
        out_shape=[shape((cap, width), BF16)] * dp_count,
        in_specs=[smem()] * 3 + [vmem()],
        out_specs=[vmem()] * dp_count,
        scratch_shapes=[pltpu.VMEM((8, tok_rows), jnp.int32), pltpu.SMEM((dp_count,), jnp.int32)],
        compiler_params=params(),
        name="select_rows",
    )(*tables, tokens)
    arrived = dp_exchange(outgoing, 0)
    *own_blocks, seg = pl.pallas_call(
        functools.partial(place_kernel, dp_count, cap),
        out_shape=[shape((micro_rows, width), BF16)] * MICRO + [shape((own_slots, TILE), jnp.int32)],
        in_specs=[smem()] * 3 + [vmem()] * dp_count,
        out_specs=[vmem()] * (MICRO + 1),
        scratch_shapes=[
            pltpu.VMEM((8, own_slots), jnp.int32),
            pltpu.SMEM((dp_count,), jnp.int32),
            pltpu.VMEM((own_slots, width), BF16),
        ],
        compiler_params=params(),
        name="place_rows",
    )(*tables, *arrived)

    def lanes(value):
        return jnp.pad(value, ((0, 0), (0, TILE - heads)))

    weights = (
        pre_gain,
        input_proj[0],
        gate_proj[0],
        state_proj[0],
        lanes(step_proj[0]),
        lanes(step_bias),
        lanes(decay_log),
        jnp.repeat(skip_gain, HEADDIM, axis=1),
        norm_gain,
        out_proj[0],
    )

    def layer(micro, blocks, carried):
        seg_part = seg[micro * micro_rows : (micro + 1) * micro_rows]
        prev = () if micro == 0 else carried
        got = pl.pallas_call(
            functools.partial(layer_kernel, micro, tensor, band),
            out_shape=[shape((micro_rows + EXTRA, width), BF16)] * tensor
            + [
                shape((micro_rows, inner), BF16),
                shape((micro_rows, inner), BF16),
                shape((micro_rows, NSTATE), BF16),
                shape((micro_rows, TILE), F32),
                shape((micro_rows, TILE), F32),
            ],
            in_specs=[smem()] + [vmem()] * (tensor + 1 + len(weights) + len(prev)),
            out_specs=[vmem()] * (tensor + 5),
            scratch_shapes=[
                pltpu.VMEM((micro_rows, feat), BF16),
                pltpu.VMEM((micro_rows, inner), BF16),
                pltpu.VMEM((micro_rows, inner), F32),
                pltpu.VMEM((micro_rows, NSTATE), BF16),
                pltpu.VMEM((micro_rows, inner), F32),
            ],
            compiler_params=params(),
            cost_estimate=cost(2 * micro_rows * feat * (3 * inner + 512), 12e6),
            name="layer_part",
        )(pos, *blocks, seg_part, *weights, *prev)
        parts, gn, carry = got[:tensor], got[tensor], got[tensor + 1 :]
        return parts, gn, carry

    def finish(parts, residual, gn):
        return pl.pallas_call(
            functools.partial(sum_kernel, tensor, inner * tensor),
            out_shape=[shape((micro_rows, width), BF16), shape((micro_rows, inner), BF16)],
            in_specs=[vmem()] * (tensor + 2),
            out_specs=[vmem()] * 2,
            compiler_params=params(),
            cost_estimate=cost(1e6, 3e6),
            name="sum_parts",
        )(*parts, residual, gn)

    def block(sources, active):
        results, ys, carried = [], [], None
        for micro in range(MICRO):
            parts, gn, carried = layer(micro, sources[micro], carried)
            parts = tensor_exchange(parts, (active,))
            result, y = finish(parts, sources[micro][0], gn)
            results.append(result)
            ys.append(y)
        return results, ys

    def gradient(ys, active):
        grad_width = feat // dp_count
        direct = grad_width % TILE == 0
        out_shape = [shape((inner, grad_width), BF16)] * dp_count if direct else [shape((inner, feat), BF16)]
        kernel = functools.partial(grad_kernel, dp_count) if direct else whole_grad_kernel
        head = (pos,) if direct else ()
        got = pl.pallas_call(
            kernel,
            out_shape=out_shape,
            in_specs=[smem()] * len(head) + [vmem()] * (MICRO + 1),
            out_specs=[vmem()] * len(out_shape),
            compiler_params=params(),
            cost_estimate=cost(2 * own_slots * inner * feat, 5e6),
            name="gradient_terms",
        )(*head, *ys, cotangent[0])
        if not direct:
            return lax.psum_scatter(got[0], "dp", scatter_dimension=1, tiled=True)
        terms = dp_exchange(got, active)
        return sum(term.astype(F32) for term in terms).astype(BF16)

    sources = [tensor_exchange([own] * tensor, (0,)) for own in own_blocks]
    latent, enc_ys = block(sources, 0)
    enc_grad = gradient(enc_ys, 0)
    rebuilt, dec_ys = block([hand_over(value) for value in latent], 1)
    dec_grad = gradient(dec_ys, 1)
    first = section == 0
    finals = []
    for micro in range(MICRO):
        own = jnp.where(first, latent[micro], rebuilt[micro])
        finals.extend(tensor_exchange([own] * tensor, (0, 1)))
    activations = pl.pallas_call(
        functools.partial(assemble_kernel, tensor),
        out_shape=shape((1, own_slots, feat), BF16),
        in_specs=[smem()] + [vmem()] * len(finals),
        out_specs=vmem(),
        compiler_params=params(),
        cost_estimate=cost(1e6, 4e6),
        name="assemble_rows",
    )(pos, *finals)
    return activations, jnp.where(first, enc_grad, dec_grad)[None]


def solution(mesh):
    return jax.shard_map(
        per_device,
        mesh=mesh,
        in_specs=(
            P("dp", None),
            P(),
            P(),
            P("section", "dp", None),
            P("section", None),
            P("section", None, "tensor"),
            P("section", None, "tensor"),
            P("section", None, None),
            P("section", None, "tensor"),
            P("section", "tensor"),
            P("section", "tensor"),
            P("section", "tensor"),
            P("section", "tensor"),
            P("section", "tensor", None),
        ),
        out_specs=(P("section", "dp", None), P("section", "tensor", "dp")),
        check_vma=False,
    )
```

time: 477 us -> 192 us (0.40)
  the two profiles are of different devices: /device:TPU:9 before, /device:TPU:29 now
where the time goes in v1:
time: 192 us; the launch traced here: 191 us
  waiting for transfers between devices  81.4 us (42%)
  starting transfers between devices  53.9 us (28%)
  Pallas kernels  42 us (22%)
  local copies, waits for them, and re-layouts  9.87 us (5%)
  other arithmetic  2.54 us (1%)
    ppermute x8, waiting for transfers between devices, hand_over(): lax.ppermute(value, ('section', 'tensor'), [(t, count + (t ^ k)) for t in...  43.5 us
    pallas_call x4, Pallas kernels, layer(): pl.pallas_call(functools.partial(layer_kernel, micro, tensor, band), out_...  31.9 us
    ppermute x24, starting transfers between devices, tensor_exchange(): lax.ppermute(values[k], ('section', 'tensor'), [(s * count + t, s * count...  31.2 us
    ppermute x9, waiting for transfers between devices, dp_exchange(): lax.ppermute(values[k], ('dp', 'section'), [(d * 2 + section, (d + k) % c...  25.2 us
    ppermute x24, waiting for transfers between devices, tensor_exchange(): lax.ppermute(values[k], ('section', 'tensor'), [(s * count + t, s * count...  12.7 us
    ppermute x9, starting transfers between devices, dp_exchange(): lax.ppermute(values[k], ('dp', 'section'), [(d * 2 + section, (d + k) % c...  12 us
    ppermute x8, starting transfers between devices, hand_over(): lax.ppermute(value, ('section', 'tensor'), [(t, count + (t ^ k)) for t in...  10.6 us
    unnamed x37, local copies, waits for them, and re-layouts  7.62 us
  transfers between devices with their start and end apart: 41, of which 6 were waited for; matrix products, arithmetic and copies ran while one was open for 2% of the time, Pallas kernels for 21%

profile of v1, /device:TPU:29, one launch (start us, length us, event | category | flops | bytes accessed | tf_op | source)
XLA Modules:
  0.0 191.1 jit_solution(5947006968581681612)
XLA Ops:
  0.7 1.3 copy-done.1
  3.3 1.0 select_rows.1
  6.5 1.4 place_rows.1
  11.2 0.7 broadcast_in_dim.8
  12.0 1.0 copy.16
  15.3 7.2 %layer_part.4 = (bf16[272,512]{1,0:T(8,128)(2,1)S(1)}, bf16[272,512]{1,0:T(8,128)(2,1)S(1)}, bf16[272,512]{1,0:T(8,128)(2,1)S(1)}, bf16[272,512]{1,0:T(8,128)(2,...) custom-call(s32[2]{0:T(128)S(1)} %pad_add_fusion.pos_ref, ...), custom_call_target="tpu_custom_call" | custom-call | flops 2147483648 | bytes 12000000 | tf_op jit(solution)/shard_map/layer_part/pallas_call | solution.py:394
  24.6 8.3 %layer_part.6 = (bf16[272,512]{1,0:T(8,128)(2,1)S(1)}, bf16[272,512]{1,0:T(8,128)(2,1)S(1)}, bf16[272,512]{1,0:T(8,128)(2,1)S(1)}, bf16[272,512]{1,0:T(8,128)(2,...) custom-call(s32[2]{0:T(128)S(1)} %pad_add_fusion.pos_ref, ...), custom_call_target="tpu_custom_call" | custom-call | flops 2147483648 | bytes 12000000 | tf_op jit(solution)/shard_map/layer_part/pallas_call | solution.py:394
  35.4 1.3 collective-permute-start.12
  36.7 1.3 collective-permute-start.11
  38.0 1.3 collective-permute-start.10
  39.4 1.3 collective-permute-start.9
  41.1 1.4 collective-permute-start.28
  42.6 42.3 %collective-permute-done.12.refs_3_ = bf16[256,512]{1,0:T(8,128)(2,1)S(1)} collective-permute-done((bf16[256,512]{1,0:T(8,128)(2,1)S(1)}, bf16[256,512]{1,0:T(8,128)(2,1)S(1)}, u32[]{:S(2)}, u32[]{:S(2)}) %collective-permute-start.12) | collective-permute-done | bytes 262176 | tf_op jit(solution)/shard_map/ppermute | solution.py:313
  84.9 1.5 collective-permute-start.27
  86.3 1.2 collective-permute-done.11.refs_2_
  87.6 1.3 collective-permute-start.26
  88.9 1.3 collective-permute-start.25
  90.2 8.0 %layer_part.5 = (bf16[272,512]{1,0:T(8,128)(2,1)S(1)}, bf16[272,512]{1,0:T(8,128)(2,1)S(1)}, bf16[272,512]{1,0:T(8,128)(2,1)S(1)}, bf16[272,512]{1,0:T(8,128)(2,...) custom-call(s32[2]{0:T(128)S(1)} %pad_add_fusion.pos_ref, ...), custom_call_target="tpu_custom_call" | custom-call | flops 2147483648 | bytes 12000000 | tf_op jit(solution)/shard_map/layer_part/pallas_call | solution.py:394
  98.1 0.7 copy-done.2
  98.8 2.2 %collective-permute-start.13 = (bf16[272,512]{1,0:T(8,128)(2,1)S(1)}, bf16[272,512]{1,0:T(8,128)(2,1)S(1)}, u32[]{:S(2)}, u32[]{:S(2)}) collective-permute-start(bf16[272,512]{1,0:T(8,128)(2,1)S(1)} %get-tuple-element.66), channel_id=1, source_target_pairs={{4,5},{5,4},{6,7},{7,6},{12,13},{13,12},{14,15},{15,14},{20,21},{2... | collective-permute-start | bytes 835592 | tf_op jit(solution)/shard_map/ppermute | solution.py:289
  101.0 3.1 %collective-permute-start.14 = (bf16[272,512]{1,0:T(8,128)(2,1)S(1)}, bf16[272,512]{1,0:T(8,128)(2,1)S(1)}, u32[]{:S(2)}, u32[]{:S(2)}) collective-permute-start(bf16[272,512]{1,0:T(8,128)(2,1)S(1)} %get-tuple-element.67), channel_id=1, source_target_pairs={{4,6},{5,7},{6,4},{7,5},{12,14},{13,15},{14,12},{15,13},{20,22},{2... | collective-permute-start | bytes 835592 | tf_op jit(solution)/shard_map/ppermute | solution.py:289
  104.2 3.1 %collective-permute-start.15 = (bf16[272,512]{1,0:T(8,128)(2,1)}, bf16[272,512]{1,0:T(8,128)(2,1)S(1)}, u32[]{:S(2)}, u32[]{:S(2)}) collective-permute-start(bf16[272,512]{1,0:T(8,128)(2,1)} %get-tuple-element.68), channel_id=1, source_target_pairs={{4,7},{5,6},{6,5},{7,4},{12,15},{13,14},{14,13},{15,12},{20,23},{2... | collective-permute-start | bytes 835592 | tf_op jit(solution)/shard_map/ppermute | solution.py:289
  107.3 2.1 %gradient_terms.2 = (bf16[512,512]{1,0:T(8,128)(2,1)S(1)}, bf16[512,512]{1,0:T(8,128)(2,1)}, bf16[512,512]{1,0:T(8,128)(2,1)S(1)}, bf16[512,512]{1,0:T(8,128)(2,1)S(1)}) custom-call(s32[2]{0:T(128)S(1)} %pad_add_fusion.pos_ref, bf16[256,512]{1,0:T(8,128)(2,1)S(1)} %get-tuple-element.92.refs_0_, bf16[256,512]{1,0:T(8,128)(2,1)S(1)} %get-tuple-element.93.refs_1_, ...), custom_call_target="tpu_custom_call" | custom-call | flops 1073741824 | bytes 5000000 | tf_op jit(solution)/shard_map/gradient_terms/pallas_call | solution.py:447
  109.3 0.8 copy-done.14
  110.1 0.8 copy-done.16
  111.0 1.5 collective-permute-start.35
  112.4 8.4 %layer_part.7 = (bf16[272,512]{1,0:T(8,128)(2,1)S(1)}, bf16[272,512]{1,0:T(8,128)(2,1)}, bf16[272,512]{1,0:T(8,128)(2,1)}, bf16[272,512]{1,0:T(8,128)(2,1)}, bf1...) custom-call(s32[2]{0:T(128)S(1)} %pad_add_fusion.pos_ref, ...), custom_call_target="tpu_custom_call" | custom-call | flops 2147483648 | bytes 12000000 | tf_op jit(solution)/shard_map/layer_part/pallas_call | solution.py:394
  120.8 0.7 copy-done.4
  121.5 2.2 %collective-permute-start.29 = (bf16[272,512]{1,0:T(8,128)(2,1)}, bf16[272,512]{1,0:T(8,128)(2,1)S(1)}, u32[]{:S(2)}, u32[]{:S(2)}) collective-permute-start(bf16[272,512]{1,0:T(8,128)(2,1)} %get-tuple-element.87), channel_id=1, source_target_pairs={{4,5},{5,4},{6,7},{7,6},{12,13},{13,12},{14,15},{15,14},{20,21},{2... | collective-permute-start | bytes 835592 | tf_op jit(solution)/shard_map/ppermute | solution.py:289
  123.7 3.1 %collective-permute-start.30 = (bf16[272,512]{1,0:T(8,128)(2,1)}, bf16[272,512]{1,0:T(8,128)(2,1)S(1)}, u32[]{:S(2)}, u32[]{:S(2)}) collective-permute-start(bf16[272,512]{1,0:T(8,128)(2,1)} %get-tuple-element.88), channel_id=1, source_target_pairs={{4,6},{5,7},{6,4},{7,5},{12,14},{13,15},{14,12},{15,13},{20,22},{2... | collective-permute-start | bytes 835592 | tf_op jit(solution)/shard_map/ppermute | solution.py:289
  126.9 3.3 %collective-permute-start.31 = (bf16[272,512]{1,0:T(8,128)(2,1)}, bf16[272,512]{1,0:T(8,128)(2,1)S(1)}, u32[]{:S(2)}, u32[]{:S(2)}) collective-permute-start(bf16[272,512]{1,0:T(8,128)(2,1)} %get-tuple-element.89), channel_id=1, source_target_pairs={{4,7},{5,6},{6,5},{7,4},{12,15},{13,14},{14,13},{15,12},{20,23},{2... | collective-permute-start | bytes 835592 | tf_op jit(solution)/shard_map/ppermute | solution.py:289
  130.2 0.9 copy-done.3
  131.6 1.3 collective-permute-start.18
  133.5 11.1 %collective-permute-done.30.refs_2_ = bf16[272,512]{1,0:T(8,128)(2,1)S(1)} collective-permute-done((bf16[272,512]{1,0:T(8,128)(2,1)}, bf16[272,512]{1,0:T(8,128)(2,1)S(1)}, u32[]{:S(2)}, u32[]{:S(2)}) %collective-permute-start.30) | collective-permute-done | bytes 278560 | tf_op jit(solution)/shard_map/ppermute | solution.py:289
  144.6 1.6 collective-permute-start.16
  146.7 1.3 collective-permute-start.34
  148.2 1.2 collective-permute-start.32
  149.4 1.8 gradient_terms.3
  151.3 0.7 collective-permute-start.36
  152.0 0.7 collective-permute-start.37
  152.7 1.6 collective-permute-done.34.refs_7_
  154.3 2.1 %collective-permute-start.38 = (bf16[512,512]{1,0:T(8,128)(2,1)S(1)}, bf16[512,512]{1,0:T(8,128)(2,1)S(1)}, u32[]{:S(2)}, u32[]{:S(2)}) collective-permute-start(bf16[512,512]{1,0:T(8,128)(2,1)S(1)} %get-tuple-element.101), channel_id=1, source_target_pairs={{4,12},{12,20},{20,28},{28,4},{5,13},{13,21},{21,29},{29,5},{6,14}... | collective-permute-start | bytes 1572872 | tf_op jit(solution)/shard_map/ppermute | solution.py:301
  156.4 1.9 %collective-permute-start.39 = (bf16[512,512]{1,0:T(8,128)(2,1)S(1)}, bf16[512,512]{1,0:T(8,128)(2,1)S(1)}, u32[]{:S(2)}, u32[]{:S(2)}) collective-permute-start(bf16[512,512]{1,0:T(8,128)(2,1)S(1)} %get-tuple-element.102), channel_id=1, source_target_pairs={{4,20},{12,28},{20,4},{28,12},{5,21},{13,29},{21,5},{29,13},{6,22}... | collective-permute-start | bytes 1572872 | tf_op jit(solution)/shard_map/ppermute | solution.py:301
  158.4 3.2 %collective-permute-start.40 = (bf16[512,512]{1,0:T(8,128)(2,1)S(1)}, bf16[512,512]{1,0:T(8,128)(2,1)S(1)}, u32[]{:S(2)}, u32[]{:S(2)}) collective-permute-start(bf16[512,512]{1,0:T(8,128)(2,1)S(1)} %get-tuple-element.103), channel_id=1, source_target_pairs={{4,28},{12,4},{20,12},{28,20},{5,29},{13,5},{21,13},{29,21},{6,30}... | collective-permute-start | bytes 1572872 | tf_op jit(solution)/shard_map/ppermute | solution.py:301
  161.5 2.0 %assemble_rows.1 = bf16[1,512,2048]{2,1,0:T(8,128)(2,1)} custom-call(s32[2]{0:T(128)S(1)} %pad_add_fusion.pos_ref, bf16[256,512]{1,0:T(8,128)(2,1)S(1)} %broadcast_select_fusion.1.refs_0_, bf16[256,512]{1,0:T(8,128)(2,1)S(1)} %collective-permute-done.16.refs_1_, bf16[256,512]{1,0:T(8,128)(2,1)S(1)} %collective-permute-done.17.refs_2_, ...), custom_call_target="tpu_custom_call" | custom-call | flops 1000000 | bytes 4000000 | tf_op jit(solution)/shard_map/assemble_rows/pallas_call | solution.py:471
  163.6 8.2 %collective-permute-done.38 = bf16[512,512]{1,0:T(8,128)(2,1)S(1)} collective-permute-done((bf16[512,512]{1,0:T(8,128)(2,1)S(1)}, bf16[512,512]{1,0:T(8,128)(2,1)S(1)}, u32[]{:S(2)}, u32[]{:S(2)}) %collective-permute-start.38) | collective-permute-done | bytes 524320 | tf_op jit(solution)/shard_map/ppermute | solution.py:301
  171.7 17.0 %collective-permute-done.39 = bf16[512,512]{1,0:T(8,128)(2,1)S(1)} collective-permute-done((bf16[512,512]{1,0:T(8,128)(2,1)S(1)}, bf16[512,512]{1,0:T(8,128)(2,1)S(1)}, u32[]{:S(2)}, u32[]{:S(2)}) %collective-permute-start.39) | collective-permute-done | bytes 524320 | tf_op jit(solution)/shard_map/ppermute | solution.py:301
  188.7 2.4 %fusion.1 = bf16[1,512,512]{2,1,0:T(8,128)(2,1)} fusion(bf16[512,512]{1,0:T(8,128)(2,1)S(1)} %collective-permute-done.37, bf16[512,512]{1,0:T(8,128)(2,1)S(1)} %collective-permute-done.36, bf16[512,512]{1,0:T(8,128)(2,1)} %collective-permute-done.35, bf16[512,512]{1,0:T(8,128)(2,1)S(1)} %get-tuple-element.94, ...), kind=kLoop, calls=%fused_computation.3 | loop fusion | flops 4456448 | bytes 4718593 | tf_op jit(solution)/shard_map/broadcast_in_dim | solution.py:480
  (94 shorter events, 15.9 us)
Async XLA Ops:
  0.6 14.6 %copy-start = (bf16[1,2048,256]{2,1,0:T(8,128)(2,1)S(1)}, bf16[1,2048,256]{2,1,0:T(8,128)(2,1)}, u32[]{:S(2)}) copy-start(bf16[1,2048,256]{2,1,0:T(8,128)(2,1)} %param.21) | copy-start | bytes 3145732
  3.3 12.0 %copy-start.9 = (f32[1,512]{1,0:T(1,128)S(1)}, f32[1,512]{1,0:T(1,128)}, u32[]{:S(2)}) copy-start(f32[1,512]{1,0:T(1,128)} %refs_13_.7) | copy-start | bytes 6148
  4.4 2.0 %collective-permute-start = (bf16[128,512]{1,0:T(8,128)(2,1)S(1)}, bf16[128,512]{1,0:T(8,128)(2,1)S(1)}, u32[]{:S(2)}, u32[]{:S(2)}) collective-permute-start(bf16[128,512]{1,0:T(8,128)(2,1)S(1)} %get-tuple-element.54), channel_id=1, source_target_pairs={{0,8},{8,16},{16,24},{24,0},{1,9},{9,17},{17,25},{25,1},{2,10},{10... | collective-permute-start | bytes 393224 | tf_op jit(solution)/shard_map/ppermute | solution.py:301
  5.1 1.4 collective-permute-start.1
  5.7 0.7 collective-permute-start.2
  7.8 6.7 %collective-permute-start.5 = (bf16[256,512]{1,0:T(8,128)(2,1)S(1)}, bf16[256,512]{1,0:T(8,128)(2,1)S(1)}, u32[]{:S(2)}, u32[]{:S(2)}) collective-permute-start(bf16[256,512]{1,0:T(8,128)(2,1)S(1)} %get-tuple-element.57.refs_0_.refs_4_), channel_id=1, source_target_pairs={{0,3},{1,2},{2,1},{3,0},{8,11},{9,10},{10,9},{11,8},{16,19},{17,18... | collective-permute-start | bytes 786440 | tf_op jit(solution)/shard_map/ppermute | solution.py:289
  8.5 6.7 %collective-permute-start.4 = (bf16[256,512]{1,0:T(8,128)(2,1)S(1)}, bf16[256,512]{1,0:T(8,128)(2,1)S(1)}, u32[]{:S(2)}, u32[]{:S(2)}) collective-permute-start(bf16[256,512]{1,0:T(8,128)(2,1)S(1)} %get-tuple-element.57.refs_0_.refs_4_), channel_id=1, source_target_pairs={{0,2},{1,3},{2,0},{3,1},{8,10},{9,11},{10,8},{11,9},{16,18},{17,19... | collective-permute-start | bytes 786440 | tf_op jit(solution)/shard_map/ppermute | solution.py:289
  9.2 6.1 %collective-permute-start.3 = (bf16[256,512]{1,0:T(8,128)(2,1)S(1)}, bf16[256,512]{1,0:T(8,128)(2,1)S(1)}, u32[]{:S(2)}, u32[]{:S(2)}) collective-permute-start(bf16[256,512]{1,0:T(8,128)(2,1)S(1)} %get-tuple-element.57.refs_0_.refs_4_), channel_id=1, source_target_pairs={{0,1},{1,0},{2,3},{3,2},{8,9},{9,8},{10,11},{11,10},{16,17},{17,16... | collective-permute-start | bytes 786440 | tf_op jit(solution)/shard_map/ppermute | solution.py:289
  13.2 10.8 %collective-permute-start.21 = (bf16[256,512]{1,0:T(8,128)(2,1)S(1)}, bf16[256,512]{1,0:T(8,128)(2,1)S(1)}, u32[]{:S(2)}, u32[]{:S(2)}) collective-permute-start(bf16[256,512]{1,0:T(8,128)(2,1)S(1)} %get-tuple-element.71.refs_0_.refs_4_), channel_id=1, source_target_pairs={{0,3},{1,2},{2,1},{3,0},{8,11},{9,10},{10,9},{11,8},{16,19},{17,18... | collective-permute-start | bytes 786440 | tf_op jit(solution)/shard_map/ppermute | solution.py:289
  13.8 10.8 %collective-permute-start.20 = (bf16[256,512]{1,0:T(8,128)(2,1)S(1)}, bf16[256,512]{1,0:T(8,128)(2,1)S(1)}, u32[]{:S(2)}, u32[]{:S(2)}) collective-permute-start(bf16[256,512]{1,0:T(8,128)(2,1)S(1)} %get-tuple-element.71.refs_0_.refs_4_), channel_id=1, source_target_pairs={{0,2},{1,3},{2,0},{3,1},{8,10},{9,11},{10,8},{11,9},{16,18},{17,19... | collective-permute-start | bytes 786440 | tf_op jit(solution)/shard_map/ppermute | solution.py:289
  14.5 10.1 %collective-permute-start.19 = (bf16[256,512]{1,0:T(8,128)(2,1)S(1)}, bf16[256,512]{1,0:T(8,128)(2,1)S(1)}, u32[]{:S(2)}, u32[]{:S(2)}) collective-permute-start(bf16[256,512]{1,0:T(8,128)(2,1)S(1)} %get-tuple-element.71.refs_0_.refs_4_), channel_id=1, source_target_pairs={{0,1},{1,0},{2,3},{3,2},{8,9},{9,8},{10,11},{11,10},{16,17},{17,16... | collective-permute-start | bytes 786440 | tf_op jit(solution)/shard_map/ppermute | solution.py:289
  22.5 11.7 %collective-permute-start.6 = (bf16[272,512]{1,0:T(8,128)(2,1)S(1)}, bf16[272,512]{1,0:T(8,128)(2,1)S(1)}, u32[]{:S(2)}, u32[]{:S(2)}) collective-permute-start(bf16[272,512]{1,0:T(8,128)(2,1)S(1)} %get-tuple-element.60), channel_id=1, source_target_pairs={{0,1},{1,0},{2,3},{3,2},{8,9},{9,8},{10,11},{11,10},{16,17},{17,16... | collective-permute-start | bytes 835592 | tf_op jit(solution)/shard_map/ppermute | solution.py:289
  23.2 11.7 %collective-permute-start.7 = (bf16[272,512]{1,0:T(8,128)(2,1)S(1)}, bf16[272,512]{1,0:T(8,128)(2,1)S(1)}, u32[]{:S(2)}, u32[]{:S(2)}) collective-permute-start(bf16[272,512]{1,0:T(8,128)(2,1)S(1)} %get-tuple-element.61), channel_id=1, source_target_pairs={{0,2},{1,3},{2,0},{3,1},{8,10},{9,11},{10,8},{11,9},{16,18},{17,19... | collective-permute-start | bytes 835592 | tf_op jit(solution)/shard_map/ppermute | solution.py:289
  23.9 11.0 %collective-permute-start.8 = (bf16[272,512]{1,0:T(8,128)(2,1)S(1)}, bf16[272,512]{1,0:T(8,128)(2,1)S(1)}, u32[]{:S(2)}, u32[]{:S(2)}) collective-permute-start(bf16[272,512]{1,0:T(8,128)(2,1)S(1)} %get-tuple-element.62), channel_id=1, source_target_pairs={{0,3},{1,2},{2,1},{3,0},{8,11},{9,10},{10,9},{11,8},{16,19},{17,18... | collective-permute-start | bytes 835592 | tf_op jit(solution)/shard_map/ppermute | solution.py:289
  32.9 5.1 %collective-permute-start.22 = (bf16[272,512]{1,0:T(8,128)(2,1)S(1)}, bf16[272,512]{1,0:T(8,128)(2,1)S(1)}, u32[]{:S(2)}, u32[]{:S(2)}) collective-permute-start(bf16[272,512]{1,0:T(8,128)(2,1)S(1)} %get-tuple-element.77), channel_id=1, source_target_pairs={{0,1},{1,0},{2,3},{3,2},{8,9},{9,8},{10,11},{11,10},{16,17},{17,16... | collective-permute-start | bytes 835592 | tf_op jit(solution)/shard_map/ppermute | solution.py:289
  33.6 5.8 %collective-permute-start.23 = (bf16[272,512]{1,0:T(8,128)(2,1)S(1)}, bf16[272,512]{1,0:T(8,128)(2,1)S(1)}, u32[]{:S(2)}, u32[]{:S(2)}) collective-permute-start(bf16[272,512]{1,0:T(8,128)(2,1)S(1)} %get-tuple-element.78), channel_id=1, source_target_pairs={{0,2},{1,3},{2,0},{3,1},{8,10},{9,11},{10,8},{11,9},{16,18},{17,19... | collective-permute-start | bytes 835592 | tf_op jit(solution)/shard_map/ppermute | solution.py:289
  34.3 6.4 %collective-permute-start.24 = (bf16[272,512]{1,0:T(8,128)(2,1)S(1)}, bf16[272,512]{1,0:T(8,128)(2,1)S(1)}, u32[]{:S(2)}, u32[]{:S(2)}) collective-permute-start(bf16[272,512]{1,0:T(8,128)(2,1)S(1)} %get-tuple-element.79), channel_id=1, source_target_pairs={{0,3},{1,2},{2,1},{3,0},{8,11},{9,10},{10,9},{11,8},{16,19},{17,18... | collective-permute-start | bytes 835592 | tf_op jit(solution)/shard_map/ppermute | solution.py:289
  35.4 71.8 %copy-start.6 = (bf16[256,512]{1,0:T(8,128)(2,1)}, bf16[256,512]{1,0:T(8,128)(2,1)S(1)}, u32[]{:S(2)}) copy-start(bf16[256,512]{1,0:T(8,128)(2,1)S(1)} %get-tuple-element.64) | copy-start | bytes 786436
  35.4 49.4 %collective-permute-start.12 = (bf16[256,512]{1,0:T(8,128)(2,1)S(1)}, bf16[256,512]{1,0:T(8,128)(2,1)S(1)}, u32[]{:S(2)}, u32[]{:S(2)}) collective-permute-start(bf16[256,512]{1,0:T(8,128)(2,1)S(1)} %get-tuple-element.64), channel_id=1, source_target_pairs={{0,7},{1,6},{2,5},{3,4},{8,15},{9,14},{10,13},{11,12},{16,23},{17,... | collective-permute-start | bytes 786440 | tf_op jit(solution)/shard_map/ppermute | solution.py:313
  36.7 50.8 %collective-permute-start.11 = (bf16[256,512]{1,0:T(8,128)(2,1)S(1)}, bf16[256,512]{1,0:T(8,128)(2,1)S(1)}, u32[]{:S(2)}, u32[]{:S(2)}) collective-permute-start(bf16[256,512]{1,0:T(8,128)(2,1)S(1)} %get-tuple-element.64), channel_id=1, source_target_pairs={{0,6},{1,7},{2,4},{3,5},{8,14},{9,15},{10,12},{11,13},{16,22},{17,... | collective-permute-start | bytes 786440 | tf_op jit(solution)/shard_map/ppermute | solution.py:313
  38.0 50.8 %collective-permute-start.10 = (bf16[256,512]{1,0:T(8,128)(2,1)S(1)}, bf16[256,512]{1,0:T(8,128)(2,1)S(1)}, u32[]{:S(2)}, u32[]{:S(2)}) collective-permute-start(bf16[256,512]{1,0:T(8,128)(2,1)S(1)} %get-tuple-element.64), channel_id=1, source_target_pairs={{0,5},{1,4},{2,7},{3,6},{8,13},{9,12},{10,15},{11,14},{16,21},{17,... | collective-permute-start | bytes 786440 | tf_op jit(solution)/shard_map/ppermute | solution.py:313
  39.4 50.8 %collective-permute-start.9 = (bf16[256,512]{1,0:T(8,128)(2,1)S(1)}, bf16[256,512]{1,0:T(8,128)(2,1)S(1)}, u32[]{:S(2)}, u32[]{:S(2)}) collective-permute-start(bf16[256,512]{1,0:T(8,128)(2,1)S(1)} %get-tuple-element.64), channel_id=1, source_target_pairs={{0,4},{1,5},{2,6},{3,7},{8,12},{9,13},{10,14},{11,15},{16,20},{17,... | collective-permute-start | bytes 786440 | tf_op jit(solution)/shard_map/ppermute | solution.py:313
  41.1 68.2 %copy-start.7 = (bf16[256,512]{1,0:T(8,128)(2,1)}, bf16[256,512]{1,0:T(8,128)(2,1)S(1)}, u32[]{:S(2)}) copy-start(bf16[256,512]{1,0:T(8,128)(2,1)S(1)} %get-tuple-element.81) | copy-start | bytes 786436
  41.1 66.1 %copy-start.12 = (bf16[1,512,2048]{2,1,0:T(8,128)(2,1)S(1)}, bf16[1,512,2048]{2,1,0:T(8,128)(2,1)}, u32[]{:S(2)}) copy-start(bf16[1,512,2048]{2,1,0:T(8,128)(2,1)} %param.17) | copy-start | bytes 6291460
  41.1 59.9 %collective-permute-start.28 = (bf16[256,512]{1,0:T(8,128)(2,1)S(1)}, bf16[256,512]{1,0:T(8,128)(2,1)S(1)}, u32[]{:S(2)}, u32[]{:S(2)}) collective-permute-start(bf16[256,512]{1,0:T(8,128)(2,1)S(1)} %get-tuple-element.81), channel_id=1, source_target_pairs={{0,7},{1,6},{2,5},{3,4},{8,15},{9,14},{10,13},{11,12},{16,23},{17,... | collective-permute-start | bytes 786440 | tf_op jit(solution)/shard_map/ppermute | solution.py:313
  84.9 19.3 %collective-permute-start.27 = (bf16[256,512]{1,0:T(8,128)(2,1)S(1)}, bf16[256,512]{1,0:T(8,128)(2,1)S(1)}, u32[]{:S(2)}, u32[]{:S(2)}) collective-permute-start(bf16[256,512]{1,0:T(8,128)(2,1)S(1)} %get-tuple-element.81), channel_id=1, source_target_pairs={{0,6},{1,7},{2,4},{3,5},{8,14},{9,15},{10,12},{11,13},{16,22},{17,... | collective-permute-start | bytes 786440 | tf_op jit(solution)/shard_map/ppermute | solution.py:313
  87.6 23.4 %collective-permute-start.26 = (bf16[256,512]{1,0:T(8,128)(2,1)S(1)}, bf16[256,512]{1,0:T(8,128)(2,1)S(1)}, u32[]{:S(2)}, u32[]{:S(2)}) collective-permute-start(bf16[256,512]{1,0:T(8,128)(2,1)S(1)} %get-tuple-element.81), channel_id=1, source_target_pairs={{0,5},{1,4},{2,7},{3,6},{8,13},{9,12},{10,15},{11,14},{16,21},{17,... | collective-permute-start | bytes 786440 | tf_op jit(solution)/shard_map/ppermute | solution.py:313
  88.9 23.6 %collective-permute-start.25 = (bf16[256,512]{1,0:T(8,128)(2,1)S(1)}, bf16[256,512]{1,0:T(8,128)(2,1)S(1)}, u32[]{:S(2)}, u32[]{:S(2)}) collective-permute-start(bf16[256,512]{1,0:T(8,128)(2,1)S(1)} %get-tuple-element.81), channel_id=1, source_target_pairs={{0,4},{1,5},{2,6},{3,7},{8,12},{9,13},{10,14},{11,15},{16,20},{17,... | collective-permute-start | bytes 786440 | tf_op jit(solution)/shard_map/ppermute | solution.py:313
  98.8 24.9 %collective-permute-start.13 = (bf16[272,512]{1,0:T(8,128)(2,1)S(1)}, bf16[272,512]{1,0:T(8,128)(2,1)S(1)}, u32[]{:S(2)}, u32[]{:S(2)}) collective-permute-start(bf16[272,512]{1,0:T(8,128)(2,1)S(1)} %get-tuple-element.66), channel_id=1, source_target_pairs={{4,5},{5,4},{6,7},{7,6},{12,13},{13,12},{14,15},{15,14},{20,21},{2... | collective-permute-start | bytes 835592 | tf_op jit(solution)/shard_map/ppermute | solution.py:289
  101.0 25.9 %collective-permute-start.14 = (bf16[272,512]{1,0:T(8,128)(2,1)S(1)}, bf16[272,512]{1,0:T(8,128)(2,1)S(1)}, u32[]{:S(2)}, u32[]{:S(2)}) collective-permute-start(bf16[272,512]{1,0:T(8,128)(2,1)S(1)} %get-tuple-element.67), channel_id=1, source_target_pairs={{4,6},{5,7},{6,4},{7,5},{12,14},{13,15},{14,12},{15,13},{20,22},{2... | collective-permute-start | bytes 835592 | tf_op jit(solution)/shard_map/ppermute | solution.py:289
  104.2 26.0 %collective-permute-start.15 = (bf16[272,512]{1,0:T(8,128)(2,1)}, bf16[272,512]{1,0:T(8,128)(2,1)S(1)}, u32[]{:S(2)}, u32[]{:S(2)}) collective-permute-start(bf16[272,512]{1,0:T(8,128)(2,1)} %get-tuple-element.68), channel_id=1, source_target_pairs={{4,7},{5,6},{6,5},{7,4},{12,15},{13,14},{14,13},{15,12},{20,23},{2... | collective-permute-start | bytes 835592 | tf_op jit(solution)/shard_map/ppermute | solution.py:289
  111.0 37.0 %collective-permute-start.35 = (bf16[512,512]{1,0:T(8,128)(2,1)}, bf16[512,512]{1,0:T(8,128)(2,1)}, u32[]{:S(2)}, u32[]{:S(2)}) collective-permute-start(bf16[512,512]{1,0:T(8,128)(2,1)} %get-tuple-element.95), channel_id=1, source_target_pairs={{0,8},{8,16},{16,24},{24,0},{1,9},{9,17},{17,25},{25,1},{2,10},{10... | collective-permute-start | bytes 1572872 | tf_op jit(solution)/shard_map/ppermute | solution.py:301
  121.5 11.4 %collective-permute-start.29 = (bf16[272,512]{1,0:T(8,128)(2,1)}, bf16[272,512]{1,0:T(8,128)(2,1)S(1)}, u32[]{:S(2)}, u32[]{:S(2)}) collective-permute-start(bf16[272,512]{1,0:T(8,128)(2,1)} %get-tuple-element.87), channel_id=1, source_target_pairs={{4,5},{5,4},{6,7},{7,6},{12,13},{13,12},{14,15},{15,14},{20,21},{2... | collective-permute-start | bytes 835592 | tf_op jit(solution)/shard_map/ppermute | solution.py:289
  123.7 20.9 %collective-permute-start.30 = (bf16[272,512]{1,0:T(8,128)(2,1)}, bf16[272,512]{1,0:T(8,128)(2,1)S(1)}, u32[]{:S(2)}, u32[]{:S(2)}) collective-permute-start(bf16[272,512]{1,0:T(8,128)(2,1)} %get-tuple-element.88), channel_id=1, source_target_pairs={{4,6},{5,7},{6,4},{7,5},{12,14},{13,15},{14,12},{15,13},{20,22},{2... | collective-permute-start | bytes 835592 | tf_op jit(solution)/shard_map/ppermute | solution.py:289
  126.9 19.3 %collective-permute-start.31 = (bf16[272,512]{1,0:T(8,128)(2,1)}, bf16[272,512]{1,0:T(8,128)(2,1)S(1)}, u32[]{:S(2)}, u32[]{:S(2)}) collective-permute-start(bf16[272,512]{1,0:T(8,128)(2,1)} %get-tuple-element.89), channel_id=1, source_target_pairs={{4,7},{5,6},{6,5},{7,4},{12,15},{13,14},{14,13},{15,12},{20,23},{2... | collective-permute-start | bytes 835592 | tf_op jit(solution)/shard_map/ppermute | solution.py:289
  131.1 15.1 %copy-start.5 = (bf16[256,512]{1,0:T(8,128)(2,1)S(1)}, bf16[256,512]{1,0:T(8,128)(2,1)}, u32[]{:S(2)}) copy-start(bf16[256,512]{1,0:T(8,128)(2,1)} %copy-done.4) | copy-start | bytes 786436
  131.1 18.3 %copy-start.13 = (bf16[1,512,2048]{2,1,0:T(8,128)(2,1)S(1)}, bf16[1,512,2048]{2,1,0:T(8,128)(2,1)}, u32[]{:S(2)}) copy-start(bf16[1,512,2048]{2,1,0:T(8,128)(2,1)} %param.17) | copy-start | bytes 6291460
  131.6 16.6 %collective-permute-start.18 = (bf16[256,512]{1,0:T(8,128)(2,1)S(1)}, bf16[256,512]{1,0:T(8,128)(2,1)S(1)}, u32[]{:S(2)}, u32[]{:S(2)}) collective-permute-start(bf16[256,512]{1,0:T(8,128)(2,1)S(1)} %broadcast_select_fusion.1.refs_0_), channel_id=1, source_target_pairs={{0,3},{1,2},{2,1},{3,0},{4,7},{5,6},{6,5},{7,4},{8,11},{9,10},{10,... | collective-permute-start | bytes 786440 | tf_op jit(solution)/shard_map/ppermute | solution.py:289
  132.9 18.4 %collective-permute-start.17 = (bf16[256,512]{1,0:T(8,128)(2,1)S(1)}, bf16[256,512]{1,0:T(8,128)(2,1)S(1)}, u32[]{:S(2)}, u32[]{:S(2)}) collective-permute-start(bf16[256,512]{1,0:T(8,128)(2,1)S(1)} %broadcast_select_fusion.1.refs_0_), channel_id=1, source_target_pairs={{0,2},{1,3},{2,0},{3,1},{4,6},{5,7},{6,4},{7,5},{8,10},{9,11},{10,... | collective-permute-start | bytes 786440 | tf_op jit(solution)/shard_map/ppermute | solution.py:289
  144.6 7.4 %collective-permute-start.16 = (bf16[256,512]{1,0:T(8,128)(2,1)S(1)}, bf16[256,512]{1,0:T(8,128)(2,1)S(1)}, u32[]{:S(2)}, u32[]{:S(2)}) collective-permute-start(bf16[256,512]{1,0:T(8,128)(2,1)S(1)} %broadcast_select_fusion.1.refs_0_), channel_id=1, source_target_pairs={{0,1},{1,0},{2,3},{3,2},{4,5},{5,4},{6,7},{7,6},{8,9},{9,8},{10,11... | collective-permute-start | bytes 786440 | tf_op jit(solution)/shard_map/ppermute | solution.py:289
  146.7 7.6 %collective-permute-start.34 = (bf16[256,512]{1,0:T(8,128)(2,1)S(1)}, bf16[256,512]{1,0:T(8,128)(2,1)S(1)}, u32[]{:S(2)}, u32[]{:S(2)}) collective-permute-start(bf16[256,512]{1,0:T(8,128)(2,1)S(1)} %broadcast_select_fusion.refs_4_), channel_id=1, source_target_pairs={{0,3},{1,2},{2,1},{3,0},{4,7},{5,6},{6,5},{7,4},{8,11},{9,10},{10,... | collective-permute-start | bytes 786440 | tf_op jit(solution)/shard_map/ppermute | solution.py:289
  148.0 8.4 %collective-permute-start.33 = (bf16[256,512]{1,0:T(8,128)(2,1)S(1)}, bf16[256,512]{1,0:T(8,128)(2,1)S(1)}, u32[]{:S(2)}, u32[]{:S(2)}) collective-permute-start(bf16[256,512]{1,0:T(8,128)(2,1)S(1)} %broadcast_select_fusion.refs_4_), channel_id=1, source_target_pairs={{0,2},{1,3},{2,0},{3,1},{4,6},{5,7},{6,4},{7,5},{8,10},{9,11},{10,... | collective-permute-start | bytes 786440 | tf_op jit(solution)/shard_map/ppermute | solution.py:289
  148.2 10.1 %collective-permute-start.32 = (bf16[256,512]{1,0:T(8,128)(2,1)S(1)}, bf16[256,512]{1,0:T(8,128)(2,1)S(1)}, u32[]{:S(2)}, u32[]{:S(2)}) collective-permute-start(bf16[256,512]{1,0:T(8,128)(2,1)S(1)} %broadcast_select_fusion.refs_4_), channel_id=1, source_target_pairs={{0,1},{1,0},{2,3},{3,2},{4,5},{5,4},{6,7},{7,6},{8,9},{9,8},{10,11... | collective-permute-start | bytes 786440 | tf_op jit(solution)/shard_map/ppermute | solution.py:289
  151.3 12.2 %collective-permute-start.36 = (bf16[512,512]{1,0:T(8,128)(2,1)S(1)}, bf16[512,512]{1,0:T(8,128)(2,1)S(1)}, u32[]{:S(2)}, u32[]{:S(2)}) collective-permute-start(bf16[512,512]{1,0:T(8,128)(2,1)S(1)} %copy-done.17), channel_id=1, source_target_pairs={{0,16},{8,24},{16,0},{24,8},{1,17},{9,25},{17,1},{25,9},{2,18},{10... | collective-permute-start | bytes 1572872 | tf_op jit(solution)/shard_map/ppermute | solution.py:301
  152.0 11.5 %collective-permute-start.37 = (bf16[512,512]{1,0:T(8,128)(2,1)S(1)}, bf16[512,512]{1,0:T(8,128)(2,1)S(1)}, u32[]{:S(2)}, u32[]{:S(2)}) collective-permute-start(bf16[512,512]{1,0:T(8,128)(2,1)S(1)} %copy-done.15), channel_id=1, source_target_pairs={{0,24},{8,0},{16,8},{24,16},{1,25},{9,1},{17,9},{25,17},{2,26},{10... | collective-permute-start | bytes 1572872 | tf_op jit(solution)/shard_map/ppermute | solution.py:301
  154.3 17.4 %collective-permute-start.38 = (bf16[512,512]{1,0:T(8,128)(2,1)S(1)}, bf16[512,512]{1,0:T(8,128)(2,1)S(1)}, u32[]{:S(2)}, u32[]{:S(2)}) collective-permute-start(bf16[512,512]{1,0:T(8,128)(2,1)S(1)} %get-tuple-element.101), channel_id=1, source_target_pairs={{4,12},{12,20},{20,28},{28,4},{5,13},{13,21},{21,29},{29,5},{6,14}... | collective-permute-start | bytes 1572872 | tf_op jit(solution)/shard_map/ppermute | solution.py:301
  156.4 32.3 %collective-permute-start.39 = (bf16[512,512]{1,0:T(8,128)(2,1)S(1)}, bf16[512,512]{1,0:T(8,128)(2,1)S(1)}, u32[]{:S(2)}, u32[]{:S(2)}) collective-permute-start(bf16[512,512]{1,0:T(8,128)(2,1)S(1)} %get-tuple-element.102), channel_id=1, source_target_pairs={{4,20},{12,28},{20,4},{28,12},{5,21},{13,29},{21,5},{29,13},{6,22}... | collective-permute-start | bytes 1572872 | tf_op jit(solution)/shard_map/ppermute | solution.py:301
  158.4 30.3 %collective-permute-start.40 = (bf16[512,512]{1,0:T(8,128)(2,1)S(1)}, bf16[512,512]{1,0:T(8,128)(2,1)S(1)}, u32[]{:S(2)}, u32[]{:S(2)}) collective-permute-start(bf16[512,512]{1,0:T(8,128)(2,1)S(1)} %get-tuple-element.103), channel_id=1, source_target_pairs={{4,28},{12,4},{20,12},{28,20},{5,29},{13,5},{21,13},{29,21},{6,30}... | collective-permute-start | bytes 1572872 | tf_op jit(solution)/shard_map/ppermute | solution.py:301
  (11 other events, 28.5 us)

commit v2 on v1

v2 whole, which is shorter than its diff:
```python
import functools

import jax
import jax.numpy as jnp
from jax import lax
from jax.experimental import pallas as pl
from jax.experimental.pallas import tpu as pltpu
from jax.sharding import PartitionSpec as P

HEADDIM = 64
NSTATE = 128
TILE = 128
EXTRA = 16
EPS = 1e-05
LOG2E = 1.4426950408889634
F32 = jnp.float32
BF16 = jnp.bfloat16
VMEM_LIMIT = 48 * 1024 * 1024

NN = (((1,), (0,)), ((), ()))
NT = (((1,), (1,)), ((), ()))
TN = (((0,), (0,)), ((), ()))


def mm(a, b, dims=NN):
    return lax.dot_general(a, b, dims, preferred_element_type=F32)


def split3(value):
    high = value.astype(BF16)
    rest = value - high.astype(F32)
    mid = rest.astype(BF16)
    low = (rest - mid.astype(F32)).astype(BF16)
    return high, mid, low


def silu(x):
    return x * (1.0 / (1.0 + jnp.exp(-x)))


def iota(shape, axis):
    return lax.broadcasted_iota(jnp.int32, shape, axis)


def vmem():
    return pl.BlockSpec(memory_space=pltpu.VMEM)


def smem():
    return pl.BlockSpec(memory_space=pltpu.SMEM)


def params():
    return pltpu.CompilerParams(vmem_limit_bytes=VMEM_LIMIT)


def cost(flops, moved):
    return pl.CostEstimate(flops=int(flops), bytes_accessed=int(moved), transcendentals=0)


def walk_baselines(rows_ref, owner_ref, count_ref, dp_count, visit):
    for owner in range(dp_count):
        count_ref[owner] = 0

    def step(b, start):
        owner = owner_ref[b]
        length = rows_ref[b]
        owner_start = count_ref[owner]
        visit(b, owner, length, start, owner_start)
        count_ref[owner] = owner_start + length
        return start + length

    lax.fori_loop(0, rows_ref.shape[0], step, jnp.int32(0))


def select_kernel(dp_count, cap, pos_ref, rows_ref, owner_ref, tokens_ref, *refs):
    outs, (slot_ref, count_ref) = refs[:dp_count], refs[dp_count:]
    me, part = pos_ref[0], pos_ref[1]
    tok_rows = tokens_ref.shape[0]
    width = outs[0].shape[1]
    local = iota((8, tok_rows), 1)
    slot_ref[...] = jnp.full((8, tok_rows), -1, jnp.int32)

    def visit(b, owner, length, start, owner_start):
        inside = (local >= start) & (local < start + length)
        slot_ref[...] = jnp.where(inside, local + (owner * cap + owner_start - start), slot_ref[...])

    walk_baselines(rows_ref, owner_ref, count_ref, dp_count, visit)
    columns = tokens_ref[:, pl.ds(pl.multiple_of(part * width, width), width)]
    slots = slot_ref[0:1, :]
    for k in range(dp_count):
        owner = me ^ k
        chosen = (iota((cap, tok_rows), 0) + owner * cap) == slots
        outs[k][...] = mm(chosen.astype(F32).astype(BF16), columns).astype(BF16)


def place_kernel(dp_count, cap, pos_ref, rows_ref, owner_ref, *refs):
    arrived = refs[:dp_count]
    out_ref, seg_ref, slot_ref, count_ref, packed_ref = refs[dp_count:]
    me = pos_ref[0]
    own_slots = seg_ref.shape[0]
    arrival = iota((8, own_slots), 1)
    turn = arrival // cap
    place = arrival - turn * cap
    sender = me ^ turn
    slot_ref[...] = jnp.full((8, own_slots), -1, jnp.int32)
    position = iota((own_slots, TILE), 0)
    seg_ref[...] = jnp.zeros((own_slots, TILE), jnp.int32)

    def visit(b, owner, length, start, owner_start):
        @pl.when(owner == me)
        def _():
            inside = (place >= owner_start) & (place < owner_start + length)
            slot = dp_count * owner_start + sender * length + place - owner_start
            slot_ref[...] = jnp.where(inside, slot, slot_ref[...])
            seg_ref[...] = jnp.where(
                position >= dp_count * owner_start, dp_count * owner_start, seg_ref[...]
            )

    walk_baselines(rows_ref, owner_ref, count_ref, dp_count, visit)
    filled = dp_count * count_ref[me]
    seg_ref[...] = jnp.where(position >= filled, filled, seg_ref[...])
    for k in range(dp_count):
        packed_ref[k * cap : (k + 1) * cap, :] = arrived[k][...]
    chosen = iota((own_slots, own_slots), 0) == slot_ref[0:1, :]
    out_ref[...] = mm(chosen.astype(F32).astype(BF16), packed_ref[...]).astype(BF16)


def layer_kernel(active, counts, band, pos_ref, *refs):
    @pl.when(pos_ref[2] == active)
    def _():
        layer_body(counts, band, pos_ref, *refs)


def layer_body(counts, band, pos_ref, *refs):
    blocks = []
    for count in counts:
        blocks.append(refs[:count])
        refs = refs[count:]
    tensor = len(counts)
    (seg_ref, gain_ref, win_ref, wgate_ref, wstate_ref, wstep_ref, bias_ref, decay_ref) = refs[:8]
    (skip_ref, ngain_ref, wout_ref) = refs[8:11]
    outs, refs = refs[11 : 11 + tensor], refs[11 + tensor :]
    normed_ref, xs_ref, z_ref, b_ref, c_ref, a_ref, cumt_ref, xlow_ref, xhigh_ref, y_ref = refs[:10]
    held, sem = refs[10:15], refs[15]
    loads = [
        pltpu.make_async_copy(source, target, sem.at[index])
        for index, (source, target) in enumerate(
            zip((wstate_ref, wstep_ref, win_ref, wgate_ref, wout_ref), held)
        )
    ]
    for load in loads:
        load.start()
    wstate_ref, wstep_ref, win_ref, wgate_ref, wout_ref = held
    part = pos_ref[1]
    rows, width = seg_ref.shape[0], blocks[0][0].shape[1]
    inner = win_ref.shape[1]
    depth = width * tensor
    piece_rows = min(block.shape[0] for pieces in blocks for block in pieces)
    for at in range(0, rows, piece_rows):
        chunks = []
        for pieces in blocks:
            height = pieces[0].shape[0]
            start = at % height
            chunks.append(pieces[at // height][start : start + piece_rows, :].astype(F32))
        square = sum(jnp.sum(chunk * chunk, axis=1, keepdims=True) for chunk in chunks)
        scale = lax.rsqrt(square * (1.0 / depth) + EPS)
        for k, chunk in enumerate(chunks):
            columns = pl.ds(pl.multiple_of((part ^ k) * width, width), width)
            normed_ref[at : at + piece_rows, columns] = (
                chunk * scale * gain_ref[:, columns]
            ).astype(BF16)
    normed = normed_ref[...]
    loads[0].wait()
    state_io = silu(mm(normed, wstate_ref[...])).astype(BF16)
    b_ref[...] = state_io[:, :NSTATE]
    c_ref[...] = state_io[:, NSTATE:]
    loads[1].wait()
    pre = mm(normed, wstep_ref[...]) + bias_ref[...]
    step = jnp.maximum(pre, 0.0) + jnp.log1p(jnp.exp(-jnp.abs(pre)))
    heads = inner // HEADDIM
    loads[2].wait()
    xs = silu(mm(normed, win_ref[...])).astype(BF16)
    xs_ref[...] = xs
    spread = (iota((TILE, inner), 1) // HEADDIM == iota((TILE, inner), 0)).astype(F32).astype(BF16)
    step_wide = sum(mm(piece, spread) for piece in split3(step))
    scaled = step_wide * xs.astype(F32)
    low_half = iota(scaled.shape, 1) % TILE < HEADDIM
    xlow_ref[...] = jnp.where(low_half, scaled, 0.0).astype(BF16)
    xhigh_ref[...] = jnp.where(low_half, 0.0, scaled).astype(BF16)
    loads[3].wait()
    z_ref[...] = mm(normed, wgate_ref[...])
    a_ref[...] = step * (jnp.exp(decay_ref[...]) * (-LOG2E))

    lane = iota((TILE, TILE), 1)
    for q in range(rows // TILE):
        here = slice(q * TILE, (q + 1) * TILE)
        keys = [slice(k * TILE, (k + 1) * TILE) for k in range(max(0, q - band), q + 1)]
        seg = seg_ref[here, :]
        row_at = iota((TILE, TILE), 0) + q * TILE
        c_rows = c_ref[here, :]
        scores = []
        cum = jnp.zeros((TILE, TILE), F32)
        for key in keys:
            at = lane + key.start
            valid = (at >= seg) & (at <= row_at)
            scores.append(jnp.where(valid, mm(c_rows, b_ref[key, :], NT), 0.0))
            ones = jnp.where(valid, 1.0, 0.0).astype(BF16)
            for piece in split3(a_ref[key, :]):
                cum = cum + mm(ones, piece)
        cumt_ref[here, :] = cum.T
        for pair in range(heads // 2):
            total = jnp.zeros((TILE, TILE), F32)
            columns = slice(pair * TILE, (pair + 1) * TILE)
            own = [
                jnp.broadcast_to(cum[:, h : h + 1], (TILE, TILE)) for h in (2 * pair, 2 * pair + 1)
            ]
            for key, score in zip(keys, scores):
                weights = [
                    (
                        jnp.exp2(jnp.minimum(own[half] - cumt_ref[key, :][h : h + 1, :], 0.0)) * score
                    ).astype(BF16)
                    for half, h in enumerate((2 * pair, 2 * pair + 1))
                ]
                values = jnp.concatenate([xlow_ref[key, columns], xhigh_ref[key, columns]], axis=0)
                total = total + mm(jnp.concatenate(weights, axis=1), values)
            y_ref[here, columns] = total

    gated = (y_ref[...] + skip_ref[...] * xs_ref[...].astype(F32)) * silu(z_ref[...])
    sq = gated * gated
    sq_high = sq.astype(BF16)
    sq_low = (sq - sq_high.astype(F32)).astype(BF16)
    ones = jnp.ones((EXTRA, inner), BF16)
    sums = mm(ones, sq_high, NT) + mm(ones, sq_low, NT)
    high, mid, low = split3(sums)
    row = iota(sums.shape, 0)
    zero = jnp.zeros(sums.shape, F32)
    message = jnp.where(
        row == 0,
        high.astype(F32),
        jnp.where(row == 1, mid.astype(F32), jnp.where(row == 2, low.astype(F32), zero)),
    ).astype(BF16)
    gn = (gated * ngain_ref[...]).astype(BF16)
    loads[4].wait()
    for k, out in enumerate(outs):
        columns = pl.ds(pl.multiple_of((part ^ k) * width, width), width)
        out[0:rows, :] = mm(gn, wout_ref[:, columns]).astype(BF16)
        out[rows : rows + EXTRA, :] = jnp.zeros((EXTRA, width), BF16)
        out[rows : rows + EXTRA, 0:rows] = message
    tail = rows + EXTRA
    outs[0][tail : tail + rows, :] = gn
    at = tail + rows
    for piece in blocks[0]:
        outs[0][at : at + piece.shape[0], :] = piece[...]
        at += piece.shape[0]


def sum_kernel(tensor, inner_all, rows, *refs):
    parts, (out_ref, y_ref) = refs[:tensor], refs[tensor:]
    width = parts[0].shape[1]
    tail = rows + EXTRA
    ones = jnp.ones((EXTRA, TILE), BF16)
    square = sum(mm(part[rows:tail, 0:rows], ones, TN) for part in parts)
    scale = lax.rsqrt(square * (1.0 / inner_all) + EPS)
    for c in range(0, width, TILE):
        columns = slice(c, c + TILE)
        total = sum(part[0:rows, columns].astype(F32) for part in parts)
        residual = parts[0][tail + rows : tail + 2 * rows, columns].astype(F32)
        out_ref[:, columns] = (residual + total * scale).astype(BF16)
        y_ref[:, columns] = (parts[0][tail : tail + rows, columns].astype(F32) * scale).astype(BF16)


def half_kernel(pos_ref, own_ref, other_ref, out_ref):
    rows = out_ref.shape[0]

    @pl.when(pos_ref[2] == 0)
    def _():
        out_ref[...] = other_ref[rows : 2 * rows, :]

    @pl.when(pos_ref[2] != 0)
    def _():
        out_ref[...] = own_ref[0:rows, :]


def grad_kernel(active, pieces, pos_ref, *refs):
    ys, cot_ref, outs = refs[: -1 - pieces], refs[-1 - pieces], refs[-pieces:]
    width = outs[0].shape[1]

    @pl.when(pos_ref[2] == active)
    def _():
        for k, out in enumerate(outs):
            if pieces == 1:
                columns = slice(0, width)
            else:
                columns = pl.ds(pl.multiple_of((pos_ref[0] ^ k) * width, width), width)
            total, at = 0.0, 0
            for y in ys:
                rows = y.shape[0]
                total = total + mm(y[...], cot_ref[at : at + rows, columns], TN)
                at += rows
            out[...] = total.astype(BF16)


def total_kernel(encoder_count, pos_ref, *refs):
    encoder, decoder, out_ref = refs[:encoder_count], refs[encoder_count:-1], refs[-1]

    def add(terms):
        rows = terms[0].shape[0]
        for at in range(0, rows, TILE):
            total = sum(term[at : at + TILE, :].astype(F32) for term in terms)
            out_ref[0, at : at + TILE, :] = total.astype(BF16)

    @pl.when(pos_ref[2] == 0)
    def _():
        add(encoder)

    @pl.when(pos_ref[2] != 0)
    def _():
        add(decoder)


def assemble_kernel(counts, pos_ref, *refs):
    groups = []
    for count in counts:
        groups.append(refs[:count])
        refs = refs[count:]
    out_ref, sem = refs
    part = pos_ref[1]
    tensor = len(counts) // 2

    def move(blocks):
        copies = []
        for k, pieces in enumerate(blocks):
            at = 0
            for piece in pieces:
                rows, width = piece.shape
                columns = pl.ds(pl.multiple_of((part ^ k) * width, width), width)
                copies.append(
                    pltpu.make_async_copy(
                        piece, out_ref.at[0, at : at + rows, columns], sem.at[len(copies)]
                    )
                )
                at += rows
        for copy in copies:
            copy.start()
        for copy in copies:
            copy.wait()

    @pl.when(pos_ref[2] == 0)
    def _():
        move(groups[:tensor])

    @pl.when(pos_ref[2] != 0)
    def _():
        move(groups[tensor:])


def tensor_gather(value):
    count = lax.axis_size("tensor")
    return [
        lax.ppermute(value, "tensor", [(t, t ^ k) for t in range(count)]) for k in range(1, count)
    ]


def tensor_cross(values, active):
    count = lax.axis_size("tensor")
    other = 1 - active
    return [
        lax.ppermute(
            value,
            ("section", "tensor"),
            [(active * count + t, other * count + (t ^ k)) for t in range(count)]
            + [(other * count + t, active * count + t) for t in range(count)],
        )
        for k, value in enumerate(values)
    ]


def dp_cross(values, active, first):
    count = lax.axis_size("dp")
    other = 1 - active
    return [
        lax.ppermute(
            value,
            ("dp", "section"),
            [(d * 2 + active, (d ^ k) * 2 + other) for d in range(count)]
            + [(d * 2 + other, d * 2 + active) for d in range(count)],
        )
        for k, value in enumerate(values, first)
    ]


def per_device(
    tokens,
    base_rows,
    baseline_owner,
    cotangent,
    pre_gain,
    input_proj,
    gate_proj,
    state_proj,
    step_proj,
    step_bias,
    decay_log,
    skip_gain,
    norm_gain,
    out_proj,
):
    dp_count = lax.axis_size("dp")
    tensor = lax.axis_size("tensor")
    tok_rows, feat = tokens.shape
    cap = 2 * tok_rows // dp_count
    own_slots = cap * dp_count
    width = feat // tensor
    inner = input_proj.shape[2]
    heads = step_proj.shape[2]
    longest = 3 * tok_rows // base_rows.shape[0] * dp_count
    band = (longest - 1 + TILE - 1) // TILE
    dp_at = lax.axis_index("dp")
    section = lax.axis_index("section")
    pos = jnp.stack([dp_at, lax.axis_index("tensor"), section]).astype(jnp.int32)
    shape = jax.ShapeDtypeStruct
    tables = (pos, base_rows, baseline_owner)

    outgoing = pl.pallas_call(
        functools.partial(select_kernel, dp_count, cap),
        out_shape=[shape((cap, width), BF16)] * dp_count,
        in_specs=[smem()] * 3 + [vmem()],
        out_specs=[vmem()] * dp_count,
        scratch_shapes=[pltpu.VMEM((8, tok_rows), jnp.int32), pltpu.SMEM((dp_count,), jnp.int32)],
        compiler_params=params(),
        name="select_rows",
    )(*tables, tokens)
    swap = [(0, 1), (1, 0)]
    barrier = lax.optimization_barrier
    cot_own = cotangent[0]
    cot_other = lax.ppermute(cot_own, "section", swap)
    arrived = [outgoing[0]] + dp_cross(outgoing[1:], 0, 1)
    arrived, cot_other = barrier((arrived, cot_other))
    own_block, seg = pl.pallas_call(
        functools.partial(place_kernel, dp_count, cap),
        out_shape=[shape((own_slots, width), BF16), shape((own_slots, TILE), jnp.int32)],
        in_specs=[smem()] * 3 + [vmem()] * dp_count,
        out_specs=[vmem()] * 2,
        scratch_shapes=[
            pltpu.VMEM((8, own_slots), jnp.int32),
            pltpu.SMEM((dp_count,), jnp.int32),
            pltpu.VMEM((own_slots, width), BF16),
        ],
        compiler_params=params(),
        name="place_rows",
    )(*tables, *arrived)

    def lanes(value):
        return jnp.pad(value, ((0, 0), (0, TILE - heads)))

    weights = (
        pre_gain,
        input_proj[0],
        gate_proj[0],
        state_proj[0],
        lanes(step_proj[0]),
        lanes(step_bias),
        lanes(decay_log),
        jnp.repeat(skip_gain, HEADDIM, axis=1),
        norm_gain,
        out_proj[0],
    )

    is_large = [index in (1, 2, 3, 4, 9) for index in range(len(weights))]
    part_rows = [3 * own_slots + EXTRA] + [own_slots + EXTRA] * (tensor - 1)

    def layer(active, blocks):
        counts = tuple(len(pieces) for pieces in blocks)
        return pl.pallas_call(
            functools.partial(layer_kernel, active, counts, band),
            out_shape=[shape((count, width), BF16) for count in part_rows],
            in_specs=[smem()]
            + [vmem()] * (sum(counts) + 1)
            + [pl.BlockSpec(memory_space=pl.ANY) if large else vmem() for large in is_large],
            out_specs=[vmem()] * tensor,
            scratch_shapes=[
                pltpu.VMEM((own_slots, feat), BF16),
                pltpu.VMEM((own_slots, inner), BF16),
                pltpu.VMEM((own_slots, inner), F32),
                pltpu.VMEM((own_slots, NSTATE), BF16),
                pltpu.VMEM((own_slots, NSTATE), BF16),
                pltpu.VMEM((own_slots, TILE), F32),
                pltpu.VMEM((own_slots, TILE), F32),
                pltpu.VMEM((own_slots, inner), BF16),
                pltpu.VMEM((own_slots, inner), BF16),
                pltpu.VMEM((own_slots, inner), F32),
            ]
            + [pltpu.VMEM(weights[index].shape, BF16) for index in (3, 4, 1, 2, 9)]
            + [pltpu.SemaphoreType.DMA((5,))],
            compiler_params=params(),
            cost_estimate=cost(2 * own_slots * feat * (3 * inner + 512), 12e6),
            name="layer_part",
        )(pos, *[piece for pieces in blocks for piece in pieces], seg, *weights)

    def finish(parts):
        return pl.pallas_call(
            functools.partial(sum_kernel, tensor, inner * tensor, own_slots),
            out_shape=[shape((own_slots, width), BF16), shape((own_slots, inner), BF16)],
            in_specs=[vmem()] * tensor,
            out_specs=[vmem()] * 2,
            compiler_params=params(),
            cost_estimate=cost(1e6, 3e6),
            name="sum_parts",
        )(*parts)

    def gradient_terms(active, ys, cot, pieces):
        return pl.pallas_call(
            functools.partial(grad_kernel, active, pieces),
            out_shape=[shape((inner, feat // pieces), BF16)] * pieces,
            in_specs=[smem()] + [vmem()] * (len(ys) + 1),
            out_specs=[vmem()] * pieces,
            compiler_params=params(),
            cost_estimate=cost(2 * own_slots * inner * feat, 5e6),
            name="gradient_terms",
        )(pos, *ys, cot)

    direct = feat // dp_count % TILE == 0
    pieces = dp_count if direct else 1
    half = own_slots // 2

    blocks = [[value] for value in tensor_cross([own_block] * tensor, 1)]
    latent, enc_y = finish(tensor_cross(layer(0, blocks), 0))

    passed = lax.ppermute(latent, "section", swap)
    mine = pl.pallas_call(
        half_kernel,
        out_shape=shape((half, width), BF16),
        in_specs=[smem()] + [vmem()] * 2,
        out_specs=vmem(),
        compiler_params=params(),
        cost_estimate=cost(1e5, 5e5),
        name="own_half",
    )(pos, latent, passed)
    gathered = tensor_gather(mine)
    enc_y, gathered[0] = barrier((enc_y, gathered[0]))
    enc_terms = gradient_terms(1, [enc_y], cot_other, pieces)
    enc_terms, gathered = barrier((enc_terms, gathered))
    swapped = [lax.ppermute(value, "section", swap) for value in gathered]
    sources = [[latent]] + [[top, bottom] for top, bottom in zip(gathered, swapped)]
    kept = [[passed]] + [[top, bottom] for top, bottom in zip(swapped, gathered)]

    enc_grad, order = [], list(range(dp_count))[::-1] if direct else []

    def send_gradient(count):
        for k in order[:count]:
            enc_grad.extend(dp_cross([enc_terms[k]], 1, k))
        del order[:count]

    sources, enc_terms = barrier((sources, enc_terms))
    send_gradient(1)
    parts = layer(1, sources)
    parts, enc_grad, enc_terms = barrier((parts, enc_grad, enc_terms))
    arrived = tensor_cross(parts, 1)
    send_gradient(1)
    arrived, enc_grad, enc_terms = barrier((arrived, enc_grad, enc_terms))
    send_gradient(dp_count)
    rebuilt, dec_y = finish(arrived)
    dec_terms = gradient_terms(0, [dec_y], cot_other, pieces)
    if direct:
        dec_grad = dp_cross(dec_terms, 0, 0)
    else:
        enc_grad, dec_grad = [
            [
                lax.ppermute(
                    lax.psum_scatter(terms[0], "dp", scatter_dimension=1, tiled=True), "section", swap
                )
            ]
            for terms in (enc_terms, dec_terms)
        ]
    rebuilt, dec_terms = barrier((rebuilt, dec_terms))
    finals = [[value] for value in tensor_cross([rebuilt] * tensor, 0)]

    groups = kept + finals
    counts = tuple(len(group) for group in groups)
    activations = pl.pallas_call(
        functools.partial(assemble_kernel, counts),
        out_shape=shape((1, own_slots, feat), BF16),
        in_specs=[smem()] + [pl.BlockSpec(memory_space=pl.ANY)] * sum(counts),
        out_specs=pl.BlockSpec(memory_space=pl.ANY),
        scratch_shapes=[pltpu.SemaphoreType.DMA((2 * tensor,))],
        compiler_params=params(),
        cost_estimate=cost(1e6, 4e6),
        name="assemble_rows",
    )(pos, *[piece for group in groups for piece in group])
    out_grad = pl.pallas_call(
        functools.partial(total_kernel, len(enc_grad)),
        out_shape=shape((1, inner, feat // dp_count), BF16),
        in_specs=[smem()] + [vmem()] * (len(enc_grad) + len(dec_grad)),
        out_specs=vmem(),
        compiler_params=params(),
        cost_estimate=cost(1e6, 4e6),
        name="gradient_total",
    )(pos, *enc_grad, *dec_grad)
    return activations, out_grad


def solution(mesh):
    return jax.shard_map(
        per_device,
        mesh=mesh,
        in_specs=(
            P("dp", None),
            P(),
            P(),
            P("section", "dp", None),
            P("section", None),
            P("section", None, "tensor"),
            P("section", None, "tensor"),
            P("section", None, None),
            P("section", None, "tensor"),
            P("section", "tensor"),
            P("section", "tensor"),
            P("section", "tensor"),
            P("section", "tensor"),
            P("section", "tensor", None),
        ),
        out_specs=(P("section", "dp", None), P("section", "tensor", "dp")),
        check_vma=False,
    )
```

time: 192 us -> 147 us (0.77)
  the two profiles are of different devices: /device:TPU:29 before, /device:TPU:9 now
where the time goes in v2:
time: 147 us; the launch traced here: 146 us
  waiting for transfers between devices  72.4 us (49%)
  starting transfers between devices  41.1 us (28%)
  Pallas kernels  26.5 us (18%)
  local copies, waits for them, and re-layouts  5.63 us (4%)
    ppermute x11, waiting for transfers between devices, dp_cross(): lax.ppermute(value, ('dp', 'section'), [(d * 2 + active, (d ^ k) * 2 + ot...  32 us
    ppermute x16, waiting for transfers between devices, tensor_cross(): lax.ppermute(value, ('section', 'tensor'), [(active * count + t, other *...  27.3 us
    ppermute x16, starting transfers between devices, tensor_cross(): lax.ppermute(value, ('section', 'tensor'), [(active * count + t, other *...  22.9 us
    pallas_call x2, Pallas kernels, layer(): pl.pallas_call(functools.partial(layer_kernel, active, counts, band), out...  15.1 us
    ppermute x11, starting transfers between devices, dp_cross(): lax.ppermute(value, ('dp', 'section'), [(d * 2 + active, (d ^ k) * 2 + ot...  12.9 us
    ppermute x3, waiting for transfers between devices, tensor_gather(): lax.ppermute(value, 'tensor', [(t, t ^ k) for t in range(count)])  9.71 us
    unnamed x19, local copies, waits for them, and re-layouts  4.32 us
  transfers between devices with their start and end apart: 35, of which 19 were waited for; matrix products, arithmetic and copies ran while one was open for 2% of the time, Pallas kernels for 12%

profile of v2, /device:TPU:9, one launch (start us, length us, event | category | flops | bytes accessed | tf_op | source)
XLA Modules:
  0.0 146.5 jit_solution(16590661712446288419)
XLA Ops:
  0.7 0.7 collective-permute-start.3
  1.5 1.2 copy-done
  2.7 0.7 copy-done.1
  3.4 0.7 copy-done.2
  4.0 1.0 select_rows.1
  5.2 2.7 %collective-permute-start.2 = (bf16[128,512]{1,0:T(8,128)(2,1)S(1)}, bf16[128,512]{1,0:T(8,128)(2,1)S(1)}, u32[]{:S(2)}, u32[]{:S(2)}) collective-permute-start(bf16[128,512]{1,0:T(8,128)(2,1)S(1)} %get-tuple-element.73), channel_id=1, source_target_pairs={{0,28},{8,20},{16,12},{24,4},{4,0},{12,8},{20,16},{28,24},{1,29},{... | collective-permute-start | bytes 393224 | tf_op jit(solution)/shard_map/ppermute | solution.py:383
  7.9 1.6 %collective-permute-done.refs_1_ = bf16[128,512]{1,0:T(8,128)(2,1)S(1)} collective-permute-done((bf16[128,512]{1,0:T(8,128)(2,1)S(1)}, bf16[128,512]{1,0:T(8,128)(2,1)S(1)}, u32[]{:S(2)}, u32[]{:S(2)}) %collective-permute-start) | collective-permute-done | bytes 131104 | tf_op jit(solution)/shard_map/ppermute | solution.py:383
  9.5 2.5 %collective-permute-done.1.refs_2_ = bf16[128,512]{1,0:T(8,128)(2,1)S(1)} collective-permute-done((bf16[128,512]{1,0:T(8,128)(2,1)S(1)}, bf16[128,512]{1,0:T(8,128)(2,1)S(1)}, u32[]{:S(2)}, u32[]{:S(2)}) %collective-permute-start.1) | collective-permute-done | bytes 131104 | tf_op jit(solution)/shard_map/ppermute | solution.py:383
  12.1 2.8 %collective-permute-done.2.refs_3_ = bf16[128,512]{1,0:T(8,128)(2,1)S(1)} collective-permute-done((bf16[128,512]{1,0:T(8,128)(2,1)S(1)}, bf16[128,512]{1,0:T(8,128)(2,1)S(1)}, u32[]{:S(2)}, u32[]{:S(2)}) %collective-permute-start.2) | collective-permute-done | bytes 131104 | tf_op jit(solution)/shard_map/ppermute | solution.py:383
  14.9 2.2 %place_rows.1 = (bf16[512,512]{1,0:T(8,128)(2,1)}, s32[512,128]{1,0:T(8,128)S(1)}) custom-call(s32[3]{0:T(128)S(1)} %pad_add_fusion.pos_ref, s32[16]{0:T(128)S(1)} %copy-done.1, s32[16]{0:T(128)S(1)} %copy-done.2, bf16[128,512]{1,0:T(8,128)(2,1)S(1)} %get-tuple-element.74.refs_0_, bf16[128,512]{1,0:T(8,128)(2,1)S(1)} %collective-permute-done.refs_1_, ...), custom_call_target="tpu_custom_call" | custom-call | tf_op jit(solution)/shard_map/place_rows/pallas_call | solution.py:440
  17.1 1.6 %collective-permute-start.5 = (bf16[512,512]{1,0:T(8,128)(2,1)}, bf16[512,512]{1,0:T(8,128)(2,1)}, u32[]{:S(2)}, u32[]{:S(2)}) collective-permute-start(bf16[512,512]{1,0:T(8,128)(2,1)} %get-tuple-element.78), channel_id=1, source_target_pairs={{4,1},{5,0},{6,3},{7,2},{0,4},{1,5},{2,6},{3,7},{12,9},{13,8},{14,... | collective-permute-start | bytes 1572872 | tf_op jit(solution)/shard_map/ppermute | solution.py:369
  18.7 1.6 %collective-permute-start.7 = (bf16[512,512]{1,0:T(8,128)(2,1)}, bf16[512,512]{1,0:T(8,128)(2,1)}, u32[]{:S(2)}, u32[]{:S(2)}) collective-permute-start(bf16[512,512]{1,0:T(8,128)(2,1)} %get-tuple-element.78), channel_id=1, source_target_pairs={{4,3},{5,2},{6,1},{7,0},{0,4},{1,5},{2,6},{3,7},{12,11},{13,10},{1... | collective-permute-start | bytes 1572872 | tf_op jit(solution)/shard_map/ppermute | solution.py:369
  20.3 1.8 %copy.16 = bf16[1,2048,8]{2,1,0:T(8,128)(2,1)} copy(bf16[1,2048,8]{1,2,0:T(8,128)(2,1)} %param.22) | data formatting | bytes 65536 | tf_op args[8]
  22.2 1.1 pad.11.refs_9_.refs_12_
  23.4 1.7 %collective-permute-done.5.refs_1_ = bf16[512,512]{1,0:T(8,128)(2,1)} collective-permute-done((bf16[512,512]{1,0:T(8,128)(2,1)}, bf16[512,512]{1,0:T(8,128)(2,1)}, u32[]{:S(2)}, u32[]{:S(2)}) %collective-permute-start.5) | collective-permute-done | bytes 524320 | tf_op jit(solution)/shard_map/ppermute | solution.py:369
  25.1 5.6 %collective-permute-done.7.refs_3_ = bf16[512,512]{1,0:T(8,128)(2,1)} collective-permute-done((bf16[512,512]{1,0:T(8,128)(2,1)}, bf16[512,512]{1,0:T(8,128)(2,1)}, u32[]{:S(2)}, u32[]{:S(2)}) %collective-permute-start.7) | collective-permute-done | bytes 524320 | tf_op jit(solution)/shard_map/ppermute | solution.py:369
  30.7 2.7 %layer_part.2 = (bf16[1552,512]{1,0:T(8,128)(2,1)}, bf16[528,512]{1,0:T(8,128)(2,1)S(1)}, bf16[528,512]{1,0:T(8,128)(2,1)S(1)}, bf16[528,512]{1,0:T(8,128)(2,1)S(1)}) custom-call(s32[3]{0:T(128)S(1)} %pad_add_fusion.pos_ref, bf16[512,512]{1,0:T(8,128)(2,1)} %collective-permute-done.4.refs_0_, bf16[512,512]{1,0:T(8,128)(2,1)} %collective-permute-done.5.refs_1_, ...), custom_call_target="tpu_custom_call" | custom-call | flops 4294967296 | bytes 12000000 | tf_op jit(solution)/shard_map/layer_part/pallas_call | solution.py:475
  33.5 13.1 %collective-permute-start.8 = (bf16[1552,512]{1,0:T(8,128)(2,1)}, bf16[1552,512]{1,0:T(8,128)(2,1)S(1)}, u32[]{:S(2)}, u32[]{:S(2)}) collective-permute-start(bf16[1552,512]{1,0:T(8,128)(2,1)} %get-tuple-element.80), channel_id=1, source_target_pairs={{0,4},{1,5},{2,6},{3,7},{4,0},{5,1},{6,2},{7,3},{8,12},{9,13},{10,... | collective-permute-start | bytes 4767752 | tf_op jit(solution)/shard_map/ppermute | solution.py:369
  47.2 1.0 collective-permute-start.9
  48.2 13.0 %collective-permute-done.10.refs_2_ = bf16[528,512]{1,0:T(8,128)(2,1)S(1)} collective-permute-done((bf16[528,512]{1,0:T(8,128)(2,1)S(1)}, bf16[528,512]{1,0:T(8,128)(2,1)S(1)}, u32[]{:S(2)}, u32[]{:S(2)}) %collective-permute-start.10) | collective-permute-done | bytes 540704 | tf_op jit(solution)/shard_map/ppermute | solution.py:369
  61.2 0.7 sum_parts.2
  62.0 1.9 %collective-permute-done.12.other_ref.refs_0_ = bf16[512,512]{1,0:T(8,128)(2,1)S(1)} collective-permute-done((bf16[512,512]{1,0:T(8,128)(2,1)S(1)}, bf16[512,512]{1,0:T(8,128)(2,1)S(1)}, u32[]{:S(2)}, u32[]{:S(2)}) %collective-permute-start.12) | collective-permute-done | bytes 524320 | tf_op jit(solution)/shard_map/ppermute | solution.py:530
  63.9 0.6 own_half.1
  64.5 1.3 collective-permute-start.13
  65.8 1.2 collective-permute-start.14
  67.2 5.1 %collective-permute-done.13.refs_1_.refs_2_ = bf16[256,512]{1,0:T(8,128)(2,1)S(1)} collective-permute-done((bf16[256,512]{1,0:T(8,128)(2,1)S(1)}, bf16[256,512]{1,0:T(8,128)(2,1)S(1)}, u32[]{:S(2)}, u32[]{:S(2)}) %collective-permute-start.13) | collective-permute-done | bytes 262176 | tf_op jit(solution)/shard_map/ppermute | solution.py:361
  72.3 2.0 %gradient_terms.2 = (bf16[512,512]{1,0:T(8,128)(2,1)S(1)}, bf16[512,512]{1,0:T(8,128)(2,1)S(1)}, bf16[512,512]{1,0:T(8,128)(2,1)S(1)}, bf16[512,512]{1,0:T(8,128)(2,1)S(1)}) custom-call(s32[3]{0:T(128)S(1)} %pad_add_fusion.pos_ref, bf16[512,512]{1,0:T(8,128)(2,1)S(1)} %get-tuple-element.86.refs_0_, bf16[512,2048]{1,0:T(8,128)(2,1)S(1)} %collective-permute-done.3.refs_1_), custom_call_target="tpu_custom_call" | custom-call | flops 1073741824 | bytes 5000000 | tf_op jit(solution)/shard_map/gradient_terms/pallas_call | solution.py:513
  74.4 4.6 %collective-permute-done.15.refs_5_.refs_6_ = bf16[256,512]{1,0:T(8,128)(2,1)S(1)} collective-permute-done((bf16[256,512]{1,0:T(8,128)(2,1)S(1)}, bf16[256,512]{1,0:T(8,128)(2,1)S(1)}, u32[]{:S(2)}, u32[]{:S(2)}) %collective-permute-start.15) | collective-permute-done | bytes 262176 | tf_op jit(solution)/shard_map/ppermute | solution.py:361
  79.0 1.2 collective-permute-start.16
  80.6 0.7 collective-permute-done.16.refs_2_.refs_1_
  82.0 1.5 %collective-permute-start.19 = (bf16[512,512]{1,0:T(8,128)(2,1)S(1)}, bf16[512,512]{1,0:T(8,128)(2,1)S(1)}, u32[]{:S(2)}, u32[]{:S(2)}) collective-permute-start(bf16[512,512]{1,0:T(8,128)(2,1)S(1)} %get-tuple-element.111), channel_id=1, source_target_pairs={{4,24},{12,16},{20,8},{28,0},{0,4},{8,12},{16,20},{24,28},{5,25},{... | collective-permute-start | bytes 1572872 | tf_op jit(solution)/shard_map/ppermute | solution.py:383
  83.5 12.4 %layer_part.3 = (bf16[1552,512]{1,0:T(8,128)(2,1)}, bf16[528,512]{1,0:T(8,128)(2,1)S(1)}, bf16[528,512]{1,0:T(8,128)(2,1)S(1)}, bf16[528,512]{1,0:T(8,128)(2,1)S(1)}) custom-call(s32[3]{0:T(128)S(1)} %pad_add_fusion.pos_ref, bf16[512,512]{1,0:T(8,128)(2,1)S(1)} %get-tuple-element.100.own_ref.refs_0_, ...), custom_call_target="tpu_custom_call" | custom-call | flops 4294967296 | bytes 12000000 | tf_op jit(solution)/shard_map/layer_part/pallas_call | solution.py:475
  96.0 0.7 collective-permute-start.20
  96.6 0.8 collective-permute-start.21
  97.4 0.8 collective-permute-start.22
  98.2 1.1 collective-permute-start.23
  99.3 11.7 %collective-permute-done.24.refs_1_ = bf16[512,512]{1,0:T(8,128)(2,1)S(1)} collective-permute-done((bf16[512,512]{1,0:T(8,128)(2,1)S(1)}, bf16[512,512]{1,0:T(8,128)(2,1)S(1)}, u32[]{:S(2)}, u32[]{:S(2)}) %collective-permute-start.24) | collective-permute-done | bytes 524320 | tf_op jit(solution)/shard_map/ppermute | solution.py:383
  111.1 0.7 sum_parts.3
  112.4 2.4 %collective-permute-start.31 = (bf16[512,512]{1,0:T(8,128)(2,1)S(1)}, bf16[512,512]{1,0:T(8,128)(2,1)S(1)}, u32[]{:S(2)}, u32[]{:S(2)}) collective-permute-start(bf16[512,512]{1,0:T(8,128)(2,1)S(1)} %get-tuple-element.129), channel_id=1, source_target_pairs={{0,4},{8,12},{16,20},{24,28},{4,0},{12,8},{20,16},{28,24},{1,5},{9... | collective-permute-start | bytes 1572872 | tf_op jit(solution)/shard_map/ppermute | solution.py:383
  115.7 0.7 collective-permute-start.28
  116.5 1.1 collective-permute-start.32
  117.6 1.6 %collective-permute-start.33 = (bf16[512,512]{1,0:T(8,128)(2,1)S(1)}, bf16[512,512]{1,0:T(8,128)(2,1)S(1)}, u32[]{:S(2)}, u32[]{:S(2)}) collective-permute-start(bf16[512,512]{1,0:T(8,128)(2,1)S(1)} %get-tuple-element.131), channel_id=1, source_target_pairs={{0,20},{8,28},{16,4},{24,12},{4,0},{12,8},{20,16},{28,24},{1,21},{... | collective-permute-start | bytes 1572872 | tf_op jit(solution)/shard_map/ppermute | solution.py:383
  119.2 4.3 %collective-permute-done.26.refs_8_ = bf16[512,512]{1,0:T(8,128)(2,1)S(1)} collective-permute-done((bf16[512,512]{1,0:T(8,128)(2,1)S(1)}, bf16[512,512]{1,0:T(8,128)(2,1)S(1)}, u32[]{:S(2)}, u32[]{:S(2)}) %collective-permute-start.26) | collective-permute-done | bytes 524320 | tf_op jit(solution)/shard_map/ppermute | solution.py:369
  123.9 3.5 %collective-permute-start.29 = (bf16[512,512]{1,0:T(8,128)(2,1)S(1)}, bf16[512,512]{1,0:T(8,128)(2,1)S(1)}, u32[]{:S(2)}, u32[]{:S(2)}) collective-permute-start(bf16[512,512]{1,0:T(8,128)(2,1)S(1)} %get-tuple-element.136), channel_id=1, source_target_pairs={{4,8},{12,0},{20,24},{28,16},{0,4},{8,12},{16,20},{24,28},{5,9},{1... | collective-permute-start | bytes 1572872 | tf_op jit(solution)/shard_map/ppermute | solution.py:383
  127.3 2.2 %collective-permute-done.28.refs_10_ = bf16[512,512]{1,0:T(8,128)(2,1)S(1)} collective-permute-done((bf16[512,512]{1,0:T(8,128)(2,1)S(1)}, bf16[512,512]{1,0:T(8,128)(2,1)S(1)}, u32[]{:S(2)}, u32[]{:S(2)}) %collective-permute-start.28) | collective-permute-done | bytes 524320 | tf_op jit(solution)/shard_map/ppermute | solution.py:369
  129.6 1.9 %assemble_rows.1 = bf16[1,512,2048]{2,1,0:T(8,128)(2,1)} custom-call(s32[3]{0:T(128)S(1)} %pad_add_fusion.pos_ref, bf16[512,512]{1,0:T(8,128)(2,1)S(1)} %collective-permute-done.12.other_ref.refs_0_, bf16[256,512]{1,0:T(8,128)(2,1)S(1)} %collective-permute-done.16.refs_2_.refs_1_, bf16[256,512]{1,0:T(8,128)(2,1)S(1)} %collective-permute-done.13.refs_1_.refs_2_, ...), custom_call_target="tpu_custom_call" | custom-call | flops 1000000 | bytes 4000000 | tf_op jit(solution)/shard_map/assemble_rows/pallas_call | solution.py:581
  132.0 12.9 %collective-permute-done.34.refs_7_ = bf16[512,512]{1,0:T(8,128)(2,1)S(1)} collective-permute-done((bf16[512,512]{1,0:T(8,128)(2,1)S(1)}, bf16[512,512]{1,0:T(8,128)(2,1)S(1)}, u32[]{:S(2)}, u32[]{:S(2)}) %collective-permute-start.34) | collective-permute-done | bytes 524320 | tf_op jit(solution)/shard_map/ppermute | solution.py:383
  144.9 1.6 %gradient_total.1 = bf16[1,512,512]{2,1,0:T(8,128)(2,1)} custom-call(s32[3]{0:T(128)S(1)} %pad_add_fusion.pos_ref, bf16[512,512]{1,0:T(8,128)(2,1)S(1)} %collective-permute-done.19.refs_0_, bf16[512,512]{1,0:T(8,128)(2,1)S(1)} %collective-permute-done.24.refs_1_, bf16[512,512]{1,0:T(8,128)(2,1)S(1)} %collective-permute-done.29.refs_2_, ...), custom_call_target="tpu_custom_call" | custom-call | flops 1000000 | bytes 4000000 | tf_op jit(solution)/shard_map/gradient_total/pallas_call | solution.py:591
  (58 shorter events, 5.2 us)
Async XLA Ops:
  0.6 21.4 %copy-start.6 = (f32[1,8]{1,0:T(1,128)S(1)}, f32[1,8]{1,0:T(1,128)}, u32[]{:S(2)}) copy-start(f32[1,8]{1,0:T(1,128)} %param.25) | copy-start | bytes 100
  0.6 21.5 %copy-start.7 = (f32[1,8]{1,0:T(1,128)S(1)}, f32[1,8]{1,0:T(1,128)}, u32[]{:S(2)}) copy-start(f32[1,8]{1,0:T(1,128)} %param.23) | copy-start | bytes 100
  0.7 21.5 %copy-start.8 = (f32[1,8]{1,0:T(1,128)S(1)}, f32[1,8]{1,0:T(1,128)}, u32[]{:S(2)}) copy-start(f32[1,8]{1,0:T(1,128)} %param.24) | copy-start | bytes 100
  0.7 30.1 %copy-start.4 = (f32[1,2048]{1,0:T(1,128)S(1)}, f32[1,2048]{1,0:T(1,128)}, u32[]{:S(2)}) copy-start(f32[1,2048]{1,0:T(1,128)} %refs_8_.1) | copy-start | bytes 24580
  0.7 30.1 %copy-start.5 = (f32[1,512]{1,0:T(1,128)S(1)}, f32[1,512]{1,0:T(1,128)}, u32[]{:S(2)}) copy-start(f32[1,512]{1,0:T(1,128)} %refs_16_.1) | copy-start | bytes 6148
  0.7 14.2 %collective-permute-start.3 = (bf16[512,2048]{1,0:T(8,128)(2,1)}, bf16[512,2048]{1,0:T(8,128)(2,1)S(1)}, u32[]{:S(2)}, u32[]{:S(2)}) collective-permute-start(bf16[512,2048]{1,0:T(8,128)(2,1)} %bitcast.14), channel_id=1, source_target_pairs={{0,4},{4,0},{1,5},{5,1},{2,6},{6,2},{3,7},{7,3},{8,12},{12,8},{9,1... | collective-permute-start | bytes 6291464 | tf_op jit(solution)/shard_map/ppermute | solution.py:437
  1.5 1.2 copy-start
  2.7 0.7 copy-start.1
  3.4 0.7 copy-start.2
  4.0 26.7 %copy-start.3 = (bf16[1,2048,256]{2,1,0:T(8,128)(2,1)S(1)}, bf16[1,2048,256]{2,1,0:T(8,128)(2,1)}, u32[]{:S(2)}) copy-start(bf16[1,2048,256]{2,1,0:T(8,128)(2,1)} %param.21) | copy-start | bytes 3145732
  5.1 4.4 %collective-permute-start = (bf16[128,512]{1,0:T(8,128)(2,1)S(1)}, bf16[128,512]{1,0:T(8,128)(2,1)S(1)}, u32[]{:S(2)}, u32[]{:S(2)}) collective-permute-start(bf16[128,512]{1,0:T(8,128)(2,1)S(1)} %get-tuple-element.71), channel_id=1, source_target_pairs={{0,12},{8,4},{16,28},{24,20},{4,0},{12,8},{20,16},{28,24},{1,13},{... | collective-permute-start | bytes 393224 | tf_op jit(solution)/shard_map/ppermute | solution.py:383
  5.2 6.9 %collective-permute-start.1 = (bf16[128,512]{1,0:T(8,128)(2,1)S(1)}, bf16[128,512]{1,0:T(8,128)(2,1)S(1)}, u32[]{:S(2)}, u32[]{:S(2)}) collective-permute-start(bf16[128,512]{1,0:T(8,128)(2,1)S(1)} %get-tuple-element.72), channel_id=1, source_target_pairs={{0,20},{8,28},{16,4},{24,12},{4,0},{12,8},{20,16},{28,24},{1,21},{... | collective-permute-start | bytes 393224 | tf_op jit(solution)/shard_map/ppermute | solution.py:383
  5.2 9.7 %collective-permute-start.2 = (bf16[128,512]{1,0:T(8,128)(2,1)S(1)}, bf16[128,512]{1,0:T(8,128)(2,1)S(1)}, u32[]{:S(2)}, u32[]{:S(2)}) collective-permute-start(bf16[128,512]{1,0:T(8,128)(2,1)S(1)} %get-tuple-element.73), channel_id=1, source_target_pairs={{0,28},{8,20},{16,12},{24,4},{4,0},{12,8},{20,16},{28,24},{1,29},{... | collective-permute-start | bytes 393224 | tf_op jit(solution)/shard_map/ppermute | solution.py:383
  17.1 6.3 %collective-permute-start.4 = (bf16[512,512]{1,0:T(8,128)(2,1)}, bf16[512,512]{1,0:T(8,128)(2,1)}, u32[]{:S(2)}, u32[]{:S(2)}) collective-permute-start(bf16[512,512]{1,0:T(8,128)(2,1)} %get-tuple-element.78), channel_id=1, source_target_pairs={{4,0},{5,1},{6,2},{7,3},{0,4},{1,5},{2,6},{3,7},{12,8},{13,9},{14,... | collective-permute-start | bytes 1572872 | tf_op jit(solution)/shard_map/ppermute | solution.py:369
  17.1 8.0 %collective-permute-start.5 = (bf16[512,512]{1,0:T(8,128)(2,1)}, bf16[512,512]{1,0:T(8,128)(2,1)}, u32[]{:S(2)}, u32[]{:S(2)}) collective-permute-start(bf16[512,512]{1,0:T(8,128)(2,1)} %get-tuple-element.78), channel_id=1, source_target_pairs={{4,1},{5,0},{6,3},{7,2},{0,4},{1,5},{2,6},{3,7},{12,9},{13,8},{14,... | collective-permute-start | bytes 1572872 | tf_op jit(solution)/shard_map/ppermute | solution.py:369
  18.7 6.5 %collective-permute-start.6 = (bf16[512,512]{1,0:T(8,128)(2,1)}, bf16[512,512]{1,0:T(8,128)(2,1)}, u32[]{:S(2)}, u32[]{:S(2)}) collective-permute-start(bf16[512,512]{1,0:T(8,128)(2,1)} %get-tuple-element.78), channel_id=1, source_target_pairs={{4,2},{5,3},{6,0},{7,1},{0,4},{1,5},{2,6},{3,7},{12,10},{13,11},{1... | collective-permute-start | bytes 1572872 | tf_op jit(solution)/shard_map/ppermute | solution.py:369
  18.7 12.0 %collective-permute-start.7 = (bf16[512,512]{1,0:T(8,128)(2,1)}, bf16[512,512]{1,0:T(8,128)(2,1)}, u32[]{:S(2)}, u32[]{:S(2)}) collective-permute-start(bf16[512,512]{1,0:T(8,128)(2,1)} %get-tuple-element.78), channel_id=1, source_target_pairs={{4,3},{5,2},{6,1},{7,0},{0,4},{1,5},{2,6},{3,7},{12,11},{13,10},{1... | collective-permute-start | bytes 1572872 | tf_op jit(solution)/shard_map/ppermute | solution.py:369
  33.5 27.7 %collective-permute-start.8 = (bf16[1552,512]{1,0:T(8,128)(2,1)}, bf16[1552,512]{1,0:T(8,128)(2,1)S(1)}, u32[]{:S(2)}, u32[]{:S(2)}) collective-permute-start(bf16[1552,512]{1,0:T(8,128)(2,1)} %get-tuple-element.80), channel_id=1, source_target_pairs={{0,4},{1,5},{2,6},{3,7},{4,0},{5,1},{6,2},{7,3},{8,12},{9,13},{10,... | collective-permute-start | bytes 4767752 | tf_op jit(solution)/shard_map/ppermute | solution.py:369
  46.6 14.6 %collective-permute-start.10 = (bf16[528,512]{1,0:T(8,128)(2,1)S(1)}, bf16[528,512]{1,0:T(8,128)(2,1)S(1)}, u32[]{:S(2)}, u32[]{:S(2)}) collective-permute-start(bf16[528,512]{1,0:T(8,128)(2,1)S(1)} %get-tuple-element.82), channel_id=1, source_target_pairs={{0,6},{1,7},{2,4},{3,5},{4,0},{5,1},{6,2},{7,3},{8,14},{9,15},{10,... | collective-permute-start | bytes 1622024 | tf_op jit(solution)/shard_map/ppermute | solution.py:369
  46.6 14.5 %collective-permute-start.11 = (bf16[528,512]{1,0:T(8,128)(2,1)S(1)}, bf16[528,512]{1,0:T(8,128)(2,1)S(1)}, u32[]{:S(2)}, u32[]{:S(2)}) collective-permute-start(bf16[528,512]{1,0:T(8,128)(2,1)S(1)} %get-tuple-element.83), channel_id=1, source_target_pairs={{0,7},{1,6},{2,5},{3,4},{4,0},{5,1},{6,2},{7,3},{8,15},{9,14},{10,... | collective-permute-start | bytes 1622024 | tf_op jit(solution)/shard_map/ppermute | solution.py:369
  47.2 14.0 %collective-permute-start.9 = (bf16[528,512]{1,0:T(8,128)(2,1)S(1)}, bf16[528,512]{1,0:T(8,128)(2,1)S(1)}, u32[]{:S(2)}, u32[]{:S(2)}) collective-permute-start(bf16[528,512]{1,0:T(8,128)(2,1)S(1)} %get-tuple-element.81), channel_id=1, source_target_pairs={{0,5},{1,4},{2,7},{3,6},{4,0},{5,1},{6,2},{7,3},{8,13},{9,12},{10,... | collective-permute-start | bytes 1622024 | tf_op jit(solution)/shard_map/ppermute | solution.py:369
  62.0 2.0 %collective-permute-start.12 = (bf16[512,512]{1,0:T(8,128)(2,1)S(1)}, bf16[512,512]{1,0:T(8,128)(2,1)S(1)}, u32[]{:S(2)}, u32[]{:S(2)}) collective-permute-start(bf16[512,512]{1,0:T(8,128)(2,1)S(1)} %get-tuple-element.100.own_ref.refs_0_), channel_id=1, source_target_pairs={{0,4},{4,0},{1,5},{5,1},{2,6},{6,2},{3,7},{7,3},{8,12},{12,8},{9,1... | collective-permute-start | bytes 1572872 | tf_op jit(solution)/shard_map/ppermute | solution.py:530
  64.5 7.8 %collective-permute-start.13 = (bf16[256,512]{1,0:T(8,128)(2,1)S(1)}, bf16[256,512]{1,0:T(8,128)(2,1)S(1)}, u32[]{:S(2)}, u32[]{:S(2)}) collective-permute-start(bf16[256,512]{1,0:T(8,128)(2,1)S(1)} %own_half.1), channel_id=1, source_target_pairs={{0,1},{1,0},{2,3},{3,2},{4,5},{5,4},{6,7},{7,6},{8,9},{9,8},{10,11... | collective-permute-start | bytes 786440 | tf_op jit(solution)/shard_map/ppermute | solution.py:361
  65.8 8.6 %collective-permute-start.14 = (bf16[256,512]{1,0:T(8,128)(2,1)S(1)}, bf16[256,512]{1,0:T(8,128)(2,1)S(1)}, u32[]{:S(2)}, u32[]{:S(2)}) collective-permute-start(bf16[256,512]{1,0:T(8,128)(2,1)S(1)} %own_half.1), channel_id=1, source_target_pairs={{0,2},{1,3},{2,0},{3,1},{4,6},{5,7},{6,4},{7,5},{8,10},{9,11},{10,... | collective-permute-start | bytes 786440 | tf_op jit(solution)/shard_map/ppermute | solution.py:361
  67.0 12.0 %collective-permute-start.15 = (bf16[256,512]{1,0:T(8,128)(2,1)S(1)}, bf16[256,512]{1,0:T(8,128)(2,1)S(1)}, u32[]{:S(2)}, u32[]{:S(2)}) collective-permute-start(bf16[256,512]{1,0:T(8,128)(2,1)S(1)} %own_half.1), channel_id=1, source_target_pairs={{0,3},{1,2},{2,1},{3,0},{4,7},{5,6},{6,5},{7,4},{8,11},{9,10},{10,... | collective-permute-start | bytes 786440 | tf_op jit(solution)/shard_map/ppermute | solution.py:361
  79.0 2.3 %collective-permute-start.16 = (bf16[256,512]{1,0:T(8,128)(2,1)S(1)}, bf16[256,512]{1,0:T(8,128)(2,1)S(1)}, u32[]{:S(2)}, u32[]{:S(2)}) collective-permute-start(bf16[256,512]{1,0:T(8,128)(2,1)S(1)} %collective-permute-done.13.refs_1_.refs_2_), channel_id=1, source_target_pairs={{0,4},{4,0},{1,5},{5,1},{2,6},{6,2},{3,7},{7,3},{8,12},{12,8},{9,1... | collective-permute-start | bytes 786440 | tf_op jit(solution)/shard_map/ppermute | solution.py:544
  80.1 1.5 %collective-permute-start.17 = (bf16[256,512]{1,0:T(8,128)(2,1)S(1)}, bf16[256,512]{1,0:T(8,128)(2,1)S(1)}, u32[]{:S(2)}, u32[]{:S(2)}) collective-permute-start(bf16[256,512]{1,0:T(8,128)(2,1)S(1)} %collective-permute-done.14.refs_3_.refs_4_), channel_id=1, source_target_pairs={{0,4},{4,0},{1,5},{5,1},{2,6},{6,2},{3,7},{7,3},{8,12},{12,8},{9,1... | collective-permute-start | bytes 786440 | tf_op jit(solution)/shard_map/ppermute | solution.py:544
  80.1 1.9 %collective-permute-start.18 = (bf16[256,512]{1,0:T(8,128)(2,1)S(1)}, bf16[256,512]{1,0:T(8,128)(2,1)S(1)}, u32[]{:S(2)}, u32[]{:S(2)}) collective-permute-start(bf16[256,512]{1,0:T(8,128)(2,1)S(1)} %collective-permute-done.15.refs_5_.refs_6_), channel_id=1, source_target_pairs={{0,4},{4,0},{1,5},{5,1},{2,6},{6,2},{3,7},{7,3},{8,12},{12,8},{9,1... | collective-permute-start | bytes 786440 | tf_op jit(solution)/shard_map/ppermute | solution.py:544
  82.0 13.9 %collective-permute-start.19 = (bf16[512,512]{1,0:T(8,128)(2,1)S(1)}, bf16[512,512]{1,0:T(8,128)(2,1)S(1)}, u32[]{:S(2)}, u32[]{:S(2)}) collective-permute-start(bf16[512,512]{1,0:T(8,128)(2,1)S(1)} %get-tuple-element.111), channel_id=1, source_target_pairs={{4,24},{12,16},{20,8},{28,0},{0,4},{8,12},{16,20},{24,28},{5,25},{... | collective-permute-start | bytes 1572872 | tf_op jit(solution)/shard_map/ppermute | solution.py:383
  96.0 15.1 %collective-permute-start.20 = (bf16[1552,512]{1,0:T(8,128)(2,1)}, bf16[1552,512]{1,0:T(8,128)(2,1)S(1)}, u32[]{:S(2)}, u32[]{:S(2)}) collective-permute-start(bf16[1552,512]{1,0:T(8,128)(2,1)} %get-tuple-element.115), channel_id=1, source_target_pairs={{4,0},{5,1},{6,2},{7,3},{0,4},{1,5},{2,6},{3,7},{12,8},{13,9},{14,... | collective-permute-start | bytes 4767752 | tf_op jit(solution)/shard_map/ppermute | solution.py:369
  96.6 14.4 %collective-permute-start.21 = (bf16[528,512]{1,0:T(8,128)(2,1)S(1)}, bf16[528,512]{1,0:T(8,128)(2,1)S(1)}, u32[]{:S(2)}, u32[]{:S(2)}) collective-permute-start(bf16[528,512]{1,0:T(8,128)(2,1)S(1)} %get-tuple-element.116), channel_id=1, source_target_pairs={{4,1},{5,0},{6,3},{7,2},{0,4},{1,5},{2,6},{3,7},{12,9},{13,8},{14,... | collective-permute-start | bytes 1622024 | tf_op jit(solution)/shard_map/ppermute | solution.py:369
  97.4 13.6 %collective-permute-start.22 = (bf16[528,512]{1,0:T(8,128)(2,1)S(1)}, bf16[528,512]{1,0:T(8,128)(2,1)S(1)}, u32[]{:S(2)}, u32[]{:S(2)}) collective-permute-start(bf16[528,512]{1,0:T(8,128)(2,1)S(1)} %get-tuple-element.117), channel_id=1, source_target_pairs={{4,2},{5,3},{6,0},{7,1},{0,4},{1,5},{2,6},{3,7},{12,10},{13,11},{1... | collective-permute-start | bytes 1622024 | tf_op jit(solution)/shard_map/ppermute | solution.py:369
  98.2 12.8 %collective-permute-start.23 = (bf16[528,512]{1,0:T(8,128)(2,1)S(1)}, bf16[528,512]{1,0:T(8,128)(2,1)S(1)}, u32[]{:S(2)}, u32[]{:S(2)}) collective-permute-start(bf16[528,512]{1,0:T(8,128)(2,1)S(1)} %get-tuple-element.118), channel_id=1, source_target_pairs={{4,3},{5,2},{6,1},{7,0},{0,4},{1,5},{2,6},{3,7},{12,11},{13,10},{1... | collective-permute-start | bytes 1622024 | tf_op jit(solution)/shard_map/ppermute | solution.py:369
  99.3 11.7 %collective-permute-start.24 = (bf16[512,512]{1,0:T(8,128)(2,1)S(1)}, bf16[512,512]{1,0:T(8,128)(2,1)S(1)}, u32[]{:S(2)}, u32[]{:S(2)}) collective-permute-start(bf16[512,512]{1,0:T(8,128)(2,1)S(1)} %get-tuple-element.120), channel_id=1, source_target_pairs={{4,16},{12,24},{20,0},{28,8},{0,4},{8,12},{16,20},{24,28},{5,17},{... | collective-permute-start | bytes 1572872 | tf_op jit(solution)/shard_map/ppermute | solution.py:383
  112.4 4.1 %collective-permute-start.31 = (bf16[512,512]{1,0:T(8,128)(2,1)S(1)}, bf16[512,512]{1,0:T(8,128)(2,1)S(1)}, u32[]{:S(2)}, u32[]{:S(2)}) collective-permute-start(bf16[512,512]{1,0:T(8,128)(2,1)S(1)} %get-tuple-element.129), channel_id=1, source_target_pairs={{0,4},{8,12},{16,20},{24,28},{4,0},{12,8},{20,16},{28,24},{1,5},{9... | collective-permute-start | bytes 1572872 | tf_op jit(solution)/shard_map/ppermute | solution.py:383
  114.8 2.9 %collective-permute-start.25 = (bf16[512,512]{1,0:T(8,128)(2,1)S(1)}, bf16[512,512]{1,0:T(8,128)(2,1)S(1)}, u32[]{:S(2)}, u32[]{:S(2)}) collective-permute-start(bf16[512,512]{1,0:T(8,128)(2,1)S(1)} %get-tuple-element.133), channel_id=1, source_target_pairs={{0,4},{1,5},{2,6},{3,7},{4,0},{5,1},{6,2},{7,3},{8,12},{9,13},{10,... | collective-permute-start | bytes 1572872 | tf_op jit(solution)/shard_map/ppermute | solution.py:369
  114.8 8.6 %collective-permute-start.26 = (bf16[512,512]{1,0:T(8,128)(2,1)S(1)}, bf16[512,512]{1,0:T(8,128)(2,1)S(1)}, u32[]{:S(2)}, u32[]{:S(2)}) collective-permute-start(bf16[512,512]{1,0:T(8,128)(2,1)S(1)} %get-tuple-element.133), channel_id=1, source_target_pairs={{0,5},{1,4},{2,7},{3,6},{4,0},{5,1},{6,2},{7,3},{8,13},{9,12},{10,... | collective-permute-start | bytes 1572872 | tf_op jit(solution)/shard_map/ppermute | solution.py:369
  115.3 8.6 %collective-permute-start.27 = (bf16[512,512]{1,0:T(8,128)(2,1)S(1)}, bf16[512,512]{1,0:T(8,128)(2,1)S(1)}, u32[]{:S(2)}, u32[]{:S(2)}) collective-permute-start(bf16[512,512]{1,0:T(8,128)(2,1)S(1)} %get-tuple-element.133), channel_id=1, source_target_pairs={{0,6},{1,7},{2,4},{3,5},{4,0},{5,1},{6,2},{7,3},{8,14},{9,15},{10,... | collective-permute-start | bytes 1572872 | tf_op jit(solution)/shard_map/ppermute | solution.py:369
  115.7 13.8 %collective-permute-start.28 = (bf16[512,512]{1,0:T(8,128)(2,1)S(1)}, bf16[512,512]{1,0:T(8,128)(2,1)S(1)}, u32[]{:S(2)}, u32[]{:S(2)}) collective-permute-start(bf16[512,512]{1,0:T(8,128)(2,1)S(1)} %get-tuple-element.133), channel_id=1, source_target_pairs={{0,7},{1,6},{2,5},{3,4},{4,0},{5,1},{6,2},{7,3},{8,15},{9,14},{10,... | collective-permute-start | bytes 1572872 | tf_op jit(solution)/shard_map/ppermute | solution.py:369
  116.5 15.1 %collective-permute-start.32 = (bf16[512,512]{1,0:T(8,128)(2,1)S(1)}, bf16[512,512]{1,0:T(8,128)(2,1)S(1)}, u32[]{:S(2)}, u32[]{:S(2)}) collective-permute-start(bf16[512,512]{1,0:T(8,128)(2,1)S(1)} %get-tuple-element.130), channel_id=1, source_target_pairs={{0,12},{8,4},{16,28},{24,20},{4,0},{12,8},{20,16},{28,24},{1,13},{... | collective-permute-start | bytes 1572872 | tf_op jit(solution)/shard_map/ppermute | solution.py:383
  117.6 14.4 %collective-permute-start.33 = (bf16[512,512]{1,0:T(8,128)(2,1)S(1)}, bf16[512,512]{1,0:T(8,128)(2,1)S(1)}, u32[]{:S(2)}, u32[]{:S(2)}) collective-permute-start(bf16[512,512]{1,0:T(8,128)(2,1)S(1)} %get-tuple-element.131), channel_id=1, source_target_pairs={{0,20},{8,28},{16,4},{24,12},{4,0},{12,8},{20,16},{28,24},{1,21},{... | collective-permute-start | bytes 1572872 | tf_op jit(solution)/shard_map/ppermute | solution.py:383
  123.4 21.4 %collective-permute-start.34 = (bf16[512,512]{1,0:T(8,128)(2,1)S(1)}, bf16[512,512]{1,0:T(8,128)(2,1)S(1)}, u32[]{:S(2)}, u32[]{:S(2)}) collective-permute-start(bf16[512,512]{1,0:T(8,128)(2,1)S(1)} %get-tuple-element.132), channel_id=1, source_target_pairs={{0,28},{8,20},{16,12},{24,4},{4,0},{12,8},{20,16},{28,24},{1,29},{... | collective-permute-start | bytes 1572872 | tf_op jit(solution)/shard_map/ppermute | solution.py:383
  123.9 21.0 %collective-permute-start.29 = (bf16[512,512]{1,0:T(8,128)(2,1)S(1)}, bf16[512,512]{1,0:T(8,128)(2,1)S(1)}, u32[]{:S(2)}, u32[]{:S(2)}) collective-permute-start(bf16[512,512]{1,0:T(8,128)(2,1)S(1)} %get-tuple-element.136), channel_id=1, source_target_pairs={{4,8},{12,0},{20,24},{28,16},{0,4},{8,12},{16,20},{24,28},{5,9},{1... | collective-permute-start | bytes 1572872 | tf_op jit(solution)/shard_map/ppermute | solution.py:383
  129.6 15.3 %collective-permute-start.30 = (bf16[512,512]{1,0:T(8,128)(2,1)S(1)}, bf16[512,512]{1,0:T(8,128)(2,1)S(1)}, u32[]{:S(2)}, u32[]{:S(2)}) collective-permute-start(bf16[512,512]{1,0:T(8,128)(2,1)S(1)} %get-tuple-element.137), channel_id=1, source_target_pairs={{4,0},{12,8},{20,16},{28,24},{0,4},{8,12},{16,20},{24,28},{5,1},{1... | collective-permute-start | bytes 1572872 | tf_op jit(solution)/shard_map/ppermute | solution.py:383

commit v3 on v2

--- a/solution.py
+++ b/solution.py
@@ -74,10 +74,14 @@
 
 
 def select_kernel(dp_count, cap, pos_ref, rows_ref, owner_ref, tokens_ref, *refs):
-    outs, (slot_ref, count_ref) = refs[:dp_count], refs[dp_count:]
+    outs, (slot_ref, count_ref, held_ref, sem) = refs[:dp_count], refs[dp_count:]
     me, part = pos_ref[0], pos_ref[1]
     tok_rows = tokens_ref.shape[0]
     width = outs[0].shape[1]
+    load = pltpu.make_async_copy(
+        tokens_ref.at[:, pl.ds(pl.multiple_of(part * width, width), width)], held_ref, sem
+    )
+    load.start()
     local = iota((8, tok_rows), 1)
     slot_ref[...] = jnp.full((8, tok_rows), -1, jnp.int32)
 
@@ -86,7 +90,8 @@
         slot_ref[...] = jnp.where(inside, local + (owner * cap + owner_start - start), slot_ref[...])
 
     walk_baselines(rows_ref, owner_ref, count_ref, dp_count, visit)
-    columns = tokens_ref[:, pl.ds(pl.multiple_of(part * width, width), width)]
+    load.wait()
+    columns = held_ref[...]
     slots = slot_ref[0:1, :]
     for k in range(dp_count):
         owner = me ^ k
@@ -256,7 +261,7 @@
 
 
 def sum_kernel(tensor, inner_all, rows, *refs):
-    parts, (out_ref, y_ref) = refs[:tensor], refs[tensor:]
+    parts, outs, y_ref = refs[:tensor], refs[tensor:-1], refs[-1]
     width = parts[0].shape[1]
     tail = rows + EXTRA
     ones = jnp.ones((EXTRA, TILE), BF16)
@@ -266,20 +271,21 @@
         columns = slice(c, c + TILE)
         total = sum(part[0:rows, columns].astype(F32) for part in parts)
         residual = parts[0][tail + rows : tail + 2 * rows, columns].astype(F32)
-        out_ref[:, columns] = (residual + total * scale).astype(BF16)
+        result = (residual + total * scale).astype(BF16)
+        size = rows // len(outs)
+        for index, out_ref in enumerate(outs):
+            out_ref[:, columns] = result[index * size : (index + 1) * size, :]
         y_ref[:, columns] = (parts[0][tail : tail + rows, columns].astype(F32) * scale).astype(BF16)
 
 
 def half_kernel(pos_ref, own_ref, other_ref, out_ref):
-    rows = out_ref.shape[0]
-
     @pl.when(pos_ref[2] == 0)
     def _():
-        out_ref[...] = other_ref[rows : 2 * rows, :]
+        out_ref[...] = other_ref[...]
 
     @pl.when(pos_ref[2] != 0)
     def _():
-        out_ref[...] = own_ref[0:rows, :]
+        out_ref[...] = own_ref[...]
 
 
 def grad_kernel(active, pieces, pos_ref, *refs):
@@ -362,7 +368,7 @@
     ]
 
 
-def tensor_cross(values, active):
+def tensor_cross(values, active, first=0):
     count = lax.axis_size("tensor")
     other = 1 - active
     return [
@@ -372,7 +378,7 @@
             [(active * count + t, other * count + (t ^ k)) for t in range(count)]
             + [(other * count + t, active * count + t) for t in range(count)],
         )
-        for k, value in enumerate(values)
+        for k, value in enumerate(values, first)
     ]
 
 
@@ -425,9 +431,14 @@
     outgoing = pl.pallas_call(
         functools.partial(select_kernel, dp_count, cap),
         out_shape=[shape((cap, width), BF16)] * dp_count,
-        in_specs=[smem()] * 3 + [vmem()],
+        in_specs=[smem()] * 3 + [pl.BlockSpec(memory_space=pl.ANY)],
         out_specs=[vmem()] * dp_count,
-        scratch_shapes=[pltpu.VMEM((8, tok_rows), jnp.int32), pltpu.SMEM((dp_count,), jnp.int32)],
+        scratch_shapes=[
+            pltpu.VMEM((8, tok_rows), jnp.int32),
+            pltpu.SMEM((dp_count,), jnp.int32),
+            pltpu.VMEM((tok_rows, width), BF16),
+            pltpu.SemaphoreType.DMA,
+        ],
         compiler_params=params(),
         name="select_rows",
     )(*tables, tokens)
@@ -498,12 +509,13 @@
             name="layer_part",
         )(pos, *[piece for pieces in blocks for piece in pieces], seg, *weights)
 
-    def finish(parts):
+    def finish(parts, count):
         return pl.pallas_call(
             functools.partial(sum_kernel, tensor, inner * tensor, own_slots),
-            out_shape=[shape((own_slots, width), BF16), shape((own_slots, inner), BF16)],
+            out_shape=[shape((own_slots // count, width), BF16)] * count
+            + [shape((own_slots, inner), BF16)],
             in_specs=[vmem()] * tensor,
-            out_specs=[vmem()] * 2,
+            out_specs=[vmem()] * (count + 1),
             compiler_params=params(),
             cost_estimate=cost(1e6, 3e6),
             name="sum_parts",
@@ -525,9 +537,9 @@
     half = own_slots // 2
 
     blocks = [[value] for value in tensor_cross([own_block] * tensor, 1)]
-    latent, enc_y = finish(tensor_cross(layer(0, blocks), 0))
-
-    passed = lax.ppermute(latent, "section", swap)
+    top, bottom, enc_y = finish(tensor_cross(layer(0, blocks), 0), 2)
+
+    passed = lax.ppermute(bottom, "section", swap)
     mine = pl.pallas_call(
         half_kernel,
         out_shape=shape((half, width), BF16),
@@ -536,32 +548,27 @@
         compiler_params=params(),
         cost_estimate=cost(1e5, 5e5),
         name="own_half",
-    )(pos, latent, passed)
+    )(pos, top, passed)
     gathered = tensor_gather(mine)
     enc_y, gathered[0] = barrier((enc_y, gathered[0]))
     enc_terms = gradient_terms(1, [enc_y], cot_other, pieces)
     enc_terms, gathered = barrier((enc_terms, gathered))
     swapped = [lax.ppermute(value, "section", swap) for value in gathered]
-    sources = [[latent]] + [[top, bottom] for top, bottom in zip(gathered, swapped)]
-    kept = [[passed]] + [[top, bottom] for top, bottom in zip(swapped, gathered)]
-
-    enc_grad, order = [], list(range(dp_count))[::-1] if direct else []
-
-    def send_gradient(count):
-        for k in order[:count]:
-            enc_grad.extend(dp_cross([enc_terms[k]], 1, k))
-        del order[:count]
+    sources = [[top, bottom]] + [list(pair) for pair in zip(gathered, swapped)]
+    kept = [list(pair) for pair in zip(swapped, gathered)]
 
     sources, enc_terms = barrier((sources, enc_terms))
-    send_gradient(1)
-    parts = layer(1, sources)
-    parts, enc_grad, enc_terms = barrier((parts, enc_grad, enc_terms))
+    first = [k for k in range(dp_count) if k != dp_count // 2] if direct else []
+    enc_grad = [dp_cross([enc_terms[k]], 1, k)[0] for k in first]
+    parts, enc_grad, enc_terms = barrier((layer(1, sources), enc_grad, enc_terms))
+    if direct:
+        enc_grad = enc_grad + dp_cross([enc_terms[dp_count // 2]], 1, dp_count // 2)
     arrived = tensor_cross(parts, 1)
-    send_gradient(1)
-    arrived, enc_grad, enc_terms = barrier((arrived, enc_grad, enc_terms))
-    send_gradient(dp_count)
-    rebuilt, dec_y = finish(arrived)
+    top, arrived = barrier((top, arrived))
+    kept = [[lax.ppermute(top, "section", swap), passed]] + kept
+    rebuilt, dec_y = finish(arrived, 1)
     dec_terms = gradient_terms(0, [dec_y], cot_other, pieces)
+    dec_terms, enc_grad = barrier((dec_terms, enc_grad))
     if direct:
         dec_grad = dp_cross(dec_terms, 0, 0)
     else:
@@ -574,7 +581,9 @@
             for terms in (enc_terms, dec_terms)
         ]
     rebuilt, dec_terms = barrier((rebuilt, dec_terms))
-    finals = [[value] for value in tensor_cross([rebuilt] * tensor, 0)]
+    finals = tensor_cross([rebuilt] * 2, 0)
+    rebuilt, finals[0] = barrier((rebuilt, finals[0]))
+    finals = [[value] for value in finals + tensor_cross([rebuilt] * (tensor - 2), 0, 2)]
 
     groups = kept + finals
     counts = tuple(len(group) for group in groups)

time: 147 us -> 147 us (level)
  waiting for transfers between devices: 72.4 us -> 64.3 us
  starting transfers between devices: 41.1 us -> 48.6 us
    ppermute x11, waiting for transfers between devices: 32 us -> 22.3 us  [dp_cross(): lax.ppermute(value, ('dp', 'section'), [(d * 2 + active, (d ^ k) * 2 + ot...]
    ppermute x16, starting transfers between devices: 22.9 us -> 29.2 us  [tensor_cross(): lax.ppermute(value, ('section', 'tensor'), [(active * count + t, other *...]
    ppermute x1 -> x2, starting transfers between devices: 0.07 us -> 5.41 us  [the longest x1 5.33 us: per_device(): kept = [[lax.ppermute(top, 'section', swap), passed]] + kept]
    ppermute x11, starting transfers between devices: 12.9 us -> 8.87 us  [dp_cross(): lax.ppermute(value, ('dp', 'section'), [(d * 2 + active, (d ^ k) * 2 + ot...]
    ppermute x16, waiting for transfers between devices: 27.3 us -> 29.4 us  [tensor_cross(): lax.ppermute(value, ('section', 'tensor'), [(active * count + t, other *...]
  transfers between devices with their start and end apart: 35 -> 36, of which waited for: 19 -> 20; matrix products, arithmetic and copies ran while one was open for 2% -> 2% of each run, Pallas kernels for 12% -> 13%
where the time goes in v3:
time: 147 us; the launch traced here: 146 us
  waiting for transfers between devices  64.3 us (44%)
  starting transfers between devices  48.6 us (33%)
  Pallas kernels  26.5 us (18%)
  local copies, waits for them, and re-layouts  5.63 us (4%)
    ppermute x16, waiting for transfers between devices, tensor_cross(): lax.ppermute(value, ('section', 'tensor'), [(active * count + t, other *...  29.4 us
    ppermute x16, starting transfers between devices, tensor_cross(): lax.ppermute(value, ('section', 'tensor'), [(active * count + t, other *...  29.2 us
    ppermute x11, waiting for transfers between devices, dp_cross(): lax.ppermute(value, ('dp', 'section'), [(d * 2 + active, (d ^ k) * 2 + ot...  22.3 us
    pallas_call x2, Pallas kernels, layer(): pl.pallas_call(functools.partial(layer_kernel, active, counts, band), out...  15.1 us
    ppermute x3, waiting for transfers between devices, tensor_gather(): lax.ppermute(value, 'tensor', [(t, t ^ k) for t in range(count)])  9.69 us
    ppermute x11, starting transfers between devices, dp_cross(): lax.ppermute(value, ('dp', 'section'), [(d * 2 + active, (d ^ k) * 2 + ot...  8.87 us
    ppermute x1, starting transfers between devices, per_device(): kept = [[lax.ppermute(top, 'section', swap), passed]] + kept  5.33 us
    unnamed x19, local copies, waits for them, and re-layouts  4.32 us
  transfers between devices with their start and end apart: 36, of which 20 were waited for; matrix products, arithmetic and copies ran while one was open for 2% of the time, Pallas kernels for 13%

profile of v3, /device:TPU:9, one launch (start us, length us, event | category | flops | bytes accessed | tf_op | source)
XLA Modules:
  0.0 146.2 jit_solution(3671062571887032005)
XLA Ops:
  0.7 0.7 collective-permute-start.3
  1.5 1.2 copy-done
  2.7 0.7 copy-done.1
  3.4 0.7 copy-done.2
  4.0 1.1 select_rows.1
  5.3 2.7 %collective-permute-start.2 = (bf16[128,512]{1,0:T(8,128)(2,1)S(1)}, bf16[128,512]{1,0:T(8,128)(2,1)S(1)}, u32[]{:S(2)}, u32[]{:S(2)}) collective-permute-start(bf16[128,512]{1,0:T(8,128)(2,1)S(1)} %get-tuple-element.82), channel_id=1, source_target_pairs={{0,28},{8,20},{16,12},{24,4},{4,0},{12,8},{20,16},{28,24},{1,29},{... | collective-permute-start | bytes 393224 | tf_op jit(solution)/shard_map/ppermute | solution.py:389
  7.9 1.6 %collective-permute-done.refs_1_ = bf16[128,512]{1,0:T(8,128)(2,1)S(1)} collective-permute-done((bf16[128,512]{1,0:T(8,128)(2,1)S(1)}, bf16[128,512]{1,0:T(8,128)(2,1)S(1)}, u32[]{:S(2)}, u32[]{:S(2)}) %collective-permute-start) | collective-permute-done | bytes 131104 | tf_op jit(solution)/shard_map/ppermute | solution.py:389
  9.6 2.5 %collective-permute-done.1.refs_2_ = bf16[128,512]{1,0:T(8,128)(2,1)S(1)} collective-permute-done((bf16[128,512]{1,0:T(8,128)(2,1)S(1)}, bf16[128,512]{1,0:T(8,128)(2,1)S(1)}, u32[]{:S(2)}, u32[]{:S(2)}) %collective-permute-start.1) | collective-permute-done | bytes 131104 | tf_op jit(solution)/shard_map/ppermute | solution.py:389
  12.1 2.8 %collective-permute-done.2.refs_3_ = bf16[128,512]{1,0:T(8,128)(2,1)S(1)} collective-permute-done((bf16[128,512]{1,0:T(8,128)(2,1)S(1)}, bf16[128,512]{1,0:T(8,128)(2,1)S(1)}, u32[]{:S(2)}, u32[]{:S(2)}) %collective-permute-start.2) | collective-permute-done | bytes 131104 | tf_op jit(solution)/shard_map/ppermute | solution.py:389
  14.9 2.2 %place_rows.1 = (bf16[512,512]{1,0:T(8,128)(2,1)}, s32[512,128]{1,0:T(8,128)S(1)}) custom-call(s32[3]{0:T(128)S(1)} %pad_add_fusion.pos_ref, s32[16]{0:T(128)S(1)} %copy-done.1, s32[16]{0:T(128)S(1)} %copy-done.2, bf16[128,512]{1,0:T(8,128)(2,1)S(1)} %get-tuple-element.83.refs_0_, bf16[128,512]{1,0:T(8,128)(2,1)S(1)} %collective-permute-done.refs_1_, ...), custom_call_target="tpu_custom_call" | custom-call | tf_op jit(solution)/shard_map/place_rows/pallas_call | solution.py:451
  17.1 1.6 %collective-permute-start.5 = (bf16[512,512]{1,0:T(8,128)(2,1)}, bf16[512,512]{1,0:T(8,128)(2,1)}, u32[]{:S(2)}, u32[]{:S(2)}) collective-permute-start(bf16[512,512]{1,0:T(8,128)(2,1)} %get-tuple-element.87), channel_id=1, source_target_pairs={{4,1},{5,0},{6,3},{7,2},{0,4},{1,5},{2,6},{3,7},{12,9},{13,8},{14,... | collective-permute-start | bytes 1572872 | tf_op jit(solution)/shard_map/ppermute | solution.py:375
  18.7 1.6 %collective-permute-start.7 = (bf16[512,512]{1,0:T(8,128)(2,1)}, bf16[512,512]{1,0:T(8,128)(2,1)}, u32[]{:S(2)}, u32[]{:S(2)}) collective-permute-start(bf16[512,512]{1,0:T(8,128)(2,1)} %get-tuple-element.87), channel_id=1, source_target_pairs={{4,3},{5,2},{6,1},{7,0},{0,4},{1,5},{2,6},{3,7},{12,11},{13,10},{1... | collective-permute-start | bytes 1572872 | tf_op jit(solution)/shard_map/ppermute | solution.py:375
  20.3 1.8 %copy.16 = bf16[1,2048,8]{2,1,0:T(8,128)(2,1)} copy(bf16[1,2048,8]{1,2,0:T(8,128)(2,1)} %param.22) | data formatting | bytes 65536 | tf_op args[8]
  22.2 1.1 pad.11.refs_9_.refs_13_
  23.4 1.7 %collective-permute-done.5.refs_1_ = bf16[512,512]{1,0:T(8,128)(2,1)} collective-permute-done((bf16[512,512]{1,0:T(8,128)(2,1)}, bf16[512,512]{1,0:T(8,128)(2,1)}, u32[]{:S(2)}, u32[]{:S(2)}) %collective-permute-start.5) | collective-permute-done | bytes 524320 | tf_op jit(solution)/shard_map/ppermute | solution.py:375
  25.2 5.6 %collective-permute-done.7.refs_3_ = bf16[512,512]{1,0:T(8,128)(2,1)} collective-permute-done((bf16[512,512]{1,0:T(8,128)(2,1)}, bf16[512,512]{1,0:T(8,128)(2,1)}, u32[]{:S(2)}, u32[]{:S(2)}) %collective-permute-start.7) | collective-permute-done | bytes 524320 | tf_op jit(solution)/shard_map/ppermute | solution.py:375
  30.8 2.7 %layer_part.2 = (bf16[1552,512]{1,0:T(8,128)(2,1)}, bf16[528,512]{1,0:T(8,128)(2,1)S(1)}, bf16[528,512]{1,0:T(8,128)(2,1)S(1)}, bf16[528,512]{1,0:T(8,128)(2,1)S(1)}) custom-call(s32[3]{0:T(128)S(1)} %pad_add_fusion.pos_ref, bf16[512,512]{1,0:T(8,128)(2,1)} %collective-permute-done.4.refs_0_, bf16[512,512]{1,0:T(8,128)(2,1)} %collective-permute-done.5.refs_1_, ...), custom_call_target="tpu_custom_call" | custom-call | flops 4294967296 | bytes 12000000 | tf_op jit(solution)/shard_map/layer_part/pallas_call | solution.py:486
  33.5 13.1 %collective-permute-start.8 = (bf16[1552,512]{1,0:T(8,128)(2,1)}, bf16[1552,512]{1,0:T(8,128)(2,1)S(1)}, u32[]{:S(2)}, u32[]{:S(2)}) collective-permute-start(bf16[1552,512]{1,0:T(8,128)(2,1)} %get-tuple-element.89), channel_id=1, source_target_pairs={{0,4},{1,5},{2,6},{3,7},{4,0},{5,1},{6,2},{7,3},{8,12},{9,13},{10,... | collective-permute-start | bytes 4767752 | tf_op jit(solution)/shard_map/ppermute | solution.py:375
  47.2 1.0 collective-permute-start.9
  48.2 13.0 %collective-permute-done.10.refs_2_ = bf16[528,512]{1,0:T(8,128)(2,1)S(1)} collective-permute-done((bf16[528,512]{1,0:T(8,128)(2,1)S(1)}, bf16[528,512]{1,0:T(8,128)(2,1)S(1)}, u32[]{:S(2)}, u32[]{:S(2)}) %collective-permute-start.10) | collective-permute-done | bytes 540704 | tf_op jit(solution)/shard_map/ppermute | solution.py:375
  61.2 0.7 sum_parts.2
  62.1 1.5 %collective-permute-done.12.other_ref.refs_1_ = bf16[256,512]{1,0:T(8,128)(2,1)S(1)} collective-permute-done((bf16[256,512]{1,0:T(8,128)(2,1)S(1)}, bf16[256,512]{1,0:T(8,128)(2,1)S(1)}, u32[]{:S(2)}, u32[]{:S(2)}) %collective-permute-start.12) | collective-permute-done | bytes 262176 | tf_op jit(solution)/shard_map/ppermute | solution.py:542
  64.2 1.3 collective-permute-start.13
  65.4 1.2 collective-permute-start.14
  66.9 5.1 %collective-permute-done.13.refs_2_.refs_3_ = bf16[256,512]{1,0:T(8,128)(2,1)S(1)} collective-permute-done((bf16[256,512]{1,0:T(8,128)(2,1)S(1)}, bf16[256,512]{1,0:T(8,128)(2,1)S(1)}, u32[]{:S(2)}, u32[]{:S(2)}) %collective-permute-start.13) | collective-permute-done | bytes 262176 | tf_op jit(solution)/shard_map/ppermute | solution.py:367
  72.0 2.0 %gradient_terms.2 = (bf16[512,512]{1,0:T(8,128)(2,1)S(1)}, bf16[512,512]{1,0:T(8,128)(2,1)S(1)}, bf16[512,512]{1,0:T(8,128)(2,1)S(1)}, bf16[512,512]{1,0:T(8,128)(2,1)S(1)}) custom-call(s32[3]{0:T(128)S(1)} %pad_add_fusion.pos_ref, bf16[512,512]{1,0:T(8,128)(2,1)S(1)} %get-tuple-element.96.refs_0_, bf16[512,2048]{1,0:T(8,128)(2,1)S(1)} %collective-permute-done.3.refs_1_), custom_call_target="tpu_custom_call" | custom-call | flops 1073741824 | bytes 5000000 | tf_op jit(solution)/shard_map/gradient_terms/pallas_call | solution.py:525
  74.0 4.6 %collective-permute-done.15.refs_6_.refs_7_ = bf16[256,512]{1,0:T(8,128)(2,1)S(1)} collective-permute-done((bf16[256,512]{1,0:T(8,128)(2,1)S(1)}, bf16[256,512]{1,0:T(8,128)(2,1)S(1)}, u32[]{:S(2)}, u32[]{:S(2)}) %collective-permute-start.15) | collective-permute-done | bytes 262176 | tf_op jit(solution)/shard_map/ppermute | solution.py:367
  78.6 1.2 collective-permute-start.16
  80.3 0.7 collective-permute-done.16.refs_3_.refs_2_
  82.1 1.6 %collective-permute-start.21 = (bf16[512,512]{1,0:T(8,128)(2,1)S(1)}, bf16[512,512]{1,0:T(8,128)(2,1)S(1)}, u32[]{:S(2)}, u32[]{:S(2)}) collective-permute-start(bf16[512,512]{1,0:T(8,128)(2,1)S(1)} %get-tuple-element.124), channel_id=1, source_target_pairs={{4,24},{12,16},{20,8},{28,0},{0,4},{8,12},{16,20},{24,28},{5,25},{... | collective-permute-start | bytes 1572872 | tf_op jit(solution)/shard_map/ppermute | solution.py:389
  83.7 12.4 %layer_part.3 = (bf16[1552,512]{1,0:T(8,128)(2,1)}, bf16[528,512]{1,0:T(8,128)(2,1)S(1)}, bf16[528,512]{1,0:T(8,128)(2,1)S(1)}, bf16[528,512]{1,0:T(8,128)(2,1)S(1)}) custom-call(s32[3]{0:T(128)S(1)} %pad_add_fusion.pos_ref, bf16[256,512]{1,0:T(8,128)(2,1)S(1)} %get-tuple-element.130.own_ref.refs_0_, bf16[256,512]{1,0:T(8,128)(2,1)S(1)} %get-tuple-element.111.refs_1_, ...), custom_call_target="tpu_custom_call" | custom-call | flops 4294967296 | bytes 12000000 | tf_op jit(solution)/shard_map/layer_part/pallas_call | solution.py:486
  96.2 1.3 collective-permute-start.23
  97.8 1.5 %collective-permute-start.25 = (bf16[528,512]{1,0:T(8,128)(2,1)S(1)}, bf16[528,512]{1,0:T(8,128)(2,1)S(1)}, u32[]{:S(2)}, u32[]{:S(2)}) collective-permute-start(bf16[528,512]{1,0:T(8,128)(2,1)S(1)} %get-tuple-element.129), channel_id=1, source_target_pairs={{4,3},{5,2},{6,1},{7,0},{0,4},{1,5},{2,6},{3,7},{12,11},{13,10},{1... | collective-permute-start | bytes 1622024 | tf_op jit(solution)/shard_map/ppermute | solution.py:375
  99.4 1.2 collective-permute-start.27
  100.6 3.2 %collective-permute-done.23.refs_1_ = bf16[528,512]{1,0:T(8,128)(2,1)S(1)} collective-permute-done((bf16[528,512]{1,0:T(8,128)(2,1)S(1)}, bf16[528,512]{1,0:T(8,128)(2,1)S(1)}, u32[]{:S(2)}, u32[]{:S(2)}) %collective-permute-start.23) | collective-permute-done | bytes 540704 | tf_op jit(solution)/shard_map/ppermute | solution.py:375
  104.1 5.4 %collective-permute-done.25.refs_3_ = bf16[528,512]{1,0:T(8,128)(2,1)S(1)} collective-permute-done((bf16[528,512]{1,0:T(8,128)(2,1)S(1)}, bf16[528,512]{1,0:T(8,128)(2,1)S(1)}, u32[]{:S(2)}, u32[]{:S(2)}) %collective-permute-start.25) | collective-permute-done | bytes 540704 | tf_op jit(solution)/shard_map/ppermute | solution.py:375
  109.6 0.7 sum_parts.3
  110.9 1.4 collective-permute-done.27.refs_3_
  112.3 2.5 %collective-permute-start.28 = (bf16[512,512]{1,0:T(8,128)(2,1)S(1)}, bf16[512,512]{1,0:T(8,128)(2,1)S(1)}, u32[]{:S(2)}, u32[]{:S(2)}) collective-permute-start(bf16[512,512]{1,0:T(8,128)(2,1)S(1)} %get-tuple-element.151), channel_id=1, source_target_pairs={{0,4},{1,5},{2,6},{3,7},{4,0},{5,1},{6,2},{7,3},{8,12},{9,13},{10,... | collective-permute-start | bytes 1572872 | tf_op jit(solution)/shard_map/ppermute | solution.py:375
  115.4 1.8 %collective-permute-start.34 = (bf16[512,512]{1,0:T(8,128)(2,1)S(1)}, bf16[512,512]{1,0:T(8,128)(2,1)S(1)}, u32[]{:S(2)}, u32[]{:S(2)}) collective-permute-start(bf16[512,512]{1,0:T(8,128)(2,1)S(1)} %get-tuple-element.147), channel_id=1, source_target_pairs={{0,20},{8,28},{16,4},{24,12},{4,0},{12,8},{20,16},{28,24},{1,21},{... | collective-permute-start | bytes 1572872 | tf_op jit(solution)/shard_map/ppermute | solution.py:389
  117.9 0.6 collective-permute-start.30
  118.6 5.4 %collective-permute-done.33.refs_5_ = bf16[512,512]{1,0:T(8,128)(2,1)S(1)} collective-permute-done((bf16[512,512]{1,0:T(8,128)(2,1)S(1)}, bf16[512,512]{1,0:T(8,128)(2,1)S(1)}, u32[]{:S(2)}, u32[]{:S(2)}) %collective-permute-start.33) | collective-permute-done | bytes 524320 | tf_op jit(solution)/shard_map/ppermute | solution.py:389
  124.0 4.6 %collective-permute-start.31 = (bf16[512,512]{1,0:T(8,128)(2,1)S(1)}, bf16[512,512]{1,0:T(8,128)(2,1)S(1)}, u32[]{:S(2)}, u32[]{:S(2)}) collective-permute-start(bf16[512,512]{1,0:T(8,128)(2,1)S(1)} %get-tuple-element.151), channel_id=1, source_target_pairs={{0,7},{1,6},{2,5},{3,4},{4,0},{5,1},{6,2},{7,3},{8,15},{9,14},{10,... | collective-permute-start | bytes 1572872 | tf_op jit(solution)/shard_map/ppermute | solution.py:375
  128.6 1.7 %collective-permute-done.34.refs_6_ = bf16[512,512]{1,0:T(8,128)(2,1)S(1)} collective-permute-done((bf16[512,512]{1,0:T(8,128)(2,1)S(1)}, bf16[512,512]{1,0:T(8,128)(2,1)S(1)}, u32[]{:S(2)}, u32[]{:S(2)}) %collective-permute-start.34) | collective-permute-done | bytes 524320 | tf_op jit(solution)/shard_map/ppermute | solution.py:389
  130.3 5.3 %collective-permute-start.26 = (bf16[256,512]{1,0:T(8,128)(2,1)S(1)}, bf16[256,512]{1,0:T(8,128)(2,1)S(1)}, u32[]{:S(2)}, u32[]{:S(2)}) collective-permute-start(bf16[256,512]{1,0:T(8,128)(2,1)S(1)} %get-tuple-element.130.own_ref.refs_0_), channel_id=1, source_target_pairs={{0,4},{4,0},{1,5},{5,1},{2,6},{6,2},{3,7},{7,3},{8,12},{12,8},{9,1... | collective-permute-start | bytes 786440 | tf_op jit(solution)/shard_map/ppermute | solution.py:568
  135.7 6.8 %collective-permute-done.35.refs_7_ = bf16[512,512]{1,0:T(8,128)(2,1)S(1)} collective-permute-done((bf16[512,512]{1,0:T(8,128)(2,1)S(1)}, bf16[512,512]{1,0:T(8,128)(2,1)S(1)}, u32[]{:S(2)}, u32[]{:S(2)}) %collective-permute-start.35) | collective-permute-done | bytes 524320 | tf_op jit(solution)/shard_map/ppermute | solution.py:389
  142.5 1.6 %gradient_total.1 = bf16[1,512,512]{2,1,0:T(8,128)(2,1)} custom-call(s32[3]{0:T(128)S(1)} %pad_add_fusion.pos_ref, bf16[512,512]{1,0:T(8,128)(2,1)S(1)} %collective-permute-done.19.refs_0_, bf16[512,512]{1,0:T(8,128)(2,1)S(1)} %collective-permute-done.20.refs_1_, bf16[512,512]{1,0:T(8,128)(2,1)S(1)} %collective-permute-done.21.refs_2_, ...), custom_call_target="tpu_custom_call" | custom-call | flops 1000000 | bytes 4000000 | tf_op jit(solution)/shard_map/gradient_total/pallas_call | solution.py:600
  144.1 2.0 %assemble_rows.1 = bf16[1,512,2048]{2,1,0:T(8,128)(2,1)} custom-call(s32[3]{0:T(128)S(1)} %pad_add_fusion.pos_ref, bf16[256,512]{1,0:T(8,128)(2,1)S(1)} %collective-permute-done.26.refs_0_, bf16[256,512]{1,0:T(8,128)(2,1)S(1)} %collective-permute-done.12.other_ref.refs_1_, bf16[256,512]{1,0:T(8,128)(2,1)S(1)} %collective-permute-done.16.refs_3_.refs_2_, ...), custom_call_target="tpu_custom_call" | custom-call | flops 1000000 | bytes 4000000 | tf_op jit(solution)/shard_map/assemble_rows/pallas_call | solution.py:590
  (60 shorter events, 6.3 us)
Async XLA Ops:
  0.6 21.4 %copy-start.6 = (f32[1,8]{1,0:T(1,128)S(1)}, f32[1,8]{1,0:T(1,128)}, u32[]{:S(2)}) copy-start(f32[1,8]{1,0:T(1,128)} %param.25) | copy-start | bytes 100
  0.6 21.6 %copy-start.7 = (f32[1,8]{1,0:T(1,128)S(1)}, f32[1,8]{1,0:T(1,128)}, u32[]{:S(2)}) copy-start(f32[1,8]{1,0:T(1,128)} %param.23) | copy-start | bytes 100
  0.7 21.6 %copy-start.8 = (f32[1,8]{1,0:T(1,128)S(1)}, f32[1,8]{1,0:T(1,128)}, u32[]{:S(2)}) copy-start(f32[1,8]{1,0:T(1,128)} %param.24) | copy-start | bytes 100
  0.7 30.1 %copy-start.4 = (f32[1,2048]{1,0:T(1,128)S(1)}, f32[1,2048]{1,0:T(1,128)}, u32[]{:S(2)}) copy-start(f32[1,2048]{1,0:T(1,128)} %refs_9_.1) | copy-start | bytes 24580
  0.7 30.1 %copy-start.5 = (f32[1,512]{1,0:T(1,128)S(1)}, f32[1,512]{1,0:T(1,128)}, u32[]{:S(2)}) copy-start(f32[1,512]{1,0:T(1,128)} %refs_17_.1) | copy-start | bytes 6148
  0.7 14.2 %collective-permute-start.3 = (bf16[512,2048]{1,0:T(8,128)(2,1)}, bf16[512,2048]{1,0:T(8,128)(2,1)S(1)}, u32[]{:S(2)}, u32[]{:S(2)}) collective-permute-start(bf16[512,2048]{1,0:T(8,128)(2,1)} %bitcast.14), channel_id=1, source_target_pairs={{0,4},{4,0},{1,5},{5,1},{2,6},{6,2},{3,7},{7,3},{8,12},{12,8},{9,1... | collective-permute-start | bytes 6291464 | tf_op jit(solution)/shard_map/ppermute | solution.py:448
  1.5 1.2 copy-start
  2.7 0.7 copy-start.1
  3.4 0.7 copy-start.2
  4.0 26.7 %copy-start.3 = (bf16[1,2048,256]{2,1,0:T(8,128)(2,1)S(1)}, bf16[1,2048,256]{2,1,0:T(8,128)(2,1)}, u32[]{:S(2)}) copy-start(bf16[1,2048,256]{2,1,0:T(8,128)(2,1)} %param.21) | copy-start | bytes 3145732
  5.1 4.4 %collective-permute-start = (bf16[128,512]{1,0:T(8,128)(2,1)S(1)}, bf16[128,512]{1,0:T(8,128)(2,1)S(1)}, u32[]{:S(2)}, u32[]{:S(2)}) collective-permute-start(bf16[128,512]{1,0:T(8,128)(2,1)S(1)} %get-tuple-element.80), channel_id=1, source_target_pairs={{0,12},{8,4},{16,28},{24,20},{4,0},{12,8},{20,16},{28,24},{1,13},{... | collective-permute-start | bytes 393224 | tf_op jit(solution)/shard_map/ppermute | solution.py:389
  5.2 6.9 %collective-permute-start.1 = (bf16[128,512]{1,0:T(8,128)(2,1)S(1)}, bf16[128,512]{1,0:T(8,128)(2,1)S(1)}, u32[]{:S(2)}, u32[]{:S(2)}) collective-permute-start(bf16[128,512]{1,0:T(8,128)(2,1)S(1)} %get-tuple-element.81), channel_id=1, source_target_pairs={{0,20},{8,28},{16,4},{24,12},{4,0},{12,8},{20,16},{28,24},{1,21},{... | collective-permute-start | bytes 393224 | tf_op jit(solution)/shard_map/ppermute | solution.py:389
  5.3 9.6 %collective-permute-start.2 = (bf16[128,512]{1,0:T(8,128)(2,1)S(1)}, bf16[128,512]{1,0:T(8,128)(2,1)S(1)}, u32[]{:S(2)}, u32[]{:S(2)}) collective-permute-start(bf16[128,512]{1,0:T(8,128)(2,1)S(1)} %get-tuple-element.82), channel_id=1, source_target_pairs={{0,28},{8,20},{16,12},{24,4},{4,0},{12,8},{20,16},{28,24},{1,29},{... | collective-permute-start | bytes 393224 | tf_op jit(solution)/shard_map/ppermute | solution.py:389
  17.1 6.3 %collective-permute-start.4 = (bf16[512,512]{1,0:T(8,128)(2,1)}, bf16[512,512]{1,0:T(8,128)(2,1)}, u32[]{:S(2)}, u32[]{:S(2)}) collective-permute-start(bf16[512,512]{1,0:T(8,128)(2,1)} %get-tuple-element.87), channel_id=1, source_target_pairs={{4,0},{5,1},{6,2},{7,3},{0,4},{1,5},{2,6},{3,7},{12,8},{13,9},{14,... | collective-permute-start | bytes 1572872 | tf_op jit(solution)/shard_map/ppermute | solution.py:375
  17.1 8.0 %collective-permute-start.5 = (bf16[512,512]{1,0:T(8,128)(2,1)}, bf16[512,512]{1,0:T(8,128)(2,1)}, u32[]{:S(2)}, u32[]{:S(2)}) collective-permute-start(bf16[512,512]{1,0:T(8,128)(2,1)} %get-tuple-element.87), channel_id=1, source_target_pairs={{4,1},{5,0},{6,3},{7,2},{0,4},{1,5},{2,6},{3,7},{12,9},{13,8},{14,... | collective-permute-start | bytes 1572872 | tf_op jit(solution)/shard_map/ppermute | solution.py:375
  18.7 6.5 %collective-permute-start.6 = (bf16[512,512]{1,0:T(8,128)(2,1)}, bf16[512,512]{1,0:T(8,128)(2,1)}, u32[]{:S(2)}, u32[]{:S(2)}) collective-permute-start(bf16[512,512]{1,0:T(8,128)(2,1)} %get-tuple-element.87), channel_id=1, source_target_pairs={{4,2},{5,3},{6,0},{7,1},{0,4},{1,5},{2,6},{3,7},{12,10},{13,11},{1... | collective-permute-start | bytes 1572872 | tf_op jit(solution)/shard_map/ppermute | solution.py:375
  18.7 12.0 %collective-permute-start.7 = (bf16[512,512]{1,0:T(8,128)(2,1)}, bf16[512,512]{1,0:T(8,128)(2,1)}, u32[]{:S(2)}, u32[]{:S(2)}) collective-permute-start(bf16[512,512]{1,0:T(8,128)(2,1)} %get-tuple-element.87), channel_id=1, source_target_pairs={{4,3},{5,2},{6,1},{7,0},{0,4},{1,5},{2,6},{3,7},{12,11},{13,10},{1... | collective-permute-start | bytes 1572872 | tf_op jit(solution)/shard_map/ppermute | solution.py:375
  33.5 27.7 %collective-permute-start.8 = (bf16[1552,512]{1,0:T(8,128)(2,1)}, bf16[1552,512]{1,0:T(8,128)(2,1)S(1)}, u32[]{:S(2)}, u32[]{:S(2)}) collective-permute-start(bf16[1552,512]{1,0:T(8,128)(2,1)} %get-tuple-element.89), channel_id=1, source_target_pairs={{0,4},{1,5},{2,6},{3,7},{4,0},{5,1},{6,2},{7,3},{8,12},{9,13},{10,... | collective-permute-start | bytes 4767752 | tf_op jit(solution)/shard_map/ppermute | solution.py:375
  46.6 14.6 %collective-permute-start.10 = (bf16[528,512]{1,0:T(8,128)(2,1)S(1)}, bf16[528,512]{1,0:T(8,128)(2,1)S(1)}, u32[]{:S(2)}, u32[]{:S(2)}) collective-permute-start(bf16[528,512]{1,0:T(8,128)(2,1)S(1)} %get-tuple-element.91), channel_id=1, source_target_pairs={{0,6},{1,7},{2,4},{3,5},{4,0},{5,1},{6,2},{7,3},{8,14},{9,15},{10,... | collective-permute-start | bytes 1622024 | tf_op jit(solution)/shard_map/ppermute | solution.py:375
  46.7 14.5 %collective-permute-start.11 = (bf16[528,512]{1,0:T(8,128)(2,1)S(1)}, bf16[528,512]{1,0:T(8,128)(2,1)S(1)}, u32[]{:S(2)}, u32[]{:S(2)}) collective-permute-start(bf16[528,512]{1,0:T(8,128)(2,1)S(1)} %get-tuple-element.92), channel_id=1, source_target_pairs={{0,7},{1,6},{2,5},{3,4},{4,0},{5,1},{6,2},{7,3},{8,15},{9,14},{10,... | collective-permute-start | bytes 1622024 | tf_op jit(solution)/shard_map/ppermute | solution.py:375
  47.2 14.0 %collective-permute-start.9 = (bf16[528,512]{1,0:T(8,128)(2,1)S(1)}, bf16[528,512]{1,0:T(8,128)(2,1)S(1)}, u32[]{:S(2)}, u32[]{:S(2)}) collective-permute-start(bf16[528,512]{1,0:T(8,128)(2,1)S(1)} %get-tuple-element.90), channel_id=1, source_target_pairs={{0,5},{1,4},{2,7},{3,6},{4,0},{5,1},{6,2},{7,3},{8,13},{9,12},{10,... | collective-permute-start | bytes 1622024 | tf_op jit(solution)/shard_map/ppermute | solution.py:375
  62.0 1.6 %collective-permute-start.12 = (bf16[256,512]{1,0:T(8,128)(2,1)S(1)}, bf16[256,512]{1,0:T(8,128)(2,1)S(1)}, u32[]{:S(2)}, u32[]{:S(2)}) collective-permute-start(bf16[256,512]{1,0:T(8,128)(2,1)S(1)} %get-tuple-element.111.refs_1_), channel_id=1, source_target_pairs={{0,4},{4,0},{1,5},{5,1},{2,6},{6,2},{3,7},{7,3},{8,12},{12,8},{9,1... | collective-permute-start | bytes 786440 | tf_op jit(solution)/shard_map/ppermute | solution.py:542
  64.2 7.8 %collective-permute-start.13 = (bf16[256,512]{1,0:T(8,128)(2,1)S(1)}, bf16[256,512]{1,0:T(8,128)(2,1)S(1)}, u32[]{:S(2)}, u32[]{:S(2)}) collective-permute-start(bf16[256,512]{1,0:T(8,128)(2,1)S(1)} %own_half.1), channel_id=1, source_target_pairs={{0,1},{1,0},{2,3},{3,2},{4,5},{5,4},{6,7},{7,6},{8,9},{9,8},{10,11... | collective-permute-start | bytes 786440 | tf_op jit(solution)/shard_map/ppermute | solution.py:367
  65.4 8.6 %collective-permute-start.14 = (bf16[256,512]{1,0:T(8,128)(2,1)S(1)}, bf16[256,512]{1,0:T(8,128)(2,1)S(1)}, u32[]{:S(2)}, u32[]{:S(2)}) collective-permute-start(bf16[256,512]{1,0:T(8,128)(2,1)S(1)} %own_half.1), channel_id=1, source_target_pairs={{0,2},{1,3},{2,0},{3,1},{4,6},{5,7},{6,4},{7,5},{8,10},{9,11},{10,... | collective-permute-start | bytes 786440 | tf_op jit(solution)/shard_map/ppermute | solution.py:367
  66.6 12.0 %collective-permute-start.15 = (bf16[256,512]{1,0:T(8,128)(2,1)S(1)}, bf16[256,512]{1,0:T(8,128)(2,1)S(1)}, u32[]{:S(2)}, u32[]{:S(2)}) collective-permute-start(bf16[256,512]{1,0:T(8,128)(2,1)S(1)} %own_half.1), channel_id=1, source_target_pairs={{0,3},{1,2},{2,1},{3,0},{4,7},{5,6},{6,5},{7,4},{8,11},{9,10},{10,... | collective-permute-start | bytes 786440 | tf_op jit(solution)/shard_map/ppermute | solution.py:367
  78.6 2.3 %collective-permute-start.16 = (bf16[256,512]{1,0:T(8,128)(2,1)S(1)}, bf16[256,512]{1,0:T(8,128)(2,1)S(1)}, u32[]{:S(2)}, u32[]{:S(2)}) collective-permute-start(bf16[256,512]{1,0:T(8,128)(2,1)S(1)} %collective-permute-done.13.refs_2_.refs_3_), channel_id=1, source_target_pairs={{0,4},{4,0},{1,5},{5,1},{2,6},{6,2},{3,7},{7,3},{8,12},{12,8},{9,1... | collective-permute-start | bytes 786440 | tf_op jit(solution)/shard_map/ppermute | solution.py:556
  79.8 1.5 %collective-permute-start.17 = (bf16[256,512]{1,0:T(8,128)(2,1)S(1)}, bf16[256,512]{1,0:T(8,128)(2,1)S(1)}, u32[]{:S(2)}, u32[]{:S(2)}) collective-permute-start(bf16[256,512]{1,0:T(8,128)(2,1)S(1)} %collective-permute-done.14.refs_4_.refs_5_), channel_id=1, source_target_pairs={{0,4},{4,0},{1,5},{5,1},{2,6},{6,2},{3,7},{7,3},{8,12},{12,8},{9,1... | collective-permute-start | bytes 786440 | tf_op jit(solution)/shard_map/ppermute | solution.py:556
  79.8 1.9 %collective-permute-start.18 = (bf16[256,512]{1,0:T(8,128)(2,1)S(1)}, bf16[256,512]{1,0:T(8,128)(2,1)S(1)}, u32[]{:S(2)}, u32[]{:S(2)}) collective-permute-start(bf16[256,512]{1,0:T(8,128)(2,1)S(1)} %collective-permute-done.15.refs_6_.refs_7_), channel_id=1, source_target_pairs={{0,4},{4,0},{1,5},{5,1},{2,6},{6,2},{3,7},{7,3},{8,12},{12,8},{9,1... | collective-permute-start | bytes 786440 | tf_op jit(solution)/shard_map/ppermute | solution.py:556
  81.7 14.4 %collective-permute-start.19 = (bf16[512,512]{1,0:T(8,128)(2,1)S(1)}, bf16[512,512]{1,0:T(8,128)(2,1)S(1)}, u32[]{:S(2)}, u32[]{:S(2)}) collective-permute-start(bf16[512,512]{1,0:T(8,128)(2,1)S(1)} %get-tuple-element.122), channel_id=1, source_target_pairs={{4,0},{12,8},{20,16},{28,24},{0,4},{8,12},{16,20},{24,28},{5,1},{1... | collective-permute-start | bytes 1572872 | tf_op jit(solution)/shard_map/ppermute | solution.py:389
  82.1 14.1 %collective-permute-start.20 = (bf16[512,512]{1,0:T(8,128)(2,1)S(1)}, bf16[512,512]{1,0:T(8,128)(2,1)S(1)}, u32[]{:S(2)}, u32[]{:S(2)}) collective-permute-start(bf16[512,512]{1,0:T(8,128)(2,1)S(1)} %get-tuple-element.123), channel_id=1, source_target_pairs={{4,8},{12,0},{20,24},{28,16},{0,4},{8,12},{16,20},{24,28},{5,9},{1... | collective-permute-start | bytes 1572872 | tf_op jit(solution)/shard_map/ppermute | solution.py:389
  82.1 14.1 %collective-permute-start.21 = (bf16[512,512]{1,0:T(8,128)(2,1)S(1)}, bf16[512,512]{1,0:T(8,128)(2,1)S(1)}, u32[]{:S(2)}, u32[]{:S(2)}) collective-permute-start(bf16[512,512]{1,0:T(8,128)(2,1)S(1)} %get-tuple-element.124), channel_id=1, source_target_pairs={{4,24},{12,16},{20,8},{28,0},{0,4},{8,12},{16,20},{24,28},{5,25},{... | collective-permute-start | bytes 1572872 | tf_op jit(solution)/shard_map/ppermute | solution.py:389
  96.1 13.5 %collective-permute-start.22 = (bf16[1552,512]{1,0:T(8,128)(2,1)}, bf16[1552,512]{1,0:T(8,128)(2,1)S(1)}, u32[]{:S(2)}, u32[]{:S(2)}) collective-permute-start(bf16[1552,512]{1,0:T(8,128)(2,1)} %get-tuple-element.126), channel_id=1, source_target_pairs={{4,0},{5,1},{6,2},{7,3},{0,4},{1,5},{2,6},{3,7},{12,8},{13,9},{14,... | collective-permute-start | bytes 4767752 | tf_op jit(solution)/shard_map/ppermute | solution.py:375
  96.2 7.6 %collective-permute-start.23 = (bf16[528,512]{1,0:T(8,128)(2,1)S(1)}, bf16[528,512]{1,0:T(8,128)(2,1)S(1)}, u32[]{:S(2)}, u32[]{:S(2)}) collective-permute-start(bf16[528,512]{1,0:T(8,128)(2,1)S(1)} %get-tuple-element.127), channel_id=1, source_target_pairs={{4,1},{5,0},{6,3},{7,2},{0,4},{1,5},{2,6},{3,7},{12,9},{13,8},{14,... | collective-permute-start | bytes 1622024 | tf_op jit(solution)/shard_map/ppermute | solution.py:375
  97.5 6.7 %collective-permute-start.24 = (bf16[528,512]{1,0:T(8,128)(2,1)S(1)}, bf16[528,512]{1,0:T(8,128)(2,1)S(1)}, u32[]{:S(2)}, u32[]{:S(2)}) collective-permute-start(bf16[528,512]{1,0:T(8,128)(2,1)S(1)} %get-tuple-element.128), channel_id=1, source_target_pairs={{4,2},{5,3},{6,0},{7,1},{0,4},{1,5},{2,6},{3,7},{12,10},{13,11},{1... | collective-permute-start | bytes 1622024 | tf_op jit(solution)/shard_map/ppermute | solution.py:375
  97.8 11.7 %collective-permute-start.25 = (bf16[528,512]{1,0:T(8,128)(2,1)S(1)}, bf16[528,512]{1,0:T(8,128)(2,1)S(1)}, u32[]{:S(2)}, u32[]{:S(2)}) collective-permute-start(bf16[528,512]{1,0:T(8,128)(2,1)S(1)} %get-tuple-element.129), channel_id=1, source_target_pairs={{4,3},{5,2},{6,1},{7,0},{0,4},{1,5},{2,6},{3,7},{12,11},{13,10},{1... | collective-permute-start | bytes 1622024 | tf_op jit(solution)/shard_map/ppermute | solution.py:375
  99.4 13.0 %collective-permute-start.27 = (bf16[512,512]{1,0:T(8,128)(2,1)S(1)}, bf16[512,512]{1,0:T(8,128)(2,1)S(1)}, u32[]{:S(2)}, u32[]{:S(2)}) collective-permute-start(bf16[512,512]{1,0:T(8,128)(2,1)S(1)} %get-tuple-element.144), channel_id=1, source_target_pairs={{4,16},{12,24},{20,0},{28,8},{0,4},{8,12},{16,20},{24,28},{5,17},{... | collective-permute-start | bytes 1572872 | tf_op jit(solution)/shard_map/ppermute | solution.py:389
  112.3 5.3 %collective-permute-start.28 = (bf16[512,512]{1,0:T(8,128)(2,1)S(1)}, bf16[512,512]{1,0:T(8,128)(2,1)S(1)}, u32[]{:S(2)}, u32[]{:S(2)}) collective-permute-start(bf16[512,512]{1,0:T(8,128)(2,1)S(1)} %get-tuple-element.151), channel_id=1, source_target_pairs={{0,4},{1,5},{2,6},{3,7},{4,0},{5,1},{6,2},{7,3},{8,12},{9,13},{10,... | collective-permute-start | bytes 1572872 | tf_op jit(solution)/shard_map/ppermute | solution.py:375
  114.9 3.1 %collective-permute-start.32 = (bf16[512,512]{1,0:T(8,128)(2,1)S(1)}, bf16[512,512]{1,0:T(8,128)(2,1)S(1)}, u32[]{:S(2)}, u32[]{:S(2)}) collective-permute-start(bf16[512,512]{1,0:T(8,128)(2,1)S(1)} %get-tuple-element.145), channel_id=1, source_target_pairs={{0,4},{8,12},{16,20},{24,28},{4,0},{12,8},{20,16},{28,24},{1,5},{9... | collective-permute-start | bytes 1572872 | tf_op jit(solution)/shard_map/ppermute | solution.py:389
  114.9 9.0 %collective-permute-start.33 = (bf16[512,512]{1,0:T(8,128)(2,1)S(1)}, bf16[512,512]{1,0:T(8,128)(2,1)S(1)}, u32[]{:S(2)}, u32[]{:S(2)}) collective-permute-start(bf16[512,512]{1,0:T(8,128)(2,1)S(1)} %get-tuple-element.146), channel_id=1, source_target_pairs={{0,12},{8,4},{16,28},{24,20},{4,0},{12,8},{20,16},{28,24},{1,13},{... | collective-permute-start | bytes 1572872 | tf_op jit(solution)/shard_map/ppermute | solution.py:389
  115.4 14.9 %collective-permute-start.34 = (bf16[512,512]{1,0:T(8,128)(2,1)S(1)}, bf16[512,512]{1,0:T(8,128)(2,1)S(1)}, u32[]{:S(2)}, u32[]{:S(2)}) collective-permute-start(bf16[512,512]{1,0:T(8,128)(2,1)S(1)} %get-tuple-element.147), channel_id=1, source_target_pairs={{0,20},{8,28},{16,4},{24,12},{4,0},{12,8},{20,16},{28,24},{1,21},{... | collective-permute-start | bytes 1572872 | tf_op jit(solution)/shard_map/ppermute | solution.py:389
  117.2 25.3 %collective-permute-start.35 = (bf16[512,512]{1,0:T(8,128)(2,1)S(1)}, bf16[512,512]{1,0:T(8,128)(2,1)S(1)}, u32[]{:S(2)}, u32[]{:S(2)}) collective-permute-start(bf16[512,512]{1,0:T(8,128)(2,1)S(1)} %get-tuple-element.148), channel_id=1, source_target_pairs={{0,28},{8,20},{16,12},{24,4},{4,0},{12,8},{20,16},{28,24},{1,29},{... | collective-permute-start | bytes 1572872 | tf_op jit(solution)/shard_map/ppermute | solution.py:389
  117.7 26.4 %collective-permute-start.29 = (bf16[512,512]{1,0:T(8,128)(2,1)S(1)}, bf16[512,512]{1,0:T(8,128)(2,1)S(1)}, u32[]{:S(2)}, u32[]{:S(2)}) collective-permute-start(bf16[512,512]{1,0:T(8,128)(2,1)S(1)} %get-tuple-element.151), channel_id=1, source_target_pairs={{0,5},{1,4},{2,7},{3,6},{4,0},{5,1},{6,2},{7,3},{8,13},{9,12},{10,... | collective-permute-start | bytes 1572872 | tf_op jit(solution)/shard_map/ppermute | solution.py:375
  117.9 26.2 %collective-permute-start.30 = (bf16[512,512]{1,0:T(8,128)(2,1)S(1)}, bf16[512,512]{1,0:T(8,128)(2,1)S(1)}, u32[]{:S(2)}, u32[]{:S(2)}) collective-permute-start(bf16[512,512]{1,0:T(8,128)(2,1)S(1)} %get-tuple-element.151), channel_id=1, source_target_pairs={{0,6},{1,7},{2,4},{3,5},{4,0},{5,1},{6,2},{7,3},{8,14},{9,15},{10,... | collective-permute-start | bytes 1572872 | tf_op jit(solution)/shard_map/ppermute | solution.py:375
  124.0 20.1 %collective-permute-start.31 = (bf16[512,512]{1,0:T(8,128)(2,1)S(1)}, bf16[512,512]{1,0:T(8,128)(2,1)S(1)}, u32[]{:S(2)}, u32[]{:S(2)}) collective-permute-start(bf16[512,512]{1,0:T(8,128)(2,1)S(1)} %get-tuple-element.151), channel_id=1, source_target_pairs={{0,7},{1,6},{2,5},{3,4},{4,0},{5,1},{6,2},{7,3},{8,15},{9,14},{10,... | collective-permute-start | bytes 1572872 | tf_op jit(solution)/shard_map/ppermute | solution.py:375
  130.3 13.8 %collective-permute-start.26 = (bf16[256,512]{1,0:T(8,128)(2,1)S(1)}, bf16[256,512]{1,0:T(8,128)(2,1)S(1)}, u32[]{:S(2)}, u32[]{:S(2)}) collective-permute-start(bf16[256,512]{1,0:T(8,128)(2,1)S(1)} %get-tuple-element.130.own_ref.refs_0_), channel_id=1, source_target_pairs={{0,4},{4,0},{1,5},{5,1},{2,6},{6,2},{3,7},{7,3},{8,12},{12,8},{9,1... | collective-permute-start | bytes 786440 | tf_op jit(solution)/shard_map/ppermute | solution.py:568

commit v4 on v3

--- a/solution.py
+++ b/solution.py
@@ -15,7 +15,7 @@
 LOG2E = 1.4426950408889634
 F32 = jnp.float32
 BF16 = jnp.bfloat16
-VMEM_LIMIT = 48 * 1024 * 1024
+VMEM_LIMIT = 45 * 1024 * 1024
 
 NN = (((1,), (0,)), ((), ()))
 NT = (((1,), (1,)), ((), ()))
@@ -175,17 +175,16 @@
             normed_ref[at : at + piece_rows, columns] = (
                 chunk * scale * gain_ref[:, columns]
             ).astype(BF16)
-    normed = normed_ref[...]
     loads[0].wait()
-    state_io = silu(mm(normed, wstate_ref[...])).astype(BF16)
+    state_io = silu(mm(normed_ref[...], wstate_ref[...])).astype(BF16)
     b_ref[...] = state_io[:, :NSTATE]
     c_ref[...] = state_io[:, NSTATE:]
     loads[1].wait()
-    pre = mm(normed, wstep_ref[...]) + bias_ref[...]
+    pre = mm(normed_ref[...], wstep_ref[...]) + bias_ref[...]
     step = jnp.maximum(pre, 0.0) + jnp.log1p(jnp.exp(-jnp.abs(pre)))
     heads = inner // HEADDIM
     loads[2].wait()
-    xs = silu(mm(normed, win_ref[...])).astype(BF16)
+    xs = silu(mm(normed_ref[...], win_ref[...])).astype(BF16)
     xs_ref[...] = xs
     spread = (iota((TILE, inner), 1) // HEADDIM == iota((TILE, inner), 0)).astype(F32).astype(BF16)
     step_wide = sum(mm(piece, spread) for piece in split3(step))
@@ -194,7 +193,7 @@
     xlow_ref[...] = jnp.where(low_half, scaled, 0.0).astype(BF16)
     xhigh_ref[...] = jnp.where(low_half, 0.0, scaled).astype(BF16)
     loads[3].wait()
-    z_ref[...] = mm(normed, wgate_ref[...])
+    z_ref[...] = mm(normed_ref[...], wgate_ref[...])
     a_ref[...] = step * (jnp.exp(decay_ref[...]) * (-LOG2E))
 
     lane = iota((TILE, TILE), 1)
@@ -558,11 +557,11 @@
     kept = [list(pair) for pair in zip(swapped, gathered)]
 
     sources, enc_terms = barrier((sources, enc_terms))
-    first = [k for k in range(dp_count) if k != dp_count // 2] if direct else []
+    first = [k for k in range(1, dp_count) if k != dp_count // 2] if direct else []
     enc_grad = [dp_cross([enc_terms[k]], 1, k)[0] for k in first]
     parts, enc_grad, enc_terms = barrier((layer(1, sources), enc_grad, enc_terms))
     if direct:
-        enc_grad = enc_grad + dp_cross([enc_terms[dp_count // 2]], 1, dp_count // 2)
+        enc_grad = enc_grad + [dp_cross([enc_terms[k]], 1, k)[0] for k in (dp_count // 2, 0)]
     arrived = tensor_cross(parts, 1)
     top, arrived = barrier((top, arrived))
     kept = [[lax.ppermute(top, "section", swap), passed]] + kept

time: 147 us -> 146 us (level)
  starting transfers between devices: 48.6 us -> 52.4 us
  waiting for transfers between devices: 64.3 us -> 60.5 us
    ppermute x11, starting transfers between devices: 8.87 us -> 13 us  [dp_cross(): lax.ppermute(value, ('dp', 'section'), [(d * 2 + active, (d ^ k) * 2 + ot...]
    ppermute x16, waiting for transfers between devices: 29.4 us -> 26.3 us  [tensor_cross(): lax.ppermute(value, ('section', 'tensor'), [(active * count + t, other *...]
    pallas_call x2, Pallas kernels: 15.1 us -> 12.9 us  [layer(): pl.pallas_call(functools.partial(layer_kernel, active, counts, band), out...]
    pallas_call x2, Pallas kernels: 2.58 us -> 4.68 us  [gradient_terms(): pl.pallas_call(functools.partial(grad_kernel, active, pieces), out_shape=...]
    unnamed x19 -> x21, local copies, waits for them, and re-layouts: 4.32 us -> 4.32 us
  transfers between devices with their start and end apart: 36 -> 36, of which waited for: 20 -> 18; matrix products, arithmetic and copies ran while one was open for 2% -> 2% of each run, Pallas kernels for 13% -> 13%
where the time goes in v4:
time: 146 us
  waiting for transfers between devices  60.5 us (41%)
  starting transfers between devices  52.4 us (36%)
  Pallas kernels  26.4 us (18%)
  local copies, waits for them, and re-layouts  5.63 us (4%)
    ppermute x16, starting transfers between devices, tensor_cross(): lax.ppermute(value, ('section', 'tensor'), [(active * count + t, other *...  28.6 us
    ppermute x16, waiting for transfers between devices, tensor_cross(): lax.ppermute(value, ('section', 'tensor'), [(active * count + t, other *...  26.3 us
    ppermute x11, waiting for transfers between devices, dp_cross(): lax.ppermute(value, ('dp', 'section'), [(d * 2 + active, (d ^ k) * 2 + ot...  22.6 us
    ppermute x11, starting transfers between devices, dp_cross(): lax.ppermute(value, ('dp', 'section'), [(d * 2 + active, (d ^ k) * 2 + ot...  13 us
    pallas_call x2, Pallas kernels, layer(): pl.pallas_call(functools.partial(layer_kernel, active, counts, band), out...  12.9 us
    ppermute x3, waiting for transfers between devices, tensor_gather(): lax.ppermute(value, 'tensor', [(t, t ^ k) for t in range(count)])  8.65 us
    ppermute x1, starting transfers between devices, per_device(): kept = [[lax.ppermute(top, 'section', swap), passed]] + kept  5.58 us
    pallas_call x2, Pallas kernels, gradient_terms(): pl.pallas_call(functools.partial(grad_kernel, active, pieces), out_shape=...  4.68 us
  transfers between devices with their start and end apart: 36, of which 18 were waited for; matrix products, arithmetic and copies ran while one was open for 2% of the time, Pallas kernels for 13%

profile of v4, /device:TPU:9, one launch (start us, length us, event | category | flops | bytes accessed | tf_op | source)
XLA Modules:
  0.0 146.0 jit_solution(6331884923049931773)
XLA Ops:
  0.7 0.7 collective-permute-start.3
  1.5 1.2 copy-done
  2.7 0.7 copy-done.1
  3.4 0.7 copy-done.2
  4.0 1.1 select_rows.1
  5.3 2.7 %collective-permute-start.2 = (bf16[128,512]{1,0:T(8,128)(2,1)S(1)}, bf16[128,512]{1,0:T(8,128)(2,1)S(1)}, u32[]{:S(2)}, u32[]{:S(2)}) collective-permute-start(bf16[128,512]{1,0:T(8,128)(2,1)S(1)} %get-tuple-element.82), channel_id=1, source_target_pairs={{0,28},{8,20},{16,12},{24,4},{4,0},{12,8},{20,16},{28,24},{1,29},{... | collective-permute-start | bytes 393224 | tf_op jit(solution)/shard_map/ppermute | solution.py:388
  8.0 1.6 %collective-permute-done.refs_1_ = bf16[128,512]{1,0:T(8,128)(2,1)S(1)} collective-permute-done((bf16[128,512]{1,0:T(8,128)(2,1)S(1)}, bf16[128,512]{1,0:T(8,128)(2,1)S(1)}, u32[]{:S(2)}, u32[]{:S(2)}) %collective-permute-start) | collective-permute-done | bytes 131104 | tf_op jit(solution)/shard_map/ppermute | solution.py:388
  9.6 2.5 %collective-permute-done.1.refs_2_ = bf16[128,512]{1,0:T(8,128)(2,1)S(1)} collective-permute-done((bf16[128,512]{1,0:T(8,128)(2,1)S(1)}, bf16[128,512]{1,0:T(8,128)(2,1)S(1)}, u32[]{:S(2)}, u32[]{:S(2)}) %collective-permute-start.1) | collective-permute-done | bytes 131104 | tf_op jit(solution)/shard_map/ppermute | solution.py:388
  12.1 2.8 %collective-permute-done.2.refs_3_ = bf16[128,512]{1,0:T(8,128)(2,1)S(1)} collective-permute-done((bf16[128,512]{1,0:T(8,128)(2,1)S(1)}, bf16[128,512]{1,0:T(8,128)(2,1)S(1)}, u32[]{:S(2)}, u32[]{:S(2)}) %collective-permute-start.2) | collective-permute-done | bytes 131104 | tf_op jit(solution)/shard_map/ppermute | solution.py:388
  14.9 2.2 %place_rows.1 = (bf16[512,512]{1,0:T(8,128)(2,1)}, s32[512,128]{1,0:T(8,128)S(1)}) custom-call(s32[3]{0:T(128)S(1)} %pad_add_fusion.pos_ref, s32[16]{0:T(128)S(1)} %copy-done.1, s32[16]{0:T(128)S(1)} %copy-done.2, bf16[128,512]{1,0:T(8,128)(2,1)S(1)} %get-tuple-element.83.refs_0_, bf16[128,512]{1,0:T(8,128)(2,1)S(1)} %collective-permute-done.refs_1_, ...), custom_call_target="tpu_custom_call" | custom-call | tf_op jit(solution)/shard_map/place_rows/pallas_call | solution.py:450
  17.1 1.6 %collective-permute-start.5 = (bf16[512,512]{1,0:T(8,128)(2,1)}, bf16[512,512]{1,0:T(8,128)(2,1)}, u32[]{:S(2)}, u32[]{:S(2)}) collective-permute-start(bf16[512,512]{1,0:T(8,128)(2,1)} %get-tuple-element.87), channel_id=1, source_target_pairs={{4,1},{5,0},{6,3},{7,2},{0,4},{1,5},{2,6},{3,7},{12,9},{13,8},{14,... | collective-permute-start | bytes 1572872 | tf_op jit(solution)/shard_map/ppermute | solution.py:374
  18.7 1.6 %collective-permute-start.7 = (bf16[512,512]{1,0:T(8,128)(2,1)}, bf16[512,512]{1,0:T(8,128)(2,1)}, u32[]{:S(2)}, u32[]{:S(2)}) collective-permute-start(bf16[512,512]{1,0:T(8,128)(2,1)} %get-tuple-element.87), channel_id=1, source_target_pairs={{4,3},{5,2},{6,1},{7,0},{0,4},{1,5},{2,6},{3,7},{12,11},{13,10},{1... | collective-permute-start | bytes 1572872 | tf_op jit(solution)/shard_map/ppermute | solution.py:374
  20.3 1.8 %copy.16 = bf16[1,2048,8]{2,1,0:T(8,128)(2,1)} copy(bf16[1,2048,8]{1,2,0:T(8,128)(2,1)} %param.22) | data formatting | bytes 65536 | tf_op args[8]
  22.2 1.1 pad.11.refs_9_.refs_13_
  23.4 1.7 %collective-permute-done.5.refs_1_ = bf16[512,512]{1,0:T(8,128)(2,1)} collective-permute-done((bf16[512,512]{1,0:T(8,128)(2,1)}, bf16[512,512]{1,0:T(8,128)(2,1)}, u32[]{:S(2)}, u32[]{:S(2)}) %collective-permute-start.5) | collective-permute-done | bytes 524320 | tf_op jit(solution)/shard_map/ppermute | solution.py:374
  25.2 5.6 %collective-permute-done.7.refs_3_ = bf16[512,512]{1,0:T(8,128)(2,1)} collective-permute-done((bf16[512,512]{1,0:T(8,128)(2,1)}, bf16[512,512]{1,0:T(8,128)(2,1)}, u32[]{:S(2)}, u32[]{:S(2)}) %collective-permute-start.7) | collective-permute-done | bytes 524320 | tf_op jit(solution)/shard_map/ppermute | solution.py:374
  30.8 1.6 %layer_part.2 = (bf16[1552,512]{1,0:T(8,128)(2,1)S(1)}, bf16[528,512]{1,0:T(8,128)(2,1)S(1)}, bf16[528,512]{1,0:T(8,128)(2,1)S(1)}, bf16[528,512]{1,0:T(8,128)(2,1)S(1)}) custom-call(s32[3]{0:T(128)S(1)} %pad_add_fusion.pos_ref, bf16[512,512]{1,0:T(8,128)(2,1)} %collective-permute-done.4.refs_0_, bf16[512,512]{1,0:T(8,128)(2,1)} %collective-permute-done.5.refs_1_, ...), custom_call_target="tpu_custom_call" | custom-call | flops 4294967296 | bytes 12000000 | tf_op jit(solution)/shard_map/layer_part/pallas_call | solution.py:485
  32.4 13.1 %collective-permute-start.8 = (bf16[1552,512]{1,0:T(8,128)(2,1)S(1)}, bf16[1552,512]{1,0:T(8,128)(2,1)S(1)}, u32[]{:S(2)}, u32[]{:S(2)}) collective-permute-start(bf16[1552,512]{1,0:T(8,128)(2,1)S(1)} %get-tuple-element.89), channel_id=1, source_target_pairs={{0,4},{1,5},{2,6},{3,7},{4,0},{5,1},{6,2},{7,3},{8,12},{9,13},{10,... | collective-permute-start | bytes 4767752 | tf_op jit(solution)/shard_map/ppermute | solution.py:374
  46.1 1.0 collective-permute-start.9
  47.1 13.0 %collective-permute-done.10.refs_2_ = bf16[528,512]{1,0:T(8,128)(2,1)S(1)} collective-permute-done((bf16[528,512]{1,0:T(8,128)(2,1)S(1)}, bf16[528,512]{1,0:T(8,128)(2,1)S(1)}, u32[]{:S(2)}, u32[]{:S(2)}) %collective-permute-start.10) | collective-permute-done | bytes 540704 | tf_op jit(solution)/shard_map/ppermute | solution.py:374
  60.1 0.7 sum_parts.2
  60.9 1.5 %collective-permute-done.12.other_ref.refs_1_ = bf16[256,512]{1,0:T(8,128)(2,1)S(1)} collective-permute-done((bf16[256,512]{1,0:T(8,128)(2,1)S(1)}, bf16[256,512]{1,0:T(8,128)(2,1)S(1)}, u32[]{:S(2)}, u32[]{:S(2)}) %collective-permute-start.12) | collective-permute-done | bytes 262176 | tf_op jit(solution)/shard_map/ppermute | solution.py:541
  63.0 1.3 collective-permute-start.13
  64.3 1.2 collective-permute-start.14
  65.7 5.1 %collective-permute-done.13.refs_2_.refs_3_ = bf16[256,512]{1,0:T(8,128)(2,1)S(1)} collective-permute-done((bf16[256,512]{1,0:T(8,128)(2,1)S(1)}, bf16[256,512]{1,0:T(8,128)(2,1)S(1)}, u32[]{:S(2)}, u32[]{:S(2)}) %collective-permute-start.13) | collective-permute-done | bytes 262176 | tf_op jit(solution)/shard_map/ppermute | solution.py:366
  70.9 3.1 %gradient_terms.2 = (bf16[512,512]{1,0:T(8,128)(2,1)S(1)}, bf16[512,512]{1,0:T(8,128)(2,1)S(1)}, bf16[512,512]{1,0:T(8,128)(2,1)S(1)}, bf16[512,512]{1,0:T(8,128)(2,1)S(1)}) custom-call(s32[3]{0:T(128)S(1)} %pad_add_fusion.pos_ref, bf16[512,512]{1,0:T(8,128)(2,1)S(1)} %get-tuple-element.96.refs_0_, bf16[512,2048]{1,0:T(8,128)(2,1)} %collective-permute-done.3.refs_1_), custom_call_target="tpu_custom_call" | custom-call | flops 1073741824 | bytes 5000000 | tf_op jit(solution)/shard_map/gradient_terms/pallas_call | solution.py:524
  73.9 3.5 %collective-permute-done.15.refs_6_.refs_7_ = bf16[256,512]{1,0:T(8,128)(2,1)S(1)} collective-permute-done((bf16[256,512]{1,0:T(8,128)(2,1)S(1)}, bf16[256,512]{1,0:T(8,128)(2,1)S(1)}, u32[]{:S(2)}, u32[]{:S(2)}) %collective-permute-start.15) | collective-permute-done | bytes 262176 | tf_op jit(solution)/shard_map/ppermute | solution.py:366
  77.5 1.2 collective-permute-start.16
  80.6 1.6 %collective-permute-start.20 = (bf16[512,512]{1,0:T(8,128)(2,1)S(1)}, bf16[512,512]{1,0:T(8,128)(2,1)S(1)}, u32[]{:S(2)}, u32[]{:S(2)}) collective-permute-start(bf16[512,512]{1,0:T(8,128)(2,1)S(1)} %get-tuple-element.123), channel_id=1, source_target_pairs={{4,24},{12,16},{20,8},{28,0},{0,4},{8,12},{16,20},{24,28},{5,25},{... | collective-permute-start | bytes 1572872 | tf_op jit(solution)/shard_map/ppermute | solution.py:388
  82.2 11.3 %layer_part.3 = (bf16[1552,512]{1,0:T(8,128)(2,1)S(1)}, bf16[528,512]{1,0:T(8,128)(2,1)S(1)}, bf16[528,512]{1,0:T(8,128)(2,1)S(1)}, bf16[528,512]{1,0:T(8,128)(2,1)S(1)}) custom-call(s32[3]{0:T(128)S(1)} %pad_add_fusion.pos_ref, bf16[256,512]{1,0:T(8,128)(2,1)S(1)} %get-tuple-element.130.own_ref.refs_0_, bf16[256,512]{1,0:T(8,128)(2,1)S(1)} %get-tuple-element.111.refs_1_, ...), custom_call_target="tpu_custom_call" | custom-call | flops 4294967296 | bytes 12000000 | tf_op jit(solution)/shard_map/layer_part/pallas_call | solution.py:485
  93.6 1.3 collective-permute-start.22
  95.2 1.5 %collective-permute-start.24 = (bf16[528,512]{1,0:T(8,128)(2,1)S(1)}, bf16[528,512]{1,0:T(8,128)(2,1)S(1)}, u32[]{:S(2)}, u32[]{:S(2)}) collective-permute-start(bf16[528,512]{1,0:T(8,128)(2,1)S(1)} %get-tuple-element.129), channel_id=1, source_target_pairs={{4,3},{5,2},{6,1},{7,0},{0,4},{1,5},{2,6},{3,7},{12,11},{13,10},{1... | collective-permute-start | bytes 1622024 | tf_op jit(solution)/shard_map/ppermute | solution.py:374
  96.7 2.6 %collective-permute-start.26 = (bf16[512,512]{1,0:T(8,128)(2,1)S(1)}, bf16[512,512]{1,0:T(8,128)(2,1)S(1)}, u32[]{:S(2)}, u32[]{:S(2)}) collective-permute-start(bf16[512,512]{1,0:T(8,128)(2,1)S(1)} %get-tuple-element.143), channel_id=1, source_target_pairs={{4,16},{12,24},{20,0},{28,8},{0,4},{8,12},{16,20},{24,28},{5,17},{... | collective-permute-start | bytes 1572872 | tf_op jit(solution)/shard_map/ppermute | solution.py:388
  99.3 1.8 %collective-permute-done.22.refs_1_ = bf16[528,512]{1,0:T(8,128)(2,1)S(1)} collective-permute-done((bf16[528,512]{1,0:T(8,128)(2,1)S(1)}, bf16[528,512]{1,0:T(8,128)(2,1)S(1)}, u32[]{:S(2)}, u32[]{:S(2)}) %collective-permute-start.22) | collective-permute-done | bytes 540704 | tf_op jit(solution)/shard_map/ppermute | solution.py:374
  101.1 1.7 %collective-permute-start.27 = (bf16[512,512]{1,0:T(8,128)(2,1)S(1)}, bf16[512,512]{1,0:T(8,128)(2,1)S(1)}, u32[]{:S(2)}, u32[]{:S(2)}) collective-permute-start(bf16[512,512]{1,0:T(8,128)(2,1)S(1)} %get-tuple-element.144), channel_id=1, source_target_pairs={{4,0},{12,8},{20,16},{28,24},{0,4},{8,12},{16,20},{24,28},{5,1},{1... | collective-permute-start | bytes 1572872 | tf_op jit(solution)/shard_map/ppermute | solution.py:388
  102.9 4.1 %collective-permute-done.24.refs_3_ = bf16[528,512]{1,0:T(8,128)(2,1)S(1)} collective-permute-done((bf16[528,512]{1,0:T(8,128)(2,1)S(1)}, bf16[528,512]{1,0:T(8,128)(2,1)S(1)}, u32[]{:S(2)}, u32[]{:S(2)}) %collective-permute-start.24) | collective-permute-done | bytes 540704 | tf_op jit(solution)/shard_map/ppermute | solution.py:374
  106.9 0.7 sum_parts.3
  107.7 1.6 %gradient_terms.3 = (bf16[512,512]{1,0:T(8,128)(2,1)S(1)}, bf16[512,512]{1,0:T(8,128)(2,1)S(1)}, bf16[512,512]{1,0:T(8,128)(2,1)S(1)}, bf16[512,512]{1,0:T(8,128)(2,1)S(1)}) custom-call(s32[3]{0:T(128)S(1)} %pad_add_fusion.pos_ref, bf16[512,512]{1,0:T(8,128)(2,1)S(1)} %get-tuple-element.136.refs_0_, bf16[512,2048]{1,0:T(8,128)(2,1)} %collective-permute-done.3.refs_1_), custom_call_target="tpu_custom_call" | custom-call | flops 1073741824 | bytes 5000000 | tf_op jit(solution)/shard_map/gradient_terms/pallas_call | solution.py:524
  109.3 1.8 %collective-permute-done.26.refs_2_ = bf16[512,512]{1,0:T(8,128)(2,1)S(1)} collective-permute-done((bf16[512,512]{1,0:T(8,128)(2,1)S(1)}, bf16[512,512]{1,0:T(8,128)(2,1)S(1)}, u32[]{:S(2)}, u32[]{:S(2)}) %collective-permute-start.26) | collective-permute-done | bytes 524320 | tf_op jit(solution)/shard_map/ppermute | solution.py:388
  111.1 2.2 %collective-permute-start.28 = (bf16[512,512]{1,0:T(8,128)(2,1)S(1)}, bf16[512,512]{1,0:T(8,128)(2,1)S(1)}, u32[]{:S(2)}, u32[]{:S(2)}) collective-permute-start(bf16[512,512]{1,0:T(8,128)(2,1)S(1)} %get-tuple-element.151), channel_id=1, source_target_pairs={{0,4},{1,5},{2,6},{3,7},{4,0},{5,1},{6,2},{7,3},{8,12},{9,13},{10,... | collective-permute-start | bytes 1572872 | tf_op jit(solution)/shard_map/ppermute | solution.py:374
  113.8 3.2 %collective-permute-start.34 = (bf16[512,512]{1,0:T(8,128)(2,1)S(1)}, bf16[512,512]{1,0:T(8,128)(2,1)S(1)}, u32[]{:S(2)}, u32[]{:S(2)}) collective-permute-start(bf16[512,512]{1,0:T(8,128)(2,1)S(1)} %get-tuple-element.147), channel_id=1, source_target_pairs={{0,20},{8,28},{16,4},{24,12},{4,0},{12,8},{20,16},{28,24},{1,21},{... | collective-permute-start | bytes 1572872 | tf_op jit(solution)/shard_map/ppermute | solution.py:388
  118.4 5.4 %collective-permute-done.33.refs_5_ = bf16[512,512]{1,0:T(8,128)(2,1)S(1)} collective-permute-done((bf16[512,512]{1,0:T(8,128)(2,1)S(1)}, bf16[512,512]{1,0:T(8,128)(2,1)S(1)}, u32[]{:S(2)}, u32[]{:S(2)}) %collective-permute-start.33) | collective-permute-done | bytes 524320 | tf_op jit(solution)/shard_map/ppermute | solution.py:388
  123.8 4.4 %collective-permute-start.31 = (bf16[512,512]{1,0:T(8,128)(2,1)S(1)}, bf16[512,512]{1,0:T(8,128)(2,1)S(1)}, u32[]{:S(2)}, u32[]{:S(2)}) collective-permute-start(bf16[512,512]{1,0:T(8,128)(2,1)S(1)} %get-tuple-element.151), channel_id=1, source_target_pairs={{0,7},{1,6},{2,5},{3,4},{4,0},{5,1},{6,2},{7,3},{8,15},{9,14},{10,... | collective-permute-start | bytes 1572872 | tf_op jit(solution)/shard_map/ppermute | solution.py:374
  128.2 1.7 %collective-permute-done.34.refs_6_ = bf16[512,512]{1,0:T(8,128)(2,1)S(1)} collective-permute-done((bf16[512,512]{1,0:T(8,128)(2,1)S(1)}, bf16[512,512]{1,0:T(8,128)(2,1)S(1)}, u32[]{:S(2)}, u32[]{:S(2)}) %collective-permute-start.34) | collective-permute-done | bytes 524320 | tf_op jit(solution)/shard_map/ppermute | solution.py:388
  129.9 5.6 %collective-permute-start.25 = (bf16[256,512]{1,0:T(8,128)(2,1)S(1)}, bf16[256,512]{1,0:T(8,128)(2,1)S(1)}, u32[]{:S(2)}, u32[]{:S(2)}) collective-permute-start(bf16[256,512]{1,0:T(8,128)(2,1)S(1)} %get-tuple-element.130.own_ref.refs_0_), channel_id=1, source_target_pairs={{0,4},{4,0},{1,5},{5,1},{2,6},{6,2},{3,7},{7,3},{8,12},{12,8},{9,1... | collective-permute-start | bytes 786440 | tf_op jit(solution)/shard_map/ppermute | solution.py:567
  135.4 6.8 %collective-permute-done.35.refs_7_ = bf16[512,512]{1,0:T(8,128)(2,1)S(1)} collective-permute-done((bf16[512,512]{1,0:T(8,128)(2,1)S(1)}, bf16[512,512]{1,0:T(8,128)(2,1)S(1)}, u32[]{:S(2)}, u32[]{:S(2)}) %collective-permute-start.35) | collective-permute-done | bytes 524320 | tf_op jit(solution)/shard_map/ppermute | solution.py:388
  142.2 1.6 %gradient_total.1 = bf16[1,512,512]{2,1,0:T(8,128)(2,1)} custom-call(s32[3]{0:T(128)S(1)} %pad_add_fusion.pos_ref, bf16[512,512]{1,0:T(8,128)(2,1)S(1)} %collective-permute-done.19.refs_0_, bf16[512,512]{1,0:T(8,128)(2,1)S(1)} %collective-permute-done.20.refs_1_, bf16[512,512]{1,0:T(8,128)(2,1)S(1)} %collective-permute-done.26.refs_2_, ...), custom_call_target="tpu_custom_call" | custom-call | flops 1000000 | bytes 4000000 | tf_op jit(solution)/shard_map/gradient_total/pallas_call | solution.py:599
  143.9 2.0 %assemble_rows.1 = bf16[1,512,2048]{2,1,0:T(8,128)(2,1)} custom-call(s32[3]{0:T(128)S(1)} %pad_add_fusion.pos_ref, bf16[256,512]{1,0:T(8,128)(2,1)S(1)} %collective-permute-done.25.refs_0_, bf16[256,512]{1,0:T(8,128)(2,1)S(1)} %collective-permute-done.12.other_ref.refs_1_, bf16[256,512]{1,0:T(8,128)(2,1)S(1)} %collective-permute-done.16.refs_3_.refs_2_, ...), custom_call_target="tpu_custom_call" | custom-call | flops 1000000 | bytes 4000000 | tf_op jit(solution)/shard_map/assemble_rows/pallas_call | solution.py:589
  (62 shorter events, 6.3 us)
Async XLA Ops:
  0.6 21.4 %copy-start.7 = (f32[1,8]{1,0:T(1,128)S(1)}, f32[1,8]{1,0:T(1,128)}, u32[]{:S(2)}) copy-start(f32[1,8]{1,0:T(1,128)} %param.25) | copy-start | bytes 100
  0.6 21.6 %copy-start.8 = (f32[1,8]{1,0:T(1,128)S(1)}, f32[1,8]{1,0:T(1,128)}, u32[]{:S(2)}) copy-start(f32[1,8]{1,0:T(1,128)} %param.23) | copy-start | bytes 100
  0.7 21.6 %copy-start.9 = (f32[1,8]{1,0:T(1,128)S(1)}, f32[1,8]{1,0:T(1,128)}, u32[]{:S(2)}) copy-start(f32[1,8]{1,0:T(1,128)} %param.24) | copy-start | bytes 100
  0.7 30.1 %copy-start.5 = (f32[1,2048]{1,0:T(1,128)S(1)}, f32[1,2048]{1,0:T(1,128)}, u32[]{:S(2)}) copy-start(f32[1,2048]{1,0:T(1,128)} %refs_9_.1) | copy-start | bytes 24580
  0.7 30.1 %copy-start.6 = (f32[1,512]{1,0:T(1,128)S(1)}, f32[1,512]{1,0:T(1,128)}, u32[]{:S(2)}) copy-start(f32[1,512]{1,0:T(1,128)} %refs_17_.1) | copy-start | bytes 6148
  0.7 14.2 %collective-permute-start.3 = (bf16[512,2048]{1,0:T(8,128)(2,1)}, bf16[512,2048]{1,0:T(8,128)(2,1)}, u32[]{:S(2)}, u32[]{:S(2)}) collective-permute-start(bf16[512,2048]{1,0:T(8,128)(2,1)} %bitcast.16), channel_id=1, source_target_pairs={{0,4},{4,0},{1,5},{5,1},{2,6},{6,2},{3,7},{7,3},{8,12},{12,8},{9,1... | collective-permute-start | bytes 6291464 | tf_op jit(solution)/shard_map/ppermute | solution.py:447
  1.5 1.2 copy-start
  2.7 0.7 copy-start.1
  3.4 0.7 copy-start.2
  4.0 26.7 %copy-start.3 = (bf16[1,2048,512]{2,1,0:T(8,128)(2,1)S(1)}, bf16[1,2048,512]{2,1,0:T(8,128)(2,1)}, u32[]{:S(2)}) copy-start(bf16[1,2048,512]{2,1,0:T(8,128)(2,1)} %param.19) | copy-start | bytes 6291460
  4.0 26.7 %copy-start.4 = (bf16[1,2048,256]{2,1,0:T(8,128)(2,1)S(1)}, bf16[1,2048,256]{2,1,0:T(8,128)(2,1)}, u32[]{:S(2)}) copy-start(bf16[1,2048,256]{2,1,0:T(8,128)(2,1)} %param.21) | copy-start | bytes 3145732
  5.1 4.4 %collective-permute-start = (bf16[128,512]{1,0:T(8,128)(2,1)S(1)}, bf16[128,512]{1,0:T(8,128)(2,1)S(1)}, u32[]{:S(2)}, u32[]{:S(2)}) collective-permute-start(bf16[128,512]{1,0:T(8,128)(2,1)S(1)} %get-tuple-element.80), channel_id=1, source_target_pairs={{0,12},{8,4},{16,28},{24,20},{4,0},{12,8},{20,16},{28,24},{1,13},{... | collective-permute-start | bytes 393224 | tf_op jit(solution)/shard_map/ppermute | solution.py:388
  5.2 6.9 %collective-permute-start.1 = (bf16[128,512]{1,0:T(8,128)(2,1)S(1)}, bf16[128,512]{1,0:T(8,128)(2,1)S(1)}, u32[]{:S(2)}, u32[]{:S(2)}) collective-permute-start(bf16[128,512]{1,0:T(8,128)(2,1)S(1)} %get-tuple-element.81), channel_id=1, source_target_pairs={{0,20},{8,28},{16,4},{24,12},{4,0},{12,8},{20,16},{28,24},{1,21},{... | collective-permute-start | bytes 393224 | tf_op jit(solution)/shard_map/ppermute | solution.py:388
  5.3 9.7 %collective-permute-start.2 = (bf16[128,512]{1,0:T(8,128)(2,1)S(1)}, bf16[128,512]{1,0:T(8,128)(2,1)S(1)}, u32[]{:S(2)}, u32[]{:S(2)}) collective-permute-start(bf16[128,512]{1,0:T(8,128)(2,1)S(1)} %get-tuple-element.82), channel_id=1, source_target_pairs={{0,28},{8,20},{16,12},{24,4},{4,0},{12,8},{20,16},{28,24},{1,29},{... | collective-permute-start | bytes 393224 | tf_op jit(solution)/shard_map/ppermute | solution.py:388
  17.1 6.3 %collective-permute-start.4 = (bf16[512,512]{1,0:T(8,128)(2,1)}, bf16[512,512]{1,0:T(8,128)(2,1)}, u32[]{:S(2)}, u32[]{:S(2)}) collective-permute-start(bf16[512,512]{1,0:T(8,128)(2,1)} %get-tuple-element.87), channel_id=1, source_target_pairs={{4,0},{5,1},{6,2},{7,3},{0,4},{1,5},{2,6},{3,7},{12,8},{13,9},{14,... | collective-permute-start | bytes 1572872 | tf_op jit(solution)/shard_map/ppermute | solution.py:374
  17.1 8.0 %collective-permute-start.5 = (bf16[512,512]{1,0:T(8,128)(2,1)}, bf16[512,512]{1,0:T(8,128)(2,1)}, u32[]{:S(2)}, u32[]{:S(2)}) collective-permute-start(bf16[512,512]{1,0:T(8,128)(2,1)} %get-tuple-element.87), channel_id=1, source_target_pairs={{4,1},{5,0},{6,3},{7,2},{0,4},{1,5},{2,6},{3,7},{12,9},{13,8},{14,... | collective-permute-start | bytes 1572872 | tf_op jit(solution)/shard_map/ppermute | solution.py:374
  18.7 6.5 %collective-permute-start.6 = (bf16[512,512]{1,0:T(8,128)(2,1)}, bf16[512,512]{1,0:T(8,128)(2,1)}, u32[]{:S(2)}, u32[]{:S(2)}) collective-permute-start(bf16[512,512]{1,0:T(8,128)(2,1)} %get-tuple-element.87), channel_id=1, source_target_pairs={{4,2},{5,3},{6,0},{7,1},{0,4},{1,5},{2,6},{3,7},{12,10},{13,11},{1... | collective-permute-start | bytes 1572872 | tf_op jit(solution)/shard_map/ppermute | solution.py:374
  18.7 12.0 %collective-permute-start.7 = (bf16[512,512]{1,0:T(8,128)(2,1)}, bf16[512,512]{1,0:T(8,128)(2,1)}, u32[]{:S(2)}, u32[]{:S(2)}) collective-permute-start(bf16[512,512]{1,0:T(8,128)(2,1)} %get-tuple-element.87), channel_id=1, source_target_pairs={{4,3},{5,2},{6,1},{7,0},{0,4},{1,5},{2,6},{3,7},{12,11},{13,10},{1... | collective-permute-start | bytes 1572872 | tf_op jit(solution)/shard_map/ppermute | solution.py:374
  32.4 27.7 %collective-permute-start.8 = (bf16[1552,512]{1,0:T(8,128)(2,1)S(1)}, bf16[1552,512]{1,0:T(8,128)(2,1)S(1)}, u32[]{:S(2)}, u32[]{:S(2)}) collective-permute-start(bf16[1552,512]{1,0:T(8,128)(2,1)S(1)} %get-tuple-element.89), channel_id=1, source_target_pairs={{0,4},{1,5},{2,6},{3,7},{4,0},{5,1},{6,2},{7,3},{8,12},{9,13},{10,... | collective-permute-start | bytes 4767752 | tf_op jit(solution)/shard_map/ppermute | solution.py:374
  45.5 14.6 %collective-permute-start.10 = (bf16[528,512]{1,0:T(8,128)(2,1)S(1)}, bf16[528,512]{1,0:T(8,128)(2,1)S(1)}, u32[]{:S(2)}, u32[]{:S(2)}) collective-permute-start(bf16[528,512]{1,0:T(8,128)(2,1)S(1)} %get-tuple-element.91), channel_id=1, source_target_pairs={{0,6},{1,7},{2,4},{3,5},{4,0},{5,1},{6,2},{7,3},{8,14},{9,15},{10,... | collective-permute-start | bytes 1622024 | tf_op jit(solution)/shard_map/ppermute | solution.py:374
  45.5 14.5 %collective-permute-start.11 = (bf16[528,512]{1,0:T(8,128)(2,1)S(1)}, bf16[528,512]{1,0:T(8,128)(2,1)S(1)}, u32[]{:S(2)}, u32[]{:S(2)}) collective-permute-start(bf16[528,512]{1,0:T(8,128)(2,1)S(1)} %get-tuple-element.92), channel_id=1, source_target_pairs={{0,7},{1,6},{2,5},{3,4},{4,0},{5,1},{6,2},{7,3},{8,15},{9,14},{10,... | collective-permute-start | bytes 1622024 | tf_op jit(solution)/shard_map/ppermute | solution.py:374
  46.1 14.0 %collective-permute-start.9 = (bf16[528,512]{1,0:T(8,128)(2,1)S(1)}, bf16[528,512]{1,0:T(8,128)(2,1)S(1)}, u32[]{:S(2)}, u32[]{:S(2)}) collective-permute-start(bf16[528,512]{1,0:T(8,128)(2,1)S(1)} %get-tuple-element.90), channel_id=1, source_target_pairs={{0,5},{1,4},{2,7},{3,6},{4,0},{5,1},{6,2},{7,3},{8,13},{9,12},{10,... | collective-permute-start | bytes 1622024 | tf_op jit(solution)/shard_map/ppermute | solution.py:374
  60.8 1.6 %collective-permute-start.12 = (bf16[256,512]{1,0:T(8,128)(2,1)S(1)}, bf16[256,512]{1,0:T(8,128)(2,1)S(1)}, u32[]{:S(2)}, u32[]{:S(2)}) collective-permute-start(bf16[256,512]{1,0:T(8,128)(2,1)S(1)} %get-tuple-element.111.refs_1_), channel_id=1, source_target_pairs={{0,4},{4,0},{1,5},{5,1},{2,6},{6,2},{3,7},{7,3},{8,12},{12,8},{9,1... | collective-permute-start | bytes 786440 | tf_op jit(solution)/shard_map/ppermute | solution.py:541
  63.0 7.8 %collective-permute-start.13 = (bf16[256,512]{1,0:T(8,128)(2,1)S(1)}, bf16[256,512]{1,0:T(8,128)(2,1)S(1)}, u32[]{:S(2)}, u32[]{:S(2)}) collective-permute-start(bf16[256,512]{1,0:T(8,128)(2,1)S(1)} %own_half.1), channel_id=1, source_target_pairs={{0,1},{1,0},{2,3},{3,2},{4,5},{5,4},{6,7},{7,6},{8,9},{9,8},{10,11... | collective-permute-start | bytes 786440 | tf_op jit(solution)/shard_map/ppermute | solution.py:366
  64.3 9.6 %collective-permute-start.14 = (bf16[256,512]{1,0:T(8,128)(2,1)S(1)}, bf16[256,512]{1,0:T(8,128)(2,1)S(1)}, u32[]{:S(2)}, u32[]{:S(2)}) collective-permute-start(bf16[256,512]{1,0:T(8,128)(2,1)S(1)} %own_half.1), channel_id=1, source_target_pairs={{0,2},{1,3},{2,0},{3,1},{4,6},{5,7},{6,4},{7,5},{8,10},{9,11},{10,... | collective-permute-start | bytes 786440 | tf_op jit(solution)/shard_map/ppermute | solution.py:366
  65.5 12.0 %collective-permute-start.15 = (bf16[256,512]{1,0:T(8,128)(2,1)S(1)}, bf16[256,512]{1,0:T(8,128)(2,1)S(1)}, u32[]{:S(2)}, u32[]{:S(2)}) collective-permute-start(bf16[256,512]{1,0:T(8,128)(2,1)S(1)} %own_half.1), channel_id=1, source_target_pairs={{0,3},{1,2},{2,1},{3,0},{4,7},{5,6},{6,5},{7,4},{8,11},{9,10},{10,... | collective-permute-start | bytes 786440 | tf_op jit(solution)/shard_map/ppermute | solution.py:366
  77.5 2.3 %collective-permute-start.16 = (bf16[256,512]{1,0:T(8,128)(2,1)S(1)}, bf16[256,512]{1,0:T(8,128)(2,1)S(1)}, u32[]{:S(2)}, u32[]{:S(2)}) collective-permute-start(bf16[256,512]{1,0:T(8,128)(2,1)S(1)} %collective-permute-done.13.refs_2_.refs_3_), channel_id=1, source_target_pairs={{0,4},{4,0},{1,5},{5,1},{2,6},{6,2},{3,7},{7,3},{8,12},{12,8},{9,1... | collective-permute-start | bytes 786440 | tf_op jit(solution)/shard_map/ppermute | solution.py:555
  78.6 1.5 %collective-permute-start.17 = (bf16[256,512]{1,0:T(8,128)(2,1)S(1)}, bf16[256,512]{1,0:T(8,128)(2,1)S(1)}, u32[]{:S(2)}, u32[]{:S(2)}) collective-permute-start(bf16[256,512]{1,0:T(8,128)(2,1)S(1)} %collective-permute-done.14.refs_4_.refs_5_), channel_id=1, source_target_pairs={{0,4},{4,0},{1,5},{5,1},{2,6},{6,2},{3,7},{7,3},{8,12},{12,8},{9,1... | collective-permute-start | bytes 786440 | tf_op jit(solution)/shard_map/ppermute | solution.py:555
  78.6 1.9 %collective-permute-start.18 = (bf16[256,512]{1,0:T(8,128)(2,1)S(1)}, bf16[256,512]{1,0:T(8,128)(2,1)S(1)}, u32[]{:S(2)}, u32[]{:S(2)}) collective-permute-start(bf16[256,512]{1,0:T(8,128)(2,1)S(1)} %collective-permute-done.15.refs_6_.refs_7_), channel_id=1, source_target_pairs={{0,4},{4,0},{1,5},{5,1},{2,6},{6,2},{3,7},{7,3},{8,12},{12,8},{9,1... | collective-permute-start | bytes 786440 | tf_op jit(solution)/shard_map/ppermute | solution.py:555
  80.6 12.9 %collective-permute-start.19 = (bf16[512,512]{1,0:T(8,128)(2,1)S(1)}, bf16[512,512]{1,0:T(8,128)(2,1)S(1)}, u32[]{:S(2)}, u32[]{:S(2)}) collective-permute-start(bf16[512,512]{1,0:T(8,128)(2,1)S(1)} %get-tuple-element.122), channel_id=1, source_target_pairs={{4,8},{12,0},{20,24},{28,16},{0,4},{8,12},{16,20},{24,28},{5,9},{1... | collective-permute-start | bytes 1572872 | tf_op jit(solution)/shard_map/ppermute | solution.py:388
  80.6 12.9 %collective-permute-start.20 = (bf16[512,512]{1,0:T(8,128)(2,1)S(1)}, bf16[512,512]{1,0:T(8,128)(2,1)S(1)}, u32[]{:S(2)}, u32[]{:S(2)}) collective-permute-start(bf16[512,512]{1,0:T(8,128)(2,1)S(1)} %get-tuple-element.123), channel_id=1, source_target_pairs={{4,24},{12,16},{20,8},{28,0},{0,4},{8,12},{16,20},{24,28},{5,25},{... | collective-permute-start | bytes 1572872 | tf_op jit(solution)/shard_map/ppermute | solution.py:388
  93.5 13.4 %collective-permute-start.21 = (bf16[1552,512]{1,0:T(8,128)(2,1)S(1)}, bf16[1552,512]{1,0:T(8,128)(2,1)S(1)}, u32[]{:S(2)}, u32[]{:S(2)}) collective-permute-start(bf16[1552,512]{1,0:T(8,128)(2,1)S(1)} %get-tuple-element.126), channel_id=1, source_target_pairs={{4,0},{5,1},{6,2},{7,3},{0,4},{1,5},{2,6},{3,7},{12,8},{13,9},{14,... | collective-permute-start | bytes 4767752 | tf_op jit(solution)/shard_map/ppermute | solution.py:374
  93.6 7.6 %collective-permute-start.22 = (bf16[528,512]{1,0:T(8,128)(2,1)S(1)}, bf16[528,512]{1,0:T(8,128)(2,1)S(1)}, u32[]{:S(2)}, u32[]{:S(2)}) collective-permute-start(bf16[528,512]{1,0:T(8,128)(2,1)S(1)} %get-tuple-element.127), channel_id=1, source_target_pairs={{4,1},{5,0},{6,3},{7,2},{0,4},{1,5},{2,6},{3,7},{12,9},{13,8},{14,... | collective-permute-start | bytes 1622024 | tf_op jit(solution)/shard_map/ppermute | solution.py:374
  94.8 8.0 %collective-permute-start.23 = (bf16[528,512]{1,0:T(8,128)(2,1)S(1)}, bf16[528,512]{1,0:T(8,128)(2,1)S(1)}, u32[]{:S(2)}, u32[]{:S(2)}) collective-permute-start(bf16[528,512]{1,0:T(8,128)(2,1)S(1)} %get-tuple-element.128), channel_id=1, source_target_pairs={{4,2},{5,3},{6,0},{7,1},{0,4},{1,5},{2,6},{3,7},{12,10},{13,11},{1... | collective-permute-start | bytes 1622024 | tf_op jit(solution)/shard_map/ppermute | solution.py:374
  95.2 11.7 %collective-permute-start.24 = (bf16[528,512]{1,0:T(8,128)(2,1)S(1)}, bf16[528,512]{1,0:T(8,128)(2,1)S(1)}, u32[]{:S(2)}, u32[]{:S(2)}) collective-permute-start(bf16[528,512]{1,0:T(8,128)(2,1)S(1)} %get-tuple-element.129), channel_id=1, source_target_pairs={{4,3},{5,2},{6,1},{7,0},{0,4},{1,5},{2,6},{3,7},{12,11},{13,10},{1... | collective-permute-start | bytes 1622024 | tf_op jit(solution)/shard_map/ppermute | solution.py:374
  96.7 14.4 %collective-permute-start.26 = (bf16[512,512]{1,0:T(8,128)(2,1)S(1)}, bf16[512,512]{1,0:T(8,128)(2,1)S(1)}, u32[]{:S(2)}, u32[]{:S(2)}) collective-permute-start(bf16[512,512]{1,0:T(8,128)(2,1)S(1)} %get-tuple-element.143), channel_id=1, source_target_pairs={{4,16},{12,24},{20,0},{28,8},{0,4},{8,12},{16,20},{24,28},{5,17},{... | collective-permute-start | bytes 1572872 | tf_op jit(solution)/shard_map/ppermute | solution.py:388
  101.1 9.9 %collective-permute-start.27 = (bf16[512,512]{1,0:T(8,128)(2,1)S(1)}, bf16[512,512]{1,0:T(8,128)(2,1)S(1)}, u32[]{:S(2)}, u32[]{:S(2)}) collective-permute-start(bf16[512,512]{1,0:T(8,128)(2,1)S(1)} %get-tuple-element.144), channel_id=1, source_target_pairs={{4,0},{12,8},{20,16},{28,24},{0,4},{8,12},{16,20},{24,28},{5,1},{1... | collective-permute-start | bytes 1572872 | tf_op jit(solution)/shard_map/ppermute | solution.py:388
  111.1 6.4 %collective-permute-start.28 = (bf16[512,512]{1,0:T(8,128)(2,1)S(1)}, bf16[512,512]{1,0:T(8,128)(2,1)S(1)}, u32[]{:S(2)}, u32[]{:S(2)}) collective-permute-start(bf16[512,512]{1,0:T(8,128)(2,1)S(1)} %get-tuple-element.151), channel_id=1, source_target_pairs={{0,4},{1,5},{2,6},{3,7},{4,0},{5,1},{6,2},{7,3},{8,12},{9,13},{10,... | collective-permute-start | bytes 1572872 | tf_op jit(solution)/shard_map/ppermute | solution.py:374
  113.3 4.4 %collective-permute-start.32 = (bf16[512,512]{1,0:T(8,128)(2,1)S(1)}, bf16[512,512]{1,0:T(8,128)(2,1)S(1)}, u32[]{:S(2)}, u32[]{:S(2)}) collective-permute-start(bf16[512,512]{1,0:T(8,128)(2,1)S(1)} %get-tuple-element.145), channel_id=1, source_target_pairs={{0,4},{8,12},{16,20},{24,28},{4,0},{12,8},{20,16},{28,24},{1,5},{9... | collective-permute-start | bytes 1572872 | tf_op jit(solution)/shard_map/ppermute | solution.py:388
  113.3 10.4 %collective-permute-start.33 = (bf16[512,512]{1,0:T(8,128)(2,1)S(1)}, bf16[512,512]{1,0:T(8,128)(2,1)S(1)}, u32[]{:S(2)}, u32[]{:S(2)}) collective-permute-start(bf16[512,512]{1,0:T(8,128)(2,1)S(1)} %get-tuple-element.146), channel_id=1, source_target_pairs={{0,12},{8,4},{16,28},{24,20},{4,0},{12,8},{20,16},{28,24},{1,13},{... | collective-permute-start | bytes 1572872 | tf_op jit(solution)/shard_map/ppermute | solution.py:388
  113.8 16.1 %collective-permute-start.34 = (bf16[512,512]{1,0:T(8,128)(2,1)S(1)}, bf16[512,512]{1,0:T(8,128)(2,1)S(1)}, u32[]{:S(2)}, u32[]{:S(2)}) collective-permute-start(bf16[512,512]{1,0:T(8,128)(2,1)S(1)} %get-tuple-element.147), channel_id=1, source_target_pairs={{0,20},{8,28},{16,4},{24,12},{4,0},{12,8},{20,16},{28,24},{1,21},{... | collective-permute-start | bytes 1572872 | tf_op jit(solution)/shard_map/ppermute | solution.py:388
  117.0 25.3 %collective-permute-start.35 = (bf16[512,512]{1,0:T(8,128)(2,1)S(1)}, bf16[512,512]{1,0:T(8,128)(2,1)S(1)}, u32[]{:S(2)}, u32[]{:S(2)}) collective-permute-start(bf16[512,512]{1,0:T(8,128)(2,1)S(1)} %get-tuple-element.148), channel_id=1, source_target_pairs={{0,28},{8,20},{16,12},{24,4},{4,0},{12,8},{20,16},{28,24},{1,29},{... | collective-permute-start | bytes 1572872 | tf_op jit(solution)/shard_map/ppermute | solution.py:388
  117.5 26.4 %collective-permute-start.29 = (bf16[512,512]{1,0:T(8,128)(2,1)S(1)}, bf16[512,512]{1,0:T(8,128)(2,1)S(1)}, u32[]{:S(2)}, u32[]{:S(2)}) collective-permute-start(bf16[512,512]{1,0:T(8,128)(2,1)S(1)} %get-tuple-element.151), channel_id=1, source_target_pairs={{0,5},{1,4},{2,7},{3,6},{4,0},{5,1},{6,2},{7,3},{8,13},{9,12},{10,... | collective-permute-start | bytes 1572872 | tf_op jit(solution)/shard_map/ppermute | solution.py:374
  117.7 26.1 %collective-permute-start.30 = (bf16[512,512]{1,0:T(8,128)(2,1)S(1)}, bf16[512,512]{1,0:T(8,128)(2,1)S(1)}, u32[]{:S(2)}, u32[]{:S(2)}) collective-permute-start(bf16[512,512]{1,0:T(8,128)(2,1)S(1)} %get-tuple-element.151), channel_id=1, source_target_pairs={{0,6},{1,7},{2,4},{3,5},{4,0},{5,1},{6,2},{7,3},{8,14},{9,15},{10,... | collective-permute-start | bytes 1572872 | tf_op jit(solution)/shard_map/ppermute | solution.py:374
  123.8 20.1 %collective-permute-start.31 = (bf16[512,512]{1,0:T(8,128)(2,1)S(1)}, bf16[512,512]{1,0:T(8,128)(2,1)S(1)}, u32[]{:S(2)}, u32[]{:S(2)}) collective-permute-start(bf16[512,512]{1,0:T(8,128)(2,1)S(1)} %get-tuple-element.151), channel_id=1, source_target_pairs={{0,7},{1,6},{2,5},{3,4},{4,0},{5,1},{6,2},{7,3},{8,15},{9,14},{10,... | collective-permute-start | bytes 1572872 | tf_op jit(solution)/shard_map/ppermute | solution.py:374
  129.9 14.0 %collective-permute-start.25 = (bf16[256,512]{1,0:T(8,128)(2,1)S(1)}, bf16[256,512]{1,0:T(8,128)(2,1)S(1)}, u32[]{:S(2)}, u32[]{:S(2)}) collective-permute-start(bf16[256,512]{1,0:T(8,128)(2,1)S(1)} %get-tuple-element.130.own_ref.refs_0_), channel_id=1, source_target_pairs={{0,4},{4,0},{1,5},{5,1},{2,6},{6,2},{3,7},{7,3},{8,12},{12,8},{9,1... | collective-permute-start | bytes 786440 | tf_op jit(solution)/shard_map/ppermute | solution.py:567
